TPU v7x, 32 devices: a whole 2x2x4 slice. The times are simulated.
32 devices in a mesh: test: 2 (over core), bx: 4 (over y, x), by: 4 (over z).
Axes of the slice: x: 2, y: 2, z: 4, core: 2. Of those that a mesh axis runs over, the one named last changes fastest.
Arguments:
- log_conductivity: float32 [32, 32, 256], P('bx', 'by'), may hold values from -3 to 3
- storage: float32 [32, 32, 256], P('bx', 'by'), may hold values from 0.5 to 2
- recharge: float32 [32, 32, 256], P('bx', 'by'), may hold values from -6 to 6
- pump_rate: float32 [8], P('test'), may hold values from 4 to 16
- pump_well: int32 [8], P('test'), may hold values from 0 to 511
- observed: float32 [8, 512], P('test'), may hold values from -9 to 9
- owner: int32 [512], replicated, may hold values from 0 to 15, as said below
- screen_column: int32 [512], replicated, may hold values from 0 to 63
- screen_top: int32 [512], replicated, may hold values from 0 to 248
Outputs:
- gradient: float32 [32, 32, 256], P('bx', 'by', 'test')
Inputs may be any that keep to these rules, and one draw needn't show every extreme that they name: `owner`: each brick owns exactly 32 wells.
All inputs are finite; a program needn't handle non-finite values.
Results may differ from a plain program's by a relative error of at most 0.0001.
Values sent between devices are 32-bit elements; how exact they have to be, the bound alone decides.
No kernel may reach another device: no remote copies, remote signals or barrier semaphores. Data moves between devices by JAX's collectives and lax.ppermute only.
A program may use at most 64 MiB of HBM per device.

v0:
```python
import jax
import jax.numpy as jnp
from jax import lax
from jax.sharding import PartitionSpec as P

SWEEPS = 3
SCREEN = 8


epsilon = 1e-06


def with_halo(block, sides, width):
    for axis, dim in sides:
        count = lax.axis_size(axis)
        forward = [(i, i + 1) for i in range(count - 1)]
        backward = [(target, source) for source, target in forward]
        low = lax.ppermute(
            lax.slice_in_dim(block, block.shape[dim] - width, None, axis=dim), axis, forward
        )
        high = lax.ppermute(lax.slice_in_dim(block, 0, width, axis=dim), axis, backward)
        block = jnp.concatenate([low, block, high], axis=dim)
    return block


def pad_depth(values):
    return jnp.pad(values, [(0, 0)] * (values.ndim - 1) + [(1, 1)])


def neighbours(padded, centre):
    z_padded = pad_depth(centre)
    return [
        padded[..., 2:, 1:-1, :],
        padded[..., :-2, 1:-1, :],
        padded[..., 1:-1, 2:, :],
        padded[..., 1:-1, :-2, :],
        z_padded[..., 2:],
        z_padded[..., :-2],
    ]


def weighted(conductance, others):
    accumulated = conductance[0] * others[0]
    for position in range(1, 6):
        accumulated = accumulated + conductance[position] * others[position]
    return accumulated


def sensitivity(conductance, heads_field, heads_padded, adjoint_field, adjoint_padded):
    near_heads = neighbours(heads_padded, heads_field)
    near_adjoint = neighbours(adjoint_padded, adjoint_field)
    accumulated = jnp.zeros_like(heads_field)
    for position in range(6):
        accumulated = accumulated + conductance[position] * (heads_field - near_heads[position]) * (
            adjoint_field - near_adjoint[position]
        )
    return -0.5 * accumulated


def relax_field(source, conductance, diagonal):
    iterate = source / diagonal
    for sweep_index in range(SWEEPS - 1):
        padded = with_halo(iterate, (("bx", 1), ("by", 2)), 1)
        iterate = (source + weighted(conductance, neighbours(padded, iterate))) / diagonal
    return iterate


def per_sweep_terms(
    log_conductivity,
    storage,
    recharge,
    pump_rate,
    pump_well,
    observed,
    owner,
    screen_column,
    screen_top,
):
    size_x, size_y, size_z = log_conductivity.shape
    tests_here = pump_rate.shape[0]
    cell_count = size_x * size_y * size_z
    padded_log = with_halo(log_conductivity, (("bx", 0), ("by", 1)), 1)
    conductance = [
        jnp.exp(0.5 * (log_conductivity + other))
        for other in neighbours(padded_log, log_conductivity)
    ]
    diagonal = storage + weighted(conductance, [1.0] * 6)
    brick_index = lax.axis_index("bx") * lax.axis_size("by") + lax.axis_index("by")
    offsets = jnp.arange(SCREEN, dtype=jnp.int32)
    screen_cells = (screen_column * size_z + screen_top)[:, None] + offsets[None, :]
    owned_here = owner == brick_index
    pump_cells = screen_cells[pump_well]
    pump_value = jnp.where(owner[pump_well] == brick_index, -pump_rate, 0.0)
    test_rows = jnp.arange(tests_here, dtype=jnp.int32)[:, None]
    flat_source = jnp.broadcast_to(recharge.reshape(1, cell_count), (tests_here, cell_count))
    flat_source = flat_source.at[test_rows, pump_cells].add(
        jnp.broadcast_to(pump_value[:, None], pump_cells.shape)
    )
    source = flat_source.reshape(tests_here, size_x, size_y, size_z)
    heads_field = relax_field(source, conductance, diagonal)
    well_heads = jnp.mean(heads_field.reshape(tests_here, cell_count)[:, screen_cells], axis=2)
    residual = jnp.where(owned_here[None, :], well_heads - observed, 0.0)
    well_count = residual.shape[1]
    misfit = lax.psum(jnp.sum(residual * residual, axis=1), ("bx", "by")) / well_count + epsilon
    weights = residual / misfit[:, None]
    values = jnp.broadcast_to(weights[:, :, None], (tests_here, well_count, SCREEN)).reshape(
        tests_here, -1
    )
    adjoint_source = (
        jnp.zeros((tests_here, cell_count), jnp.float32).at[:, screen_cells.reshape(-1)].add(values)
    )
    adjoint_field = relax_field(
        adjoint_source.reshape(tests_here, size_x, size_y, size_z), conductance, diagonal
    )
    stacked = with_halo(
        jnp.concatenate([heads_field, adjoint_field], axis=0), (("bx", 1), ("by", 2)), 1
    )
    test_terms = sensitivity(
        conductance, heads_field, stacked[:tests_here], adjoint_field, stacked[tests_here:]
    )
    return (test_terms, misfit)


def local(
    log_conductivity,
    storage,
    recharge,
    pump_rate,
    pump_well,
    observed,
    owner,
    screen_column,
    screen_top,
):
    tests_here = pump_rate.shape[0]
    test_terms, misfit = per_sweep_terms(
        log_conductivity,
        storage,
        recharge,
        pump_rate,
        pump_well,
        observed,
        owner,
        screen_column,
        screen_top,
    )
    local_sum = jnp.sum(test_terms, axis=0)
    all_tests = tests_here * lax.axis_size("test")
    gradient = lax.psum_scatter(local_sum, "test", scatter_dimension=2, tiled=True)
    return gradient / all_tests


def solution(mesh):
    placed = (
        P("bx", "by", None),
        P("bx", "by", None),
        P("bx", "by", None),
        P("test"),
        P("test"),
        P("test", None),
        P(),
        P(),
        P(),
    )
    return jax.shard_map(
        local, mesh=mesh, in_specs=placed, out_specs=P("bx", "by", "test"), check_vma=False
    )
```

profile of v0, /device:TPU:0, one launch (start us, length us, event | category | flops | bytes accessed | tf_op | source)
XLA Modules:
  0.0 230.1 jit_solution(8506230737984295614)
XLA Ops:
  6.5 0.7 fusion.117
  7.3 4.8 %collective-permute-start.1 = (f32[1,8,256]{2,1,0:T(8,128)S(1)}, f32[1,8,256]{2,1,0:T(8,128)S(1)}, u32[]{:S(2)}, u32[]{:S(2)}) collective-permute-start(f32[1,8,256]{2,1,0:T(8,128)S(1)} %get-tuple-element.35), channel_id=1, source_target_pairs={{0,4},{4,8},{8,12},{1,5},{5,9},{9,13},{2,6},{6,10},{10,14},{3,7},{... | collective-permute-start | bytes 24584 | tf_op jit(solution)/shard_map/ppermute | solution.py:18
  12.1 1.3 collective-permute-start
  15.5 1.3 gather_fusion.1
  16.8 0.8 constant_dynamic-update-slice_fusion.1
  17.7 1.3 collective-permute-start.2
  19.0 4.5 %collective-permute-start.3 = (f32[10,1,256]{2,1,0:T(1,128)S(1)}, f32[10,1,256]{2,1,0:T(1,128)S(1)}, u32[]{:S(2)}, u32[]{:S(2)}) collective-permute-start(f32[10,1,256]{2,1,0:T(1,128)S(1)} %get-tuple-element.32), channel_id=1, source_target_pairs={{0,1},{1,2},{2,3},{4,5},{5,6},{6,7},{8,9},{9,10},{10,11},{12,13},{... | collective-permute-start | bytes 30728 | tf_op jit(solution)/shard_map/ppermute | solution.py:18
  24.5 0.9 copy.25
  25.4 2.1 scatter_fusion
  27.6 1.2 add_add_fusion
  28.8 1.3 collective-permute-start.4
  30.1 5.2 %collective-permute-start.5 = (f32[4,1,8,256]{3,2,1,0:T(8,128)S(1)}, f32[4,1,8,256]{3,2,1,0:T(8,128)S(1)}, u32[]{:S(2)}, u32[]{:S(2)}) collective-permute-start(f32[4,1,8,256]{3,2,1,0:T(8,128)S(1)} %get-tuple-element.30), channel_id=1, source_target_pairs={{0,4},{4,8},{8,12},{1,5},{5,9},{9,13},{2,6},{6,10},{10,14},{3,7},{... | collective-permute-start | bytes 98312 | tf_op jit(solution)/shard_map/ppermute | solution.py:18
  35.3 1.6 collective-permute-done.5
  37.0 1.3 collective-permute-start.6
  38.3 4.5 %collective-permute-start.7 = (f32[4,10,1,256]{3,2,1,0:T(1,128)S(1)}, f32[4,10,1,256]{3,2,1,0:T(1,128)S(1)}, u32[]{:S(2)}, u32[]{:S(2)}) collective-permute-start(f32[4,10,1,256]{3,2,1,0:T(1,128)S(1)} %get-tuple-element.23), channel_id=1, source_target_pairs={{0,1},{1,2},{2,3},{4,5},{5,6},{6,7},{8,9},{9,10},{10,11},{12,13},{... | collective-permute-start | bytes 122888 | tf_op jit(solution)/shard_map/ppermute | solution.py:18
  43.1 1.4 collective-permute-done.7
  44.8 1.3 collective-permute-start.8
  46.1 5.4 %collective-permute-start.9 = (f32[4,1,8,256]{3,2,1,0:T(8,128)S(1)}, f32[4,1,8,256]{3,2,1,0:T(8,128)S(1)}, u32[]{:S(2)}, u32[]{:S(2)}) collective-permute-start(f32[4,1,8,256]{3,2,1,0:T(8,128)S(1)} %get-tuple-element.28), channel_id=1, source_target_pairs={{0,4},{4,8},{8,12},{1,5},{5,9},{9,13},{2,6},{6,10},{10,14},{3,7},{... | collective-permute-start | bytes 98312 | tf_op jit(solution)/shard_map/ppermute | solution.py:18
  51.5 1.6 collective-permute-done.9
  53.2 1.3 collective-permute-start.10
  54.5 4.9 %collective-permute-start.11 = (f32[4,10,1,256]{3,2,1,0:T(1,128)S(1)}, f32[4,10,1,256]{3,2,1,0:T(1,128)S(1)}, u32[]{:S(2)}, u32[]{:S(2)}) collective-permute-start(f32[4,10,1,256]{3,2,1,0:T(1,128)S(1)} %get-tuple-element.21), channel_id=1, source_target_pairs={{0,1},{1,2},{2,3},{4,5},{5,6},{6,7},{8,9},{9,10},{10,11},{12,13},{... | collective-permute-start | bytes 122888 | tf_op jit(solution)/shard_map/ppermute | solution.py:18
  59.7 1.3 collective-permute-done.11
  61.3 4.7 %copy.20 = f32[4,8,8,256]{0,3,2,1:T(8,128)} copy(f32[4,8,8,256]{3,2,1,0:T(8,128)S(1)} %fusion.14) | data formatting | bytes 524288 | tf_op jit(solution)/shard_map/div | solution.py:64
  65.9 14.1 %gather_fusion.2 = f32[4096,4]{1,0:T(8,128)S(1)} fusion(f32[4,16384]{0,1:T(8,128)} %bitcast.38, s32[4096]{0:T(1024)S(1)} %broadcast_clamp_fusion), kind=kCustom, calls=%fused_computation.2 | custom fusion | bytes 147456 | tf_op jit(solution)/shard_map/gather | solution.py:101
  80.9 46.5 %psum.7 = f32[4]{0:T(128)S(1)} all-reduce(f32[4]{0:T(128)S(1)} %multiply_reduce_fusion), channel_id=1, replica_groups=mesh['test'=2,'bx'=4,'by'=4] {'bx','by'}, use_global_device_ids=true, to_apply=%region_3.4 | all-reduce | flops 4 | bytes 32 | tf_op jit(solution)/shard_map/psum | solution.py:104
  127.5 26.1 %scatter_custom_fusion.1 = f32[4,16384]{0,1:T(8,128)} fusion(s32[4096]{0:T(1024)S(1)} %bitcast.41, f32[]{:T(128)} %constant.21.clone.1, f32[4,512]{0,1:T(8,128)S(1)} %broadcast_divide_fusion), kind=kCustom, calls=%fused_computation.5 | custom fusion | flops 16384 | bytes 524292 | tf_op jit(solution)/shard_map/scatter-add | solution.py:110
  153.6 5.2 %copy.24 = f32[4,8,8,256]{3,2,1,0:T(8,128)S(1)} copy(f32[4,8,8,256]{0,3,2,1:T(8,128)} %bitcast.37) | data formatting | bytes 524288 | tf_op jit(solution)/shard_map/reshape | solution.py:113
  158.9 1.3 collective-permute-start.12
  160.2 4.5 %collective-permute-start.13 = (f32[4,1,8,256]{3,2,1,0:T(8,128)S(1)}, f32[4,1,8,256]{3,2,1,0:T(8,128)S(1)}, u32[]{:S(2)}, u32[]{:S(2)}) collective-permute-start(f32[4,1,8,256]{3,2,1,0:T(8,128)S(1)} %get-tuple-element.26), channel_id=1, source_target_pairs={{0,4},{4,8},{8,12},{1,5},{5,9},{9,13},{2,6},{6,10},{10,14},{3,7},{... | collective-permute-start | bytes 98312 | tf_op jit(solution)/shard_map/ppermute | solution.py:18
  164.8 1.6 collective-permute-done.13
  166.4 1.3 collective-permute-start.14
  167.7 4.5 %collective-permute-start.15 = (f32[4,10,1,256]{3,2,1,0:T(1,128)S(1)}, f32[4,10,1,256]{3,2,1,0:T(1,128)S(1)}, u32[]{:S(2)}, u32[]{:S(2)}) collective-permute-start(f32[4,10,1,256]{3,2,1,0:T(1,128)S(1)} %get-tuple-element.19), channel_id=1, source_target_pairs={{0,1},{1,2},{2,3},{4,5},{5,6},{6,7},{8,9},{9,10},{10,11},{12,13},{... | collective-permute-start | bytes 122888 | tf_op jit(solution)/shard_map/ppermute | solution.py:18
  172.3 1.6 collective-permute-done.15
  174.2 1.3 collective-permute-start.16
  175.5 4.9 %collective-permute-start.17 = (f32[4,1,8,256]{3,2,1,0:T(8,128)S(1)}, f32[4,1,8,256]{3,2,1,0:T(8,128)S(1)}, u32[]{:S(2)}, u32[]{:S(2)}) collective-permute-start(f32[4,1,8,256]{3,2,1,0:T(8,128)S(1)} %get-tuple-element.24), channel_id=1, source_target_pairs={{0,4},{4,8},{8,12},{1,5},{5,9},{9,13},{2,6},{6,10},{10,14},{3,7},{... | collective-permute-start | bytes 98312 | tf_op jit(solution)/shard_map/ppermute | solution.py:18
  180.4 1.6 collective-permute-done.17
  182.0 1.3 collective-permute-start.18
  183.3 4.9 %collective-permute-start.19 = (f32[4,10,1,256]{3,2,1,0:T(1,128)S(1)}, f32[4,10,1,256]{3,2,1,0:T(1,128)S(1)}, u32[]{:S(2)}, u32[]{:S(2)}) collective-permute-start(f32[4,10,1,256]{3,2,1,0:T(1,128)S(1)} %get-tuple-element.17), channel_id=1, source_target_pairs={{0,1},{1,2},{2,3},{4,5},{5,6},{6,7},{8,9},{9,10},{10,11},{12,13},{... | collective-permute-start | bytes 122888 | tf_op jit(solution)/shard_map/ppermute | solution.py:18
  188.2 1.6 collective-permute-done.19
  190.1 1.3 collective-permute-start.20
  191.4 5.4 %collective-permute-start.21 = (f32[8,1,8,256]{3,2,1,0:T(8,128)S(1)}, f32[8,1,8,256]{3,2,1,0:T(8,128)S(1)}, u32[]{:S(2)}, u32[]{:S(2)}) collective-permute-start(f32[8,1,8,256]{3,2,1,0:T(8,128)S(1)} %get-tuple-element.14), channel_id=1, source_target_pairs={{0,4},{4,8},{8,12},{1,5},{5,9},{9,13},{2,6},{6,10},{10,14},{3,7},{... | collective-permute-start | bytes 196616 | tf_op jit(solution)/shard_map/ppermute | solution.py:18
  197.1 1.6 collective-permute-done.21
  198.8 1.3 collective-permute-start.22
  200.1 4.9 %collective-permute-start.23 = (f32[8,10,1,256]{3,2,1,0:T(1,128)S(1)}, f32[8,10,1,256]{3,2,1,0:T(1,128)S(1)}, u32[]{:S(2)}, u32[]{:S(2)}) collective-permute-start(f32[8,10,1,256]{3,2,1,0:T(1,128)S(1)} %get-tuple-element.13), channel_id=1, source_target_pairs={{0,1},{1,2},{2,3},{4,5},{5,6},{6,7},{8,9},{9,10},{10,11},{12,13},{... | collective-permute-start | bytes 245768 | tf_op jit(solution)/shard_map/ppermute | solution.py:18
  205.5 1.6 collective-permute-done.23
  207.0 1.1 fusion.34
  208.2 13.7 %reduce-scatter.2.cloned.1.call-done = f32[8,8,128]{2,1,0:T(8,128)} async-done(((f32[8,8,256]{2,1,0:T(8,128)}), f32[8,8,128]{2,1,0:T(8,128)}) %reduce-scatter.2.cloned.1.call-update) | async-done | bytes 32784 | tf_op jit(solution)/shard_map/reduce_scatter | solution.py:149
  221.8 1.4 broadcast_multiply_fusion
  (61 shorter events, 7.0 us)
Async XLA Ops:
  6.5 52.8 %copy-start = (s32[512]{0:T(512)S(1)}, s32[512]{0:T(512)}, u32[]{:S(2)}) copy-start(s32[512]{0:T(512)} %param.15) | copy-start | bytes 6148
  6.5 53.0 %copy-start.1 = (f32[4,512]{1,0:T(4,128)S(1)}, f32[4,512]{1,0:T(4,128)}, u32[]{:S(2)}) copy-start(f32[4,512]{1,0:T(4,128)} %param.14) | copy-start | bytes 24580
  6.5 215.3 %reduce-scatter.2.cloned.1.call-start = ((), (), s32[]{:S(2)}) async-start(), calls=%async_computation.1 | async-start | bytes 98304 | tf_op jit(solution)/shard_map/reduce_scatter | solution.py:149
  7.3 9.6 %collective-permute-start.1 = (f32[1,8,256]{2,1,0:T(8,128)S(1)}, f32[1,8,256]{2,1,0:T(8,128)S(1)}, u32[]{:S(2)}, u32[]{:S(2)}) collective-permute-start(f32[1,8,256]{2,1,0:T(8,128)S(1)} %get-tuple-element.35), channel_id=1, source_target_pairs={{0,4},{4,8},{8,12},{1,5},{5,9},{9,13},{2,6},{6,10},{10,14},{3,7},{... | collective-permute-start | bytes 24584 | tf_op jit(solution)/shard_map/ppermute | solution.py:18
  12.1 5.6 %collective-permute-start = (f32[1,8,256]{2,1,0:T(8,128)S(1)}, f32[1,8,256]{2,1,0:T(8,128)S(1)}, u32[]{:S(2)}, u32[]{:S(2)}) collective-permute-start(f32[1,8,256]{2,1,0:T(8,128)S(1)} %get-tuple-element.34), channel_id=1, source_target_pairs={{4,0},{8,4},{12,8},{5,1},{9,5},{13,9},{6,2},{10,6},{14,10},{7,3},{... | collective-permute-start | bytes 24584 | tf_op jit(solution)/shard_map/ppermute | solution.py:21
  17.7 9.8 %collective-permute-start.2 = (f32[10,1,256]{2,1,0:T(1,128)S(1)}, f32[10,1,256]{2,1,0:T(1,128)S(1)}, u32[]{:S(2)}, u32[]{:S(2)}) collective-permute-start(f32[10,1,256]{2,1,0:T(1,128)S(1)} %get-tuple-element.33), channel_id=1, source_target_pairs={{1,0},{2,1},{3,2},{5,4},{6,5},{7,6},{9,8},{10,9},{11,10},{13,12},{... | collective-permute-start | bytes 30728 | tf_op jit(solution)/shard_map/ppermute | solution.py:21
  19.0 8.6 %collective-permute-start.3 = (f32[10,1,256]{2,1,0:T(1,128)S(1)}, f32[10,1,256]{2,1,0:T(1,128)S(1)}, u32[]{:S(2)}, u32[]{:S(2)}) collective-permute-start(f32[10,1,256]{2,1,0:T(1,128)S(1)} %get-tuple-element.32), channel_id=1, source_target_pairs={{0,1},{1,2},{2,3},{4,5},{5,6},{6,7},{8,9},{9,10},{10,11},{12,13},{... | collective-permute-start | bytes 30728 | tf_op jit(solution)/shard_map/ppermute | solution.py:18
  28.8 6.5 %collective-permute-start.4 = (f32[4,1,8,256]{3,2,1,0:T(8,128)S(1)}, f32[4,1,8,256]{3,2,1,0:T(8,128)S(1)}, u32[]{:S(2)}, u32[]{:S(2)}) collective-permute-start(f32[4,1,8,256]{3,2,1,0:T(8,128)S(1)} %get-tuple-element.31), channel_id=1, source_target_pairs={{4,0},{8,4},{12,8},{5,1},{9,5},{13,9},{6,2},{10,6},{14,10},{7,3},{... | collective-permute-start | bytes 98312 | tf_op jit(solution)/shard_map/ppermute | solution.py:21
  30.1 6.8 %collective-permute-start.5 = (f32[4,1,8,256]{3,2,1,0:T(8,128)S(1)}, f32[4,1,8,256]{3,2,1,0:T(8,128)S(1)}, u32[]{:S(2)}, u32[]{:S(2)}) collective-permute-start(f32[4,1,8,256]{3,2,1,0:T(8,128)S(1)} %get-tuple-element.30), channel_id=1, source_target_pairs={{0,4},{4,8},{8,12},{1,5},{5,9},{9,13},{2,6},{6,10},{10,14},{3,7},{... | collective-permute-start | bytes 98312 | tf_op jit(solution)/shard_map/ppermute | solution.py:18
  37.0 6.1 %collective-permute-start.6 = (f32[4,10,1,256]{3,2,1,0:T(1,128)S(1)}, f32[4,10,1,256]{3,2,1,0:T(1,128)S(1)}, u32[]{:S(2)}, u32[]{:S(2)}) collective-permute-start(f32[4,10,1,256]{3,2,1,0:T(1,128)S(1)} %get-tuple-element.22), channel_id=1, source_target_pairs={{1,0},{2,1},{3,2},{5,4},{6,5},{7,6},{9,8},{10,9},{11,10},{13,12},{... | collective-permute-start | bytes 122888 | tf_op jit(solution)/shard_map/ppermute | solution.py:21
  38.3 6.2 %collective-permute-start.7 = (f32[4,10,1,256]{3,2,1,0:T(1,128)S(1)}, f32[4,10,1,256]{3,2,1,0:T(1,128)S(1)}, u32[]{:S(2)}, u32[]{:S(2)}) collective-permute-start(f32[4,10,1,256]{3,2,1,0:T(1,128)S(1)} %get-tuple-element.23), channel_id=1, source_target_pairs={{0,1},{1,2},{2,3},{4,5},{5,6},{6,7},{8,9},{9,10},{10,11},{12,13},{... | collective-permute-start | bytes 122888 | tf_op jit(solution)/shard_map/ppermute | solution.py:18
  44.8 6.8 %collective-permute-start.8 = (f32[4,1,8,256]{3,2,1,0:T(8,128)S(1)}, f32[4,1,8,256]{3,2,1,0:T(8,128)S(1)}, u32[]{:S(2)}, u32[]{:S(2)}) collective-permute-start(f32[4,1,8,256]{3,2,1,0:T(8,128)S(1)} %get-tuple-element.29), channel_id=1, source_target_pairs={{4,0},{8,4},{12,8},{5,1},{9,5},{13,9},{6,2},{10,6},{14,10},{7,3},{... | collective-permute-start | bytes 98312 | tf_op jit(solution)/shard_map/ppermute | solution.py:21
  46.1 7.0 %collective-permute-start.9 = (f32[4,1,8,256]{3,2,1,0:T(8,128)S(1)}, f32[4,1,8,256]{3,2,1,0:T(8,128)S(1)}, u32[]{:S(2)}, u32[]{:S(2)}) collective-permute-start(f32[4,1,8,256]{3,2,1,0:T(8,128)S(1)} %get-tuple-element.28), channel_id=1, source_target_pairs={{0,4},{4,8},{8,12},{1,5},{5,9},{9,13},{2,6},{6,10},{10,14},{3,7},{... | collective-permute-start | bytes 98312 | tf_op jit(solution)/shard_map/ppermute | solution.py:18
  53.2 6.5 %collective-permute-start.10 = (f32[4,10,1,256]{3,2,1,0:T(1,128)S(1)}, f32[4,10,1,256]{3,2,1,0:T(1,128)S(1)}, u32[]{:S(2)}, u32[]{:S(2)}) collective-permute-start(f32[4,10,1,256]{3,2,1,0:T(1,128)S(1)} %get-tuple-element.20), channel_id=1, source_target_pairs={{1,0},{2,1},{3,2},{5,4},{6,5},{7,6},{9,8},{10,9},{11,10},{13,12},{... | collective-permute-start | bytes 122888 | tf_op jit(solution)/shard_map/ppermute | solution.py:21
  54.5 6.5 %collective-permute-start.11 = (f32[4,10,1,256]{3,2,1,0:T(1,128)S(1)}, f32[4,10,1,256]{3,2,1,0:T(1,128)S(1)}, u32[]{:S(2)}, u32[]{:S(2)}) collective-permute-start(f32[4,10,1,256]{3,2,1,0:T(1,128)S(1)} %get-tuple-element.21), channel_id=1, source_target_pairs={{0,1},{1,2},{2,3},{4,5},{5,6},{6,7},{8,9},{9,10},{10,11},{12,13},{... | collective-permute-start | bytes 122888 | tf_op jit(solution)/shard_map/ppermute | solution.py:18
  158.9 5.9 %collective-permute-start.12 = (f32[4,1,8,256]{3,2,1,0:T(8,128)S(1)}, f32[4,1,8,256]{3,2,1,0:T(8,128)S(1)}, u32[]{:S(2)}, u32[]{:S(2)}) collective-permute-start(f32[4,1,8,256]{3,2,1,0:T(8,128)S(1)} %get-tuple-element.27), channel_id=1, source_target_pairs={{4,0},{8,4},{12,8},{5,1},{9,5},{13,9},{6,2},{10,6},{14,10},{7,3},{... | collective-permute-start | bytes 98312 | tf_op jit(solution)/shard_map/ppermute | solution.py:21
  160.2 6.1 %collective-permute-start.13 = (f32[4,1,8,256]{3,2,1,0:T(8,128)S(1)}, f32[4,1,8,256]{3,2,1,0:T(8,128)S(1)}, u32[]{:S(2)}, u32[]{:S(2)}) collective-permute-start(f32[4,1,8,256]{3,2,1,0:T(8,128)S(1)} %get-tuple-element.26), channel_id=1, source_target_pairs={{0,4},{4,8},{8,12},{1,5},{5,9},{9,13},{2,6},{6,10},{10,14},{3,7},{... | collective-permute-start | bytes 98312 | tf_op jit(solution)/shard_map/ppermute | solution.py:18
  166.4 5.9 %collective-permute-start.14 = (f32[4,10,1,256]{3,2,1,0:T(1,128)S(1)}, f32[4,10,1,256]{3,2,1,0:T(1,128)S(1)}, u32[]{:S(2)}, u32[]{:S(2)}) collective-permute-start(f32[4,10,1,256]{3,2,1,0:T(1,128)S(1)} %get-tuple-element.18), channel_id=1, source_target_pairs={{1,0},{2,1},{3,2},{5,4},{6,5},{7,6},{9,8},{10,9},{11,10},{13,12},{... | collective-permute-start | bytes 122888 | tf_op jit(solution)/shard_map/ppermute | solution.py:21
  167.7 6.2 %collective-permute-start.15 = (f32[4,10,1,256]{3,2,1,0:T(1,128)S(1)}, f32[4,10,1,256]{3,2,1,0:T(1,128)S(1)}, u32[]{:S(2)}, u32[]{:S(2)}) collective-permute-start(f32[4,10,1,256]{3,2,1,0:T(1,128)S(1)} %get-tuple-element.19), channel_id=1, source_target_pairs={{0,1},{1,2},{2,3},{4,5},{5,6},{6,7},{8,9},{9,10},{10,11},{12,13},{... | collective-permute-start | bytes 122888 | tf_op jit(solution)/shard_map/ppermute | solution.py:18
  174.2 6.2 %collective-permute-start.16 = (f32[4,1,8,256]{3,2,1,0:T(8,128)S(1)}, f32[4,1,8,256]{3,2,1,0:T(8,128)S(1)}, u32[]{:S(2)}, u32[]{:S(2)}) collective-permute-start(f32[4,1,8,256]{3,2,1,0:T(8,128)S(1)} %get-tuple-element.25), channel_id=1, source_target_pairs={{4,0},{8,4},{12,8},{5,1},{9,5},{13,9},{6,2},{10,6},{14,10},{7,3},{... | collective-permute-start | bytes 98312 | tf_op jit(solution)/shard_map/ppermute | solution.py:21
  175.5 6.4 %collective-permute-start.17 = (f32[4,1,8,256]{3,2,1,0:T(8,128)S(1)}, f32[4,1,8,256]{3,2,1,0:T(8,128)S(1)}, u32[]{:S(2)}, u32[]{:S(2)}) collective-permute-start(f32[4,1,8,256]{3,2,1,0:T(8,128)S(1)} %get-tuple-element.24), channel_id=1, source_target_pairs={{0,4},{4,8},{8,12},{1,5},{5,9},{9,13},{2,6},{6,10},{10,14},{3,7},{... | collective-permute-start | bytes 98312 | tf_op jit(solution)/shard_map/ppermute | solution.py:18
  182.0 6.2 %collective-permute-start.18 = (f32[4,10,1,256]{3,2,1,0:T(1,128)S(1)}, f32[4,10,1,256]{3,2,1,0:T(1,128)S(1)}, u32[]{:S(2)}, u32[]{:S(2)}) collective-permute-start(f32[4,10,1,256]{3,2,1,0:T(1,128)S(1)} %get-tuple-element.16), channel_id=1, source_target_pairs={{1,0},{2,1},{3,2},{5,4},{6,5},{7,6},{9,8},{10,9},{11,10},{13,12},{... | collective-permute-start | bytes 122888 | tf_op jit(solution)/shard_map/ppermute | solution.py:21
  183.3 6.5 %collective-permute-start.19 = (f32[4,10,1,256]{3,2,1,0:T(1,128)S(1)}, f32[4,10,1,256]{3,2,1,0:T(1,128)S(1)}, u32[]{:S(2)}, u32[]{:S(2)}) collective-permute-start(f32[4,10,1,256]{3,2,1,0:T(1,128)S(1)} %get-tuple-element.17), channel_id=1, source_target_pairs={{0,1},{1,2},{2,3},{4,5},{5,6},{6,7},{8,9},{9,10},{10,11},{12,13},{... | collective-permute-start | bytes 122888 | tf_op jit(solution)/shard_map/ppermute | solution.py:18
  190.1 7.1 %collective-permute-start.20 = (f32[8,1,8,256]{3,2,1,0:T(8,128)S(1)}, f32[8,1,8,256]{3,2,1,0:T(8,128)S(1)}, u32[]{:S(2)}, u32[]{:S(2)}) collective-permute-start(f32[8,1,8,256]{3,2,1,0:T(8,128)S(1)} %get-tuple-element.15), channel_id=1, source_target_pairs={{4,0},{8,4},{12,8},{5,1},{9,5},{13,9},{6,2},{10,6},{14,10},{7,3},{... | collective-permute-start | bytes 196616 | tf_op jit(solution)/shard_map/ppermute | solution.py:21
  191.4 7.3 %collective-permute-start.21 = (f32[8,1,8,256]{3,2,1,0:T(8,128)S(1)}, f32[8,1,8,256]{3,2,1,0:T(8,128)S(1)}, u32[]{:S(2)}, u32[]{:S(2)}) collective-permute-start(f32[8,1,8,256]{3,2,1,0:T(8,128)S(1)} %get-tuple-element.14), channel_id=1, source_target_pairs={{0,4},{4,8},{8,12},{1,5},{5,9},{9,13},{2,6},{6,10},{10,14},{3,7},{... | collective-permute-start | bytes 196616 | tf_op jit(solution)/shard_map/ppermute | solution.py:18
  198.8 6.6 %collective-permute-start.22 = (f32[8,10,1,256]{3,2,1,0:T(1,128)S(1)}, f32[8,10,1,256]{3,2,1,0:T(1,128)S(1)}, u32[]{:S(2)}, u32[]{:S(2)}) collective-permute-start(f32[8,10,1,256]{3,2,1,0:T(1,128)S(1)} %get-tuple-element.12), channel_id=1, source_target_pairs={{1,0},{2,1},{3,2},{5,4},{6,5},{7,6},{9,8},{10,9},{11,10},{13,12},{... | collective-permute-start | bytes 245768 | tf_op jit(solution)/shard_map/ppermute | solution.py:21
  200.1 6.9 %collective-permute-start.23 = (f32[8,10,1,256]{3,2,1,0:T(1,128)S(1)}, f32[8,10,1,256]{3,2,1,0:T(1,128)S(1)}, u32[]{:S(2)}, u32[]{:S(2)}) collective-permute-start(f32[8,10,1,256]{3,2,1,0:T(1,128)S(1)} %get-tuple-element.13), channel_id=1, source_target_pairs={{0,1},{1,2},{2,3},{4,5},{5,6},{6,7},{8,9},{9,10},{10,11},{12,13},{... | collective-permute-start | bytes 245768 | tf_op jit(solution)/shard_map/ppermute | solution.py:18
Sparse Core Ops, SparseCore 0:
  208.3 13.4 reduce-scatter.1
where the time goes:
time: 231 us; the launch traced here: 230 us
  starting transfers between devices  74 us (32%)
  blocking collectives  46.5 us (20%)
  other arithmetic  36.6 us (16%)
  waiting for transfers between devices  29.8 us (13%)
  local copies, waits for them, and re-layouts  29.2 us (13%)
  between operations  13.9 us (6%)
    ppermute x12, starting transfers between devices, with_halo(): lax.ppermute(lax.slice_in_dim(block, block.shape[dim] - width, None, axis...  58.5 us
    psum x1, blocking collectives, per_sweep_terms(): lax.psum(jnp.sum(residual * residual, axis=1), ('bx', 'by')) / well_count  46.5 us
    scatter-add x1, other arithmetic, per_sweep_terms(): jnp.zeros((tests_here, cell_count), jnp.float32)  26.1 us
    ppermute x12, starting transfers between devices, with_halo(): lax.ppermute(lax.slice_in_dim(block, 0, width, axis=dim), axis, backward)  15.5 us
    ppermute x12, waiting for transfers between devices, with_halo(): lax.ppermute(lax.slice_in_dim(block, block.shape[dim] - width, None, axis...  15.3 us
    gather x1, local copies, waits for them, and re-layouts, per_sweep_terms(): heads_field.reshape(tests_here, cell_count)[:, screen_cells]  14.1 us
    reduce_scatter x1, waiting for transfers between devices, local(): lax.psum_scatter(local_sum, 'test', scatter_dimension=2, tiled=True)  13.7 us
    reshape x1, local copies, waits for them, and re-layouts, per_sweep_terms(): adjoint_source.reshape(tests_here, size_x, size_y, size_z)  5.24 us
  transfers between devices with their start and end apart: 25, of which 13 were waited for; matrix products, arithmetic and copies ran while one was open for 4% of the time, Pallas kernels for 0%

commit v1 on v0

v1 whole, which is shorter than its diff:
```python
import functools

import jax
import jax.numpy as jnp
from jax import lax
from jax.experimental import pallas as pl
from jax.experimental.pallas import tpu as pltpu
from jax.sharding import PartitionSpec as P

SCREEN = 8
LANES = 128
DEEP = 4
EPSILON = 1e-06


def row_plan(size):
    rows = []
    for field, reach in ((0, DEEP), (1, DEEP - 1), (2, DEEP - 1)):
        for dx in range(1, reach):
            rows.append((field, dx, reach - dx))
    return rows


def corner_rows(plan):
    return 2 * sum(count for _, _, count in plan)


def block_index(field, dx):
    return (0, DEEP, 2 * DEEP - 1)[field] + dx - 1


def side_partners(axis, count, tests):
    even, odd = [], []
    for test in range(tests):
        for place in range(count):
            me = test * count + place
            other = (test ^ 1 if (test ^ 1) < tests else test) * count + place
            up = place ^ 1
            even.append((me, test * count + up if up < count else other))
            down = ((place + 1) ^ 1) - 1
            odd.append((me, test * count + down if 0 <= down < count else other))
    return even, odd


def swap_sides(send_even, send_odd, axis, tests):
    even, odd = side_partners(axis, lax.axis_size(axis), tests)
    return lax.ppermute(send_even, ("test", axis), even), lax.ppermute(send_odd, ("test", axis), odd)


def pack_y(log_ref, sto_ref, rec_ref, even_ref, odd_ref):
    size_x, size_y, _ = log_ref.shape
    is_even = lax.axis_index("by") % 2 == 0
    rows = 3 * DEEP - 2
    for x in range(size_x):
        start = 0
        for ref, reach in ((log_ref, DEEP), (sto_ref, DEEP - 1), (rec_ref, DEEP - 1)):
            up = ref[x, size_y - reach :, :]
            down = ref[x, :reach, :]
            at = pl.ds(x * rows + start, reach)
            even_ref[at, :] = jnp.where(is_even, up, down)
            odd_ref[at, :] = jnp.where(is_even, down, up)
            start += reach


def pack_x(plan, log_ref, sto_ref, rec_ref, ey_ref, oy_ref, even_ref, odd_ref):
    size_x, size_y, _ = log_ref.shape
    y_even = lax.axis_index("by") % 2 == 0
    x_even = lax.axis_index("bx") % 2 == 0
    rows = 3 * DEEP - 2
    blocks = (3 * DEEP - 2) * size_y
    first = (0, DEEP, 2 * DEEP - 1)
    for field, (ref, reach) in enumerate(((log_ref, DEEP), (sto_ref, DEEP - 1), (rec_ref, DEEP - 1))):
        for dx in range(1, reach + 1):
            up, down = ref[size_x - dx], ref[dx - 1]
            at = pl.ds(block_index(field, dx) * size_y, size_y)
            even_ref[at, :] = jnp.where(x_even, up, down)
            odd_ref[at, :] = jnp.where(x_even, down, up)
    place = blocks
    for field, dx, count in plan:
        reach = DEEP if field == 0 else DEEP - 1
        for x_up, x_down, side in ((size_x - dx, dx - 1, 0), (size_x - dx, dx - 1, 1)):
            parts = []
            for x in (x_up, x_down):
                start = x * rows + first[field] + (reach - count if side == 0 else 0)
                got_e, got_o = ey_ref[pl.ds(start, count), :], oy_ref[pl.ds(start, count), :]
                parts.append(jnp.where(y_even, got_o, got_e) if side == 0 else jnp.where(y_even, got_e, got_o))
            at = pl.ds(place, count)
            even_ref[at, :] = jnp.where(x_even, parts[0], parts[1])
            odd_ref[at, :] = jnp.where(x_even, parts[1], parts[0])
            place += count


def tile_marks(tests):
    sub = lax.broadcasted_iota(jnp.int32, (8, LANES), 0)
    lane = lax.broadcasted_iota(jnp.int32, (8, LANES), 1)
    half = sub // tests
    return sub, lane, half


def shift_up(values, lane, half):
    turned = pltpu.roll(values, LANES - 1, values.ndim - 1)
    crossed = jnp.where(half == 0, pltpu.roll(turned, 4, values.ndim - 2), 0.0)
    return jnp.where(lane == LANES - 1, crossed, turned)


def shift_down(values, lane, half):
    turned = pltpu.roll(values, 1, values.ndim - 1)
    crossed = jnp.where(half == 1, pltpu.roll(turned, 4, values.ndim - 2), 0.0)
    return jnp.where(lane == 0, crossed, turned)


def sum_z(values, lane, half):
    down = pltpu.roll(values, 1, values.ndim - 1)
    up = pltpu.roll(values, LANES - 1, values.ndim - 1)
    crossed = pltpu.roll(jnp.where(lane == 0, down, up), 4, values.ndim - 2)
    edge = ((lane == 0) & (half == 1)) | ((lane == LANES - 1) & (half == 0))
    crossed = jnp.where(edge, crossed, 0.0)
    return jnp.where(lane == 0, crossed, down) + jnp.where(lane == LANES - 1, crossed, up)


def sweep(source_ref, gamma_ref, from_ref, to_ref, low, high, lane, half):
    def one_row(x, carry):
        centre = from_ref[x, low:high]
        total = from_ref[x - 1, low:high] + from_ref[x + 1, low:high]
        total = total + from_ref[x, low - 1 : high - 1] + from_ref[x, low + 1 : high + 1]
        total = total + sum_z(centre, lane, half)
        to_ref[x, low:high] = source_ref[x, low:high] + gamma_ref[x, low:high] * total
        return carry

    lax.fori_loop(low, high, one_row, 0)


def wells_kernel(tests, per_brick, owner_ref, packed_ref, observed_ref, window_ref, own_ref, obs_ref, count_ref, index_ref):
    bricks = count_ref.shape[0]
    for brick in range(bricks):
        count_ref[brick] = 0
    n_wells = owner_ref.shape[0]

    def one_well(well, found):
        brick = owner_ref[well]
        packed = packed_ref[well]
        rank = count_ref[brick]
        count_ref[brick] = rank + 1
        window_ref[found] = packed + ((brick * per_brick + rank) << 16)
        at = jnp.where((packed >> 29) & 1 == 1, rank, per_brick)
        own_ref[at] = packed
        index_ref[at] = well
        return found + ((packed >> 30) & 1)

    found = lax.fori_loop(0, n_wells, one_well, jnp.int32(0), unroll=8)
    window_ref[n_wells] = found
    lane = lax.broadcasted_iota(jnp.int32, (1, LANES), 1)

    def one_value(rank, values):
        well = index_ref[rank]
        for test in range(tests):
            values = jnp.where(lane == test * per_brick + rank, observed_ref[test, well], values)
        return values

    obs_ref[...] = lax.fori_loop(0, per_brick, one_value, jnp.zeros((1, LANES), jnp.float32), unroll=8)


def heads_kernel(
    plan,
    tests,
    per_brick,
    log_ref,
    sto_ref,
    rec_ref,
    ey_ref,
    oy_ref,
    ex_ref,
    ox_ref,
    own_ref,
    obs_ref,
    pump_ref,
    rate_ref,
    gamma_ref,
    delta_ref,
    e_ref,
    inv_e_ref,
    head_ref,
    row_ref,
    log_w,
    sto_w,
    rec_w,
    e_w,
    gam_w,
    del_w,
    bet_w,
    one_ref,
    two_ref,
    bet_ref,
):
    size_x, size_y, size_z = log_ref.shape
    wide_x, wide_y = size_x + 2 * DEEP, size_y + 2 * DEEP
    bx, by = lax.axis_index("bx"), lax.axis_index("by")
    y_even, x_even = by % 2 == 0, bx % 2 == 0
    no_low_y, no_high_y = by == 0, by == lax.axis_size("by") - 1
    no_low_x, no_high_x = bx == 0, bx == lax.axis_size("bx") - 1
    rows = 3 * DEEP - 2
    blocks = rows * size_y
    first = (0, DEEP, 2 * DEEP - 1)
    fields = ((log_ref, log_w, DEEP), (sto_ref, sto_w, DEEP - 1), (rec_ref, rec_w, DEEP - 1))
    for field, (ref, wide, reach) in enumerate(fields):
        fill = 1.0 if field == 1 else 0.0
        wide[...] = jnp.full(wide.shape, fill, jnp.float32)
        for x in range(size_x):
            wide[DEEP + x, DEEP : DEEP + size_y, :] = ref[x]
            at = pl.ds(x * rows + first[field], reach)
            got_e, got_o = ey_ref[at, :], oy_ref[at, :]
            low, high = jnp.where(y_even, got_o, got_e), jnp.where(y_even, got_e, got_o)
            wide[DEEP + x, DEEP - reach : DEEP, :] = jnp.where(no_low_y, fill, low)
            wide[DEEP + x, DEEP + size_y : DEEP + size_y + reach, :] = jnp.where(no_high_y, fill, high)
        for dx in range(1, reach + 1):
            at = pl.ds(block_index(field, dx) * size_y, size_y)
            got_e, got_o = ex_ref[at, :], ox_ref[at, :]
            low, high = jnp.where(x_even, got_o, got_e), jnp.where(x_even, got_e, got_o)
            wide[DEEP - dx, DEEP : DEEP + size_y, :] = jnp.where(no_low_x, fill, low)
            wide[DEEP + size_x + dx - 1, DEEP : DEEP + size_y, :] = jnp.where(no_high_x, fill, high)
    place = blocks
    for field, dx, count in plan:
        wide = fields[field][1]
        fill = 1.0 if field == 1 else 0.0
        for side in (0, 1):
            at = pl.ds(place, count)
            got_e, got_o = ex_ref[at, :], ox_ref[at, :]
            low, high = jnp.where(x_even, got_o, got_e), jnp.where(x_even, got_e, got_o)
            to = pl.ds(DEEP - count, count) if side == 0 else pl.ds(DEEP + size_y, count)
            absent = no_low_y if side == 0 else no_high_y
            wide[DEEP - dx, to, :] = jnp.where(absent | no_low_x, fill, low)
            wide[DEEP + size_x + dx - 1, to, :] = jnp.where(absent | no_high_x, fill, high)
            place += count

    row_at = lax.broadcasted_iota(jnp.int32, (wide_y, size_z), 0)
    z_at = lax.broadcasted_iota(jnp.int32, (wide_y, size_z), 1)
    inside_y = ((row_at >= DEEP) | jnp.logical_not(no_low_y)) & ((row_at < DEEP + size_y) | jnp.logical_not(no_high_y))

    def one_exp(x, carry):
        e_w[x] = jnp.exp(0.5 * log_w[x])
        return carry

    lax.fori_loop(0, wide_x, one_exp, 0)

    def one_row(x, carry):
        e = e_w[x]
        total = e_w[x - 1] + e_w[x + 1]
        total = total + pltpu.roll(e, 1, 0) + pltpu.roll(e, wide_y - 1, 0)
        total = total + jnp.where(z_at == 0, 1.0, pltpu.roll(e, 1, 1))
        total = total + jnp.where(z_at == size_z - 1, 1.0, pltpu.roll(e, size_z - 1, 1))
        inside_x = ((x >= DEEP) | jnp.logical_not(no_low_x)) & ((x < DEEP + size_x) | jnp.logical_not(no_high_x))
        delta = jnp.where(inside_y & inside_x, e / (sto_w[x] + e * total), 0.0)
        del_w[x] = delta
        gam_w[x] = delta * e
        bet_w[x] = delta * rec_w[x]
        return carry

    lax.fori_loop(1, wide_x - 1, one_row, 0)
    sub, lane, half = tile_marks(tests)

    def spread(wide, x, y):
        low = jnp.broadcast_to(wide[x, pl.ds(y, 1), :LANES], (8, LANES))
        high = jnp.broadcast_to(wide[x, pl.ds(y, 1), LANES:], (8, LANES))
        return jnp.where(half == 0, low, high)

    def spread_row(x, carry):
        for y in range(1, wide_y - 1):
            gamma_ref[x, y] = spread(gam_w, x, y)
            delta_ref[x, y] = spread(del_w, x, y)
            bet_ref[x, y] = spread(bet_w, x, y)
        return carry

    lax.fori_loop(1, wide_x - 1, spread_row, 0)

    def spread_near(x, carry):
        for y in range(DEEP - 1, DEEP + size_y + 1):
            e = spread(e_w, x, y)
            e_ref[x, y] = e
            inv_e_ref[x, y] = 1.0 / e
        return carry

    lax.fori_loop(DEEP - 1, DEEP + size_x + 1, spread_near, 0)
    z_of = half * LANES + lane
    for test in range(tests):
        packed = pump_ref[test]

        @pl.when((packed >> 30) & 1 == 1)
        def _(packed=packed, test=test):
            x, y, top = (packed >> 12) & 15, (packed >> 8) & 15, packed & 255
            hit = (z_of >= top) & (z_of < top + SCREEN) & (sub % tests == test)
            bet_ref[x, y] = bet_ref[x, y] - jnp.where(hit, delta_ref[x, y] * rate_ref[test], 0.0)

    sweep(bet_ref, gamma_ref, bet_ref, one_ref, 2, wide_y - 2, lane, half)
    sweep(bet_ref, gamma_ref, one_ref, two_ref, 3, wide_y - 3, lane, half)

    def one_head(x, carry):
        head_ref[x, 3 : wide_y - 3] = two_ref[x, 3 : wide_y - 3] * inv_e_ref[x, 3 : wide_y - 3]
        return carry

    lax.fori_loop(3, wide_x - 3, one_head, 0)
    slot_of = lane - per_brick * (sub % tests)
    gathered = jnp.zeros((8, LANES), jnp.float32)
    for rank in range(per_brick):
        packed = own_ref[rank]
        x, y, top = (packed >> 12) & 15, (packed >> 8) & 15, packed & 255
        hit = (z_of >= top) & (z_of < top + SCREEN)
        mean = jnp.sum(jnp.where(hit, head_ref[x, y], 0.0), axis=1, keepdims=True)
        gathered = jnp.where(slot_of == rank, mean, gathered)
    residual = jnp.sum(gathered, axis=0, keepdims=True) * (1.0 / SCREEN) - obs_ref[...]
    row_ref[...] = jnp.broadcast_to(residual[None], row_ref.shape)


def adjoint_kernel(
    tests,
    per_brick,
    split,
    scale,
    resid_ref,
    window_ref,
    gamma_ref,
    delta_ref,
    e_ref,
    inv_e_ref,
    head_ref,
    *rest,
):
    outs, (weight_ref, bet_ref, one_ref, two_ref, adj_ref) = rest[:-5], rest[-5:]
    wide_x, wide_y = gamma_ref.shape[:2]
    size_x, size_y = wide_x - 2 * DEEP, wide_y - 2 * DEEP
    n_wells = window_ref.shape[0] - 1
    sub, lane, half = tile_marks(tests)
    z_of = half * LANES + lane
    resid = resid_ref[:, 0, :]
    squares = jnp.sum(resid * resid, axis=0, keepdims=True)
    row_lane = lax.broadcasted_iota(jnp.int32, (1, LANES), 1)
    misfit = jnp.zeros((1, LANES), jnp.float32)
    for test in range(tests):
        mine = row_lane // per_brick == test
        total = jnp.sum(jnp.where(mine, squares, 0.0), axis=1, keepdims=True)
        misfit = jnp.where(mine, total / n_wells + EPSILON, misfit)
    weight_ref[...] = resid / misfit

    def clear(x, carry):
        bet_ref[x] = jnp.zeros(bet_ref.shape[1:], jnp.float32)
        return carry

    lax.fori_loop(0, wide_x, clear, 0)
    slot_of = lane - per_brick * (sub % tests)

    def one_well(place, carry):
        packed = window_ref[place]
        x, y, top = (packed >> 12) & 15, (packed >> 8) & 15, packed & 255
        slot = (packed >> 16) & 0x1FFF
        brick, rank = slot // per_brick, slot % per_brick
        row = jnp.broadcast_to(weight_ref[pl.ds(brick, 1), :], (8, LANES))
        value = jnp.sum(jnp.where(slot_of == rank, row, 0.0), axis=1, keepdims=True)
        hit = (z_of >= top) & (z_of < top + SCREEN)
        bet_ref[x, y] = bet_ref[x, y] + jnp.where(hit, value, 0.0)
        return carry

    lax.fori_loop(0, window_ref[n_wells], one_well, 0)

    def scaled(x, carry):
        bet_ref[x, 1 : wide_y - 1] = bet_ref[x, 1 : wide_y - 1] * delta_ref[x, 1 : wide_y - 1]
        return carry

    lax.fori_loop(1, wide_x - 1, scaled, 0)
    sweep(bet_ref, gamma_ref, bet_ref, one_ref, 2, wide_y - 2, lane, half)
    sweep(bet_ref, gamma_ref, one_ref, two_ref, 3, wide_y - 3, lane, half)

    def one_adjoint(x, carry):
        adj_ref[x, 3 : wide_y - 3] = two_ref[x, 3 : wide_y - 3] * inv_e_ref[x, 3 : wide_y - 3]
        return carry

    lax.fori_loop(3, wide_x - 3, one_adjoint, 0)
    own_y = slice(DEEP, DEEP + size_y)

    def one_row(x, carry):
        e, head, adjoint = e_ref[x, own_y], head_ref[x, own_y], adj_ref[x, own_y]

        def face(near_x, near_y):
            gap = (head - head_ref[near_x, near_y]) * (adjoint - adj_ref[near_x, near_y])
            return e_ref[near_x, near_y] * gap

        total = face(x - 1, own_y) + face(x + 1, own_y)
        total = total + face(x, slice(DEEP - 1, DEEP + size_y - 1)) + face(x, slice(DEEP + 1, DEEP + size_y + 1))
        total = total * e
        last = (lane == LANES - 1) & (half == 1)
        e_next = jnp.where(last, 1.0, shift_up(e, lane, half))
        gap = (head - shift_up(head, lane, half)) * (adjoint - shift_up(adjoint, lane, half))
        upper = e * e_next * gap
        begin = (lane == 0) & (half == 0)
        lower = jnp.where(begin, e * head * adjoint, shift_down(upper, lane, half))
        total = (total + upper + lower) * scale
        total = total + pltpu.roll(total, 7, 1)
        total = total + pltpu.roll(total, 6, 1)
        for y in range(size_y):
            low, high = total[y, 0:1], total[y, 4:5]
            if split:
                first = lax.axis_index("test") == 0
                outs[0][x - DEEP, pl.ds(y, 1), :] = jnp.where(first, low, high)
                outs[1][x - DEEP, pl.ds(y, 1), :] = jnp.where(first, high, low)
            else:
                outs[0][x - DEEP, pl.ds(y, 1), :LANES] = low
                outs[0][x - DEEP, pl.ds(y, 1), LANES:] = high
        return carry

    lax.fori_loop(DEEP, DEEP + size_x, one_row, 0)


def vmem():
    return pl.BlockSpec(memory_space=pltpu.VMEM)


def smem():
    return pl.BlockSpec(memory_space=pltpu.SMEM)


def f32(*shape):
    return jax.ShapeDtypeStruct(shape, jnp.float32)


def i32(*shape):
    return jax.ShapeDtypeStruct(shape, jnp.int32)


PARAMS = pltpu.CompilerParams(vmem_limit_bytes=24 * 1024 * 1024)


def local(log_conductivity, storage, recharge, pump_rate, pump_well, observed, owner, screen_column, screen_top):
    size_x, size_y, size_z = log_conductivity.shape
    tests = pump_rate.shape[0]
    n_wells = owner.shape[0]
    groups, n_bx, n_by = lax.axis_size("test"), lax.axis_size("bx"), lax.axis_size("by")
    bricks = n_bx * n_by
    per_brick = n_wells // bricks
    plan = row_plan(size_y)
    rows_y = (3 * DEEP - 2) * size_x
    rows_x = (3 * DEEP - 2) * size_y + corner_rows(plan)
    wide_x, wide_y = size_x + 2 * DEEP, size_y + 2 * DEEP

    bx, by = lax.axis_index("bx"), lax.axis_index("by")
    well_x = (owner // n_by - bx) * size_x + screen_column // size_y + DEEP
    well_y = (owner % n_by - by) * size_y + screen_column % size_y + DEEP
    out_x = jnp.maximum(jnp.maximum(DEEP - well_x, well_x - (DEEP + size_x - 1)), 0)
    out_y = jnp.maximum(jnp.maximum(DEEP - well_y, well_y - (DEEP + size_y - 1)), 0)
    in_window = (out_x + out_y < DEEP).astype(jnp.int32)
    owned = ((out_x == 0) & (out_y == 0)).astype(jnp.int32)
    packed = (in_window << 30) + (owned << 29) + ((well_x & 15) << 12) + ((well_y & 15) << 8) + screen_top
    pump_packed = packed[pump_well]

    even_y, odd_y = pl.pallas_call(
        pack_y,
        out_shape=[f32(rows_y, size_z)] * 2,
        in_specs=[vmem()] * 3,
        out_specs=[vmem()] * 2,
        compiler_params=PARAMS,
        name="pack_y",
    )(log_conductivity, storage, recharge)
    got_even_y, got_odd_y = swap_sides(even_y, odd_y, "by", groups)

    window, own, obs = pl.pallas_call(
        functools.partial(wells_kernel, tests, per_brick),
        out_shape=[i32(n_wells + 1), i32(per_brick + 1), f32(1, LANES)],
        in_specs=[smem()] * 3,
        out_specs=[smem(), smem(), vmem()],
        scratch_shapes=[pltpu.SMEM((bricks,), jnp.int32), pltpu.SMEM((per_brick + 1,), jnp.int32)],
        compiler_params=PARAMS,
        name="wells",
    )(owner, packed, observed)

    even_x, odd_x = pl.pallas_call(
        functools.partial(pack_x, plan),
        out_shape=[f32(rows_x, size_z)] * 2,
        in_specs=[vmem()] * 5,
        out_specs=[vmem()] * 2,
        compiler_params=PARAMS,
        name="pack_x",
    )(log_conductivity, storage, recharge, got_even_y, got_odd_y)
    got_even_x, got_odd_x = swap_sides(even_x, odd_x, "bx", groups)

    tiles = (wide_x, wide_y, 8, LANES)
    wide = (wide_x, wide_y, size_z)
    gamma, delta, e, inv_e, head, row = pl.pallas_call(
        functools.partial(heads_kernel, plan, tests, per_brick),
        out_shape=[f32(*tiles)] * 5 + [f32(bricks, 1, LANES)],
        in_specs=[vmem()] * 7 + [smem(), vmem(), smem(), smem()],
        out_specs=[vmem()] * 6,
        scratch_shapes=[pltpu.VMEM(wide, jnp.float32)] * 7 + [pltpu.VMEM(tiles, jnp.float32)] * 3,
        compiler_params=PARAMS,
        name="heads",
    )(log_conductivity, storage, recharge, got_even_y, got_odd_y, got_even_x, got_odd_x, own, obs, pump_packed, pump_rate)

    residuals = lax.all_to_all(row, ("bx", "by"), 0, 0)

    all_tests = tests * groups
    split = groups == 2
    out_shape = [f32(size_x, size_y, LANES)] * 2 if split else [f32(size_x, size_y, size_z)]
    partial = pl.pallas_call(
        functools.partial(adjoint_kernel, tests, per_brick, split, -0.5 / all_tests),
        out_shape=out_shape,
        in_specs=[vmem(), smem()] + [vmem()] * 5,
        out_specs=[vmem()] * len(out_shape),
        scratch_shapes=[pltpu.VMEM((bricks, LANES), jnp.float32)] + [pltpu.VMEM(tiles, jnp.float32)] * 4,
        compiler_params=PARAMS,
        name="adjoint",
    )(residuals, window, gamma, delta, e, inv_e, head)
    if split:
        return partial[0] + lax.ppermute(partial[1], "test", [(0, 1), (1, 0)])
    return lax.psum_scatter(partial[0], "test", scatter_dimension=2, tiled=True)


def solution(mesh):
    placed = (
        P("bx", "by", None),
        P("bx", "by", None),
        P("bx", "by", None),
        P("test"),
        P("test"),
        P("test", None),
        P(),
        P(),
        P(),
    )
    return jax.shard_map(local, mesh=mesh, in_specs=placed, out_specs=P("bx", "by", "test"), check_vma=False)
```

time: 231 us -> 48.4 us (0.21)
  starting transfers between devices: 74 us -> 5.14 us
  other arithmetic: 36.6 us -> 0.65 us
  blocking collectives: 46.5 us -> 15 us
  waiting for transfers between devices: 29.8 us -> 2.27 us
  local copies, waits for them, and re-layouts: 29.2 us -> 5.21 us
  Pallas kernels: 0 us -> 19.4 us
  between operations: 13.9 us -> 0.1 us
    ppermute x24 -> x5, starting transfers between devices: 74 us -> 5.14 us  [the longest x2 5.07 us: swap_sides(): lax.ppermute(send_even, ('test', axis), even)]
    psum x1 -> x0, blocking collectives: 46.5 us -> none  [per_sweep_terms(): lax.psum(jnp.sum(residual * residual, axis=1), ('bx', 'by')) / well_count]
    scatter-add x2 -> x0, other arithmetic: 28.2 us -> none  [the longest x1 26.1 us: per_sweep_terms(): jnp.zeros((tests_here, cell_count), jnp.float32)]
    pallas_call x0 -> x5, Pallas kernels: none -> 19.4 us  [the longest x1 9.11 us: local(): pl.pallas_call(functools.partial(adjoint_kernel, tests, per_brick, split,...]
    gather x3 -> x1, local copies, waits for them, and re-layouts: 16 us -> 0.64 us  [local(): pump_packed = packed[pump_well]]
    all_to_all x0 -> x1, blocking collectives: none -> 15 us  [local(): residuals = lax.all_to_all(row, ('bx', 'by'), 0, 0)]
    ppermute x24 -> x5, waiting for transfers between devices: 16.2 us -> 2.27 us  [the longest x1 1.19 us: local(): return partial[0] + lax.ppermute(partial[1], 'test', [(0, 1), (1, 0)])]
    reduce_scatter x1 -> x0, waiting for transfers between devices: 13.7 us -> none  [local(): lax.psum_scatter(local_sum, 'test', scatter_dimension=2, tiled=True)]
  transfers between devices with their start and end apart: 25 -> 5, of which waited for: 13 -> 2; matrix products, arithmetic and copies ran while one was open for 4% -> 1% of each run, Pallas kernels for 0% -> 11%
where the time goes in v1:
time: 48.4 us; the launch traced here: 47.8 us
  Pallas kernels  19.4 us (40%)
  blocking collectives  15 us (31%)
  local copies, waits for them, and re-layouts  5.21 us (11%)
  starting transfers between devices  5.14 us (11%)
  waiting for transfers between devices  2.27 us (5%)
  other arithmetic  0.65 us (1%)
    all_to_all x1, blocking collectives, local(): residuals = lax.all_to_all(row, ('bx', 'by'), 0, 0)  15 us
    pallas_call x1, Pallas kernels, local(): pl.pallas_call(functools.partial(adjoint_kernel, tests, per_brick, split,...  9.11 us
    pallas_call x1, Pallas kernels, local(): pl.pallas_call(functools.partial(heads_kernel, plan, tests, per_brick), o...  5.11 us
    pallas_call x1, Pallas kernels, local(): pl.pallas_call(functools.partial(wells_kernel, tests, per_brick), out_sha...  5.09 us
    ppermute x2, starting transfers between devices, swap_sides(): lax.ppermute(send_even, ('test', axis), even)  5.07 us
    unnamed x24, local copies, waits for them, and re-layouts  4.56 us
    ppermute x1, waiting for transfers between devices, local(): return partial[0] + lax.ppermute(partial[1], 'test', [(0, 1), (1, 0)])  1.19 us
    ppermute x2, waiting for transfers between devices, swap_sides(): lax.ppermute(send_even, ('test', axis), even)  1.07 us
  transfers between devices with their start and end apart: 5, of which 2 were waited for; matrix products, arithmetic and copies ran while one was open for 1% of the time, Pallas kernels for 11%

profile of v1, /device:TPU:0, one launch (start us, length us, event | category | flops | bytes accessed | tf_op | source)
XLA Modules:
  0.0 47.8 jit_solution(16725838052291625364)
XLA Ops:
  0.0 0.0 copy-start
  0.0 0.8 %copy-done = f32[8,8,256]{2,1,0:T(8,128)S(1)} copy-done((f32[8,8,256]{2,1,0:T(8,128)S(1)}, f32[8,8,256]{2,1,0:T(8,128)}, u32[]{:S(2)}) %copy-start) | copy-done | bytes 65560
  0.8 0.0 copy-start.2
  0.8 0.8 %copy-done.2 = f32[8,8,256]{2,1,0:T(8,128)S(1)} copy-done((f32[8,8,256]{2,1,0:T(8,128)S(1)}, f32[8,8,256]{2,1,0:T(8,128)}, u32[]{:S(2)}) %copy-start.2) | copy-done | bytes 65560
  1.7 0.0 copy-start.4
  1.7 0.8 %copy-done.4 = f32[8,8,256]{2,1,0:T(8,128)S(1)} copy-done((f32[8,8,256]{2,1,0:T(8,128)S(1)}, f32[8,8,256]{2,1,0:T(8,128)}, u32[]{:S(2)}) %copy-start.4) | copy-done | bytes 65560
  2.5 0.0 copy-start.1
  2.5 0.0 copy-start.3
  2.5 0.0 copy-start.5
  2.5 0.1 pack_y.1
  2.6 3.1 %collective-permute-start = (f32[80,256]{1,0:T(8,128)S(1)}, f32[80,256]{1,0:T(8,128)S(1)}, u32[]{:S(2)}, u32[]{:S(2)}) collective-permute-start(f32[80,256]{1,0:T(8,128)S(1)} %get-tuple-element.20), channel_id=1, source_target_pairs={{0,1},{1,0},{2,3},{3,2},{16,17},{17,16},{18,19},{19,18},{4,5},{5,4... | collective-permute-start | bytes 245768 | tf_op jit(solution)/shard_map/ppermute | solution.py:47
  5.7 0.0 collective-permute-start.1
  5.7 0.0 copy-start.10
  5.7 0.0 copy-start.9
  5.7 0.0 copy-start.7
  5.7 0.7 %copy-done.10 = s32[512]{0:T(512)S(1)} copy-done((s32[512]{0:T(512)S(1)}, s32[512]{0:T(512)}, u32[]{:S(2)}) %copy-start.10) | copy-done | bytes 2072
  6.4 0.0 copy-done.9
  6.4 0.0 copy-done.7
  6.4 0.0 copy-start.11
  6.4 0.6 %copy-done.11 = s32[4]{0:T(128)S(1)} copy-done((s32[4]{0:T(128)S(1)}, s32[4]{0:T(128)}, u32[]{:S(2)}) %copy-start.11) | copy-done | bytes 40
  7.1 1.1 %collective-permute-done.ey_ref = f32[80,256]{1,0:T(8,128)S(1)} collective-permute-done((f32[80,256]{1,0:T(8,128)S(1)}, f32[80,256]{1,0:T(8,128)S(1)}, u32[]{:S(2)}, u32[]{:S(2)}) %collective-permute-start) | collective-permute-done | bytes 81952 | tf_op jit(solution)/shard_map/ppermute | solution.py:47
  8.1 0.0 collective-permute-done.1.oy_ref
  8.1 0.0 copy-done.1
  8.1 0.0 copy-done.3
  8.1 0.0 copy-done.5
  8.1 0.1 pack_x.1
  8.2 2.0 %collective-permute-start.2 = (f32[104,256]{1,0:T(8,128)S(1)}, f32[104,256]{1,0:T(8,128)S(1)}, u32[]{:S(2)}, u32[]{:S(2)}) collective-permute-start(f32[104,256]{1,0:T(8,128)S(1)} %get-tuple-element.22), channel_id=1, source_target_pairs={{0,4},{4,0},{8,12},{12,8},{16,20},{20,16},{24,28},{28,24},{1,5},{5... | collective-permute-start | bytes 319496 | tf_op jit(solution)/shard_map/ppermute | solution.py:47
  10.2 0.0 collective-permute-start.3
  10.2 0.0 copy-start.6
  10.2 0.6 %gather_fusion = s32[4]{0:T(128)S(1)} fusion(s32[512]{0:T(512)S(1)} %add_add_fusion.packed_ref, s32[1024]{0:T(1024)S(1)} %pad_clamp_fusion), kind=kCustom, calls=%fused_computation | custom fusion | bytes 48 | tf_op jit(solution)/shard_map/gather | solution.py:450
  10.9 0.0 copy-done.6
  10.9 5.1 %wells.1 = (s32[513]{0:T(1024)S(1)}, s32[33]{0:T(128)S(1)}, f32[1,128]{1,0:T(1,128)S(1)}) custom-call(s32[512]{0:T(512)S(1)} %copy-done.7, s32[512]{0:T(512)S(1)} %add_add_fusion.packed_ref, f32[4,512]{1,0:T(4,128)S(1)} %copy-done.6), custom_call_target="tpu_custom_call" | custom-call | tf_op jit(solution)/shard_map/wells/pallas_call | solution.py:462
  16.0 0.0 collective-permute-done.2.ex_ref
  16.0 0.0 collective-permute-done.3.ox_ref
  16.0 0.0 copy-start.8
  16.0 0.6 %copy-done.8 = f32[4]{0:T(128)S(1)} copy-done((f32[4]{0:T(128)S(1)}, f32[4]{0:T(128)}, u32[]{:S(2)}) %copy-start.8) | copy-done | bytes 40
  16.7 5.1 %heads.1 = (f32[16,16,8,128]{3,2,1,0:T(8,128)S(1)}, f32[16,16,8,128]{3,2,1,0:T(8,128)S(1)}, f32[16,16,8,128]{3,2,1,0:T(8,128)S(1)}, f32[16,16,8,128]{3,2,1,0:T(8...) custom-call(f32[8,8,256]{2,1,0:T(8,128)S(1)} %copy-done.1, f32[8,8,256]{2,1,0:T(8,128)S(1)} %copy-done.3, ...), custom_call_target="tpu_custom_call" | custom-call | tf_op jit(solution)/shard_map/heads/pallas_call | solution.py:484
  21.8 15.0 %all_to_all.5.resid_ref = f32[16,1,128]{2,1,0:T(1,128)S(1)} all-to-all(f32[16,1,128]{2,1,0:T(1,128)S(1)} %get-tuple-element.26), channel_id=1, replica_groups=mesh['test'=2,'bx'=4,'by'=4] {'bx','by'}, dimensions={0} | all-to-all | bytes 16384 | tf_op jit(solution)/shard_map/all_to_all | solution.py:494
  36.8 9.1 %adjoint.1 = (f32[8,8,128]{2,1,0:T(8,128)S(1)}, f32[8,8,128]{2,1,0:T(8,128)S(1)}) custom-call(f32[16,1,128]{2,1,0:T(1,128)S(1)} %all_to_all.5.resid_ref, s32[513]{0:T(1024)S(1)} %get-tuple-element.27.window_ref, f32[16,16,8,128]{3,2,1,0:T(8,128)S(1)} %get-tuple-element.28.gamma_ref, f32[16,16,8,128]{3,2,1,0:T(8,128)S(1)} %get-tuple-element.29.delta_ref, ...), custom_call_target="tpu_custom_call" | custom-call | tf_op jit(solution)/shard_map/adjoint/pallas_call | solution.py:499
  45.9 0.1 collective-permute-start.4
  46.0 1.2 %collective-permute-done.4 = f32[8,8,128]{2,1,0:T(8,128)S(1)} collective-permute-done((f32[8,8,128]{2,1,0:T(8,128)S(1)}, f32[8,8,128]{2,1,0:T(8,128)S(1)}, u32[]{:S(2)}, u32[]{:S(2)}) %collective-permute-start.4) | collective-permute-done | bytes 32800 | tf_op jit(solution)/shard_map/ppermute | solution.py:509
  47.2 0.6 %add.63 = f32[8,8,128]{2,1,0:T(8,128)} add(f32[8,8,128]{2,1,0:T(8,128)S(1)} %get-tuple-element.33, f32[8,8,128]{2,1,0:T(8,128)S(1)} %collective-permute-done.4) | non-fusion elementwise | flops 8192 | bytes 98304 | tf_op jit(solution)/shard_map/add | solution.py:509
  (3 shorter events, 0.0 us)
Async XLA Ops:
  0.0 0.8 %copy-start = (f32[8,8,256]{2,1,0:T(8,128)S(1)}, f32[8,8,256]{2,1,0:T(8,128)}, u32[]{:S(2)}) copy-start(f32[8,8,256]{2,1,0:T(8,128)} %log_ref.5) | copy-start | bytes 196612
  0.8 0.8 %copy-start.2 = (f32[8,8,256]{2,1,0:T(8,128)S(1)}, f32[8,8,256]{2,1,0:T(8,128)}, u32[]{:S(2)}) copy-start(f32[8,8,256]{2,1,0:T(8,128)} %sto_ref.5) | copy-start | bytes 196612
  1.7 0.8 %copy-start.4 = (f32[8,8,256]{2,1,0:T(8,128)S(1)}, f32[8,8,256]{2,1,0:T(8,128)}, u32[]{:S(2)}) copy-start(f32[8,8,256]{2,1,0:T(8,128)} %rec_ref.5) | copy-start | bytes 196612
  2.5 5.6 %copy-start.1 = (f32[8,8,256]{2,1,0:T(8,128)S(1)}, f32[8,8,256]{2,1,0:T(8,128)}, u32[]{:S(2)}) copy-start(f32[8,8,256]{2,1,0:T(8,128)} %log_ref.5) | copy-start | bytes 196612
  2.5 5.6 %copy-start.3 = (f32[8,8,256]{2,1,0:T(8,128)S(1)}, f32[8,8,256]{2,1,0:T(8,128)}, u32[]{:S(2)}) copy-start(f32[8,8,256]{2,1,0:T(8,128)} %sto_ref.5) | copy-start | bytes 196612
  2.5 5.6 %copy-start.5 = (f32[8,8,256]{2,1,0:T(8,128)S(1)}, f32[8,8,256]{2,1,0:T(8,128)}, u32[]{:S(2)}) copy-start(f32[8,8,256]{2,1,0:T(8,128)} %rec_ref.5) | copy-start | bytes 196612
  2.6 5.5 %collective-permute-start = (f32[80,256]{1,0:T(8,128)S(1)}, f32[80,256]{1,0:T(8,128)S(1)}, u32[]{:S(2)}, u32[]{:S(2)}) collective-permute-start(f32[80,256]{1,0:T(8,128)S(1)} %get-tuple-element.20), channel_id=1, source_target_pairs={{0,1},{1,0},{2,3},{3,2},{16,17},{17,16},{18,19},{19,18},{4,5},{5,4... | collective-permute-start | bytes 245768 | tf_op jit(solution)/shard_map/ppermute | solution.py:47
  5.7 2.4 %collective-permute-start.1 = (f32[80,256]{1,0:T(8,128)S(1)}, f32[80,256]{1,0:T(8,128)S(1)}, u32[]{:S(2)}, u32[]{:S(2)}) collective-permute-start(f32[80,256]{1,0:T(8,128)S(1)} %get-tuple-element.21), channel_id=1, source_target_pairs={{0,16},{1,2},{2,1},{3,19},{16,0},{17,18},{18,17},{19,3},{4,20},{5,... | collective-permute-start | bytes 245768 | tf_op jit(solution)/shard_map/ppermute | solution.py:47
  5.7 0.7 %copy-start.10 = (s32[512]{0:T(512)S(1)}, s32[512]{0:T(512)}, u32[]{:S(2)}) copy-start(s32[512]{0:T(512)} %param.16) | copy-start | bytes 6148
  5.7 0.7 %copy-start.9 = (s32[512]{0:T(512)S(1)}, s32[512]{0:T(512)}, u32[]{:S(2)}) copy-start(s32[512]{0:T(512)} %param.17) | copy-start | bytes 6148
  5.7 0.7 %copy-start.7 = (s32[512]{0:T(512)S(1)}, s32[512]{0:T(512)}, u32[]{:S(2)}) copy-start(s32[512]{0:T(512)} %owner_ref.1) | copy-start | bytes 6148
  6.4 0.7 %copy-start.11 = (s32[4]{0:T(128)S(1)}, s32[4]{0:T(128)}, u32[]{:S(2)}) copy-start(s32[4]{0:T(128)} %param.13) | copy-start | bytes 52
  8.2 7.8 %collective-permute-start.2 = (f32[104,256]{1,0:T(8,128)S(1)}, f32[104,256]{1,0:T(8,128)S(1)}, u32[]{:S(2)}, u32[]{:S(2)}) collective-permute-start(f32[104,256]{1,0:T(8,128)S(1)} %get-tuple-element.22), channel_id=1, source_target_pairs={{0,4},{4,0},{8,12},{12,8},{16,20},{20,16},{24,28},{28,24},{1,5},{5... | collective-permute-start | bytes 319496 | tf_op jit(solution)/shard_map/ppermute | solution.py:47
  10.2 5.8 %collective-permute-start.3 = (f32[104,256]{1,0:T(8,128)S(1)}, f32[104,256]{1,0:T(8,128)S(1)}, u32[]{:S(2)}, u32[]{:S(2)}) collective-permute-start(f32[104,256]{1,0:T(8,128)S(1)} %get-tuple-element.23), channel_id=1, source_target_pairs={{0,16},{4,8},{8,4},{12,28},{16,0},{20,24},{24,20},{28,12},{1,17},{... | collective-permute-start | bytes 319496 | tf_op jit(solution)/shard_map/ppermute | solution.py:47
  10.2 0.7 %copy-start.6 = (f32[4,512]{1,0:T(4,128)S(1)}, f32[4,512]{1,0:T(4,128)}, u32[]{:S(2)}) copy-start(f32[4,512]{1,0:T(4,128)} %observed_ref.1) | copy-start | bytes 24580
  16.0 0.7 %copy-start.8 = (f32[4]{0:T(128)S(1)}, f32[4]{0:T(128)}, u32[]{:S(2)}) copy-start(f32[4]{0:T(128)} %rate_ref.1) | copy-start | bytes 52
  45.9 1.3 %collective-permute-start.4 = (f32[8,8,128]{2,1,0:T(8,128)S(1)}, f32[8,8,128]{2,1,0:T(8,128)S(1)}, u32[]{:S(2)}, u32[]{:S(2)}) collective-permute-start(f32[8,8,128]{2,1,0:T(8,128)S(1)} %get-tuple-element.34), channel_id=1, source_target_pairs={{0,16},{16,0},{1,17},{17,1},{2,18},{18,2},{3,19},{19,3},{4,20},{20... | collective-permute-start | bytes 98312 | tf_op jit(solution)/shard_map/ppermute | solution.py:509

commit v2 on v1

--- a/solution.py
+++ b/solution.py
@@ -11,6 +11,12 @@
 LANES = 128
 DEEP = 4
 EPSILON = 1e-06
+WELL_CHUNK = 512
+WELLS_AT_ONCE = 16
+
+
+def list_length(per_brick):
+    return -(-9 * per_brick // LANES) * LANES
 
 
 def row_plan(size):
@@ -47,7 +53,15 @@
     return lax.ppermute(send_even, ("test", axis), even), lax.ppermute(send_odd, ("test", axis), odd)
 
 
-def pack_y(log_ref, sto_ref, rec_ref, even_ref, odd_ref):
+def load_and_pack(*refs):
+    n_in = (len(refs) - 3) // 2
+    sources, loaded, (even_ref, odd_ref, sems) = refs[:n_in], refs[n_in : 2 * n_in], refs[2 * n_in :]
+    copies = [pltpu.make_async_copy(a, b, sems.at[i]) for i, (a, b) in enumerate(zip(sources, loaded))]
+    for copy in copies:
+        copy.start()
+    for copy in copies[:3]:
+        copy.wait()
+    log_ref, sto_ref, rec_ref = loaded[:3]
     size_x, size_y, _ = log_ref.shape
     is_even = lax.axis_index("by") % 2 == 0
     rows = 3 * DEEP - 2
@@ -60,6 +74,8 @@
             even_ref[at, :] = jnp.where(is_even, up, down)
             odd_ref[at, :] = jnp.where(is_even, down, up)
             start += reach
+    for copy in copies[3:]:
+        copy.wait()
 
 
 def pack_x(plan, log_ref, sto_ref, rec_ref, ey_ref, oy_ref, even_ref, odd_ref):
@@ -127,37 +143,62 @@
         to_ref[x, low:high] = source_ref[x, low:high] + gamma_ref[x, low:high] * total
         return carry
 
-    lax.fori_loop(low, high, one_row, 0)
-
-
-def wells_kernel(tests, per_brick, owner_ref, packed_ref, observed_ref, window_ref, own_ref, obs_ref, count_ref, index_ref):
-    bricks = count_ref.shape[0]
-    for brick in range(bricks):
-        count_ref[brick] = 0
-    n_wells = owner_ref.shape[0]
-
-    def one_well(well, found):
-        brick = owner_ref[well]
-        packed = packed_ref[well]
-        rank = count_ref[brick]
-        count_ref[brick] = rank + 1
-        window_ref[found] = packed + ((brick * per_brick + rank) << 16)
-        at = jnp.where((packed >> 29) & 1 == 1, rank, per_brick)
-        own_ref[at] = packed
-        index_ref[at] = well
-        return found + ((packed >> 30) & 1)
-
-    found = lax.fori_loop(0, n_wells, one_well, jnp.int32(0), unroll=8)
-    window_ref[n_wells] = found
+    lax.fori_loop(low, high, one_row, 0, unroll=True)
+
+
+def wells_kernel(tests, per_brick, owner_ref, xy_ref, top_ref, window_ref, owned_ref, observed_ref, pump_ref, table_ref, obs_ref, bricks):
+    n_wells = owner_ref.shape[1]
+    chunk = WELL_CHUNK if n_wells % WELL_CHUNK == 0 else n_wells
+    listed = list_length(per_brick)
+    before = lax.broadcasted_iota(jnp.int32, (chunk, chunk), 0) < lax.broadcasted_iota(jnp.int32, (chunk, chunk), 1)
+    before = jnp.where(before, 1.0, 0.0).astype(jnp.bfloat16)
+    brick_at = lax.broadcasted_iota(jnp.int32, (bricks, chunk), 0)
+    list_at = lax.broadcasted_iota(jnp.int32, (listed, chunk), 0).astype(jnp.float32)
+    own_at = (lax.broadcasted_iota(jnp.int32, (LANES, chunk), 0) % per_brick).astype(jnp.float32)
+    lane_at = lax.broadcasted_iota(jnp.int32, (1, chunk), 1)
+    first_row = lax.broadcasted_iota(jnp.int32, (16, chunk), 0) == 0
+    total = jnp.zeros((bricks + 16, 1), jnp.float32)
+    result = jnp.zeros((32, listed + LANES + 16), jnp.float32)
+    for start in range(0, n_wells, chunk):
+        part = slice(start, start + chunk)
+        owner = owner_ref[:, part]
+        near, mine = window_ref[:, part], owned_ref[:, part]
+        ones = jnp.where(brick_at == owner, 1.0, 0.0)
+        counted = jnp.concatenate([ones, jnp.where(first_row, near, 0.0)], axis=0)
+        prefix = jnp.dot(counted.astype(jnp.bfloat16), before, preferred_element_type=jnp.float32) + total
+        total = total + jnp.sum(counted, axis=1, keepdims=True)
+        rank = jnp.sum(ones * prefix[:bricks], axis=0, keepdims=True)
+        in_list = jnp.where((list_at == prefix[bricks : bricks + 1]) & (near > 0.5), 1.0, 0.0)
+        in_own = jnp.where((own_at == rank) & (mine > 0.5), 1.0, 0.0)
+        pumps = [jnp.where(lane_at + start == pump_ref[:, test : test + 1], 1.0, 0.0) for test in range(tests)]
+        pumps.append(jnp.zeros((16 - tests, chunk), jnp.float32))
+        chosen = jnp.concatenate([in_list, in_own] + pumps, axis=0).astype(jnp.bfloat16)
+        slot = owner * per_brick + rank.astype(jnp.int32)
+        numbers = [xy_ref[:, part], top_ref[:, part], slot & 255, slot >> 8]
+        rows = [number.astype(jnp.float32) for number in numbers] + [near]
+        for test in range(tests):
+            value = observed_ref[test : test + 1, part]
+            for _ in range(3):
+                piece = value.astype(jnp.bfloat16).astype(jnp.float32)
+                rows.append(piece)
+                value = value - piece
+        rows.append(jnp.zeros((32 - len(rows), chunk), jnp.float32))
+        carried = jnp.concatenate(rows, axis=0).astype(jnp.bfloat16)
+        result = result + lax.dot_general(carried, chosen, (((1,), (1,)), ((), ())), preferred_element_type=jnp.float32)
+    numbers = [result[row : row + 1].astype(jnp.int32) for row in range(5)]
+    words = numbers[1] + (numbers[0] << 8) + (numbers[2] << 16) + (numbers[3] << 24) + (numbers[4] << 30)
+    listed_rows = listed // LANES
+    for row in range(listed_rows + 1):
+        table_ref[row : row + 1, :] = words[:, row * LANES : (row + 1) * LANES]
+    table_ref[listed_rows + 1 : listed_rows + 2, : LANES // 8] = words[:, listed + LANES :]
+    found = jnp.broadcast_to(total[bricks : bricks + 1], (1, LANES)).astype(jnp.int32)
+    table_ref[listed_rows + 2 : listed_rows + 3, :] = found
     lane = lax.broadcasted_iota(jnp.int32, (1, LANES), 1)
-
-    def one_value(rank, values):
-        well = index_ref[rank]
-        for test in range(tests):
-            values = jnp.where(lane == test * per_brick + rank, observed_ref[test, well], values)
-        return values
-
-    obs_ref[...] = lax.fori_loop(0, per_brick, one_value, jnp.zeros((1, LANES), jnp.float32), unroll=8)
+    values = jnp.zeros((1, LANES), jnp.float32)
+    for test in range(tests):
+        pieces = [result[row : row + 1, listed : listed + LANES] for row in range(5 + 3 * test, 8 + 3 * test)]
+        values = jnp.where(lane // per_brick == test, pieces[0] + (pieces[1] + pieces[2]), values)
+    obs_ref[...] = values
 
 
 def heads_kernel(
@@ -171,9 +212,8 @@
     oy_ref,
     ex_ref,
     ox_ref,
-    own_ref,
+    table_ref,
     obs_ref,
-    pump_ref,
     rate_ref,
     gamma_ref,
     delta_ref,
@@ -240,7 +280,7 @@
         e_w[x] = jnp.exp(0.5 * log_w[x])
         return carry
 
-    lax.fori_loop(0, wide_x, one_exp, 0)
+    lax.fori_loop(0, wide_x, one_exp, 0, unroll=True)
 
     def one_row(x, carry):
         e = e_w[x]
@@ -255,7 +295,7 @@
         bet_w[x] = delta * rec_w[x]
         return carry
 
-    lax.fori_loop(1, wide_x - 1, one_row, 0)
+    lax.fori_loop(1, wide_x - 1, one_row, 0, unroll=True)
     sub, lane, half = tile_marks(tests)
 
     def spread(wide, x, y):
@@ -270,7 +310,7 @@
             bet_ref[x, y] = spread(bet_w, x, y)
         return carry
 
-    lax.fori_loop(1, wide_x - 1, spread_row, 0)
+    lax.fori_loop(1, wide_x - 1, spread_row, 0, unroll=True)
 
     def spread_near(x, carry):
         for y in range(DEEP - 1, DEEP + size_y + 1):
@@ -279,16 +319,17 @@
             inv_e_ref[x, y] = 1.0 / e
         return carry
 
-    lax.fori_loop(DEEP - 1, DEEP + size_x + 1, spread_near, 0)
+    lax.fori_loop(DEEP - 1, DEEP + size_x + 1, spread_near, 0, unroll=True)
     z_of = half * LANES + lane
+    listed_rows = list_length(per_brick) // LANES
     for test in range(tests):
-        packed = pump_ref[test]
+        packed = table_ref[listed_rows + 1, test]
 
         @pl.when((packed >> 30) & 1 == 1)
         def _(packed=packed, test=test):
             x, y, top = (packed >> 12) & 15, (packed >> 8) & 15, packed & 255
             hit = (z_of >= top) & (z_of < top + SCREEN) & (sub % tests == test)
-            bet_ref[x, y] = bet_ref[x, y] - jnp.where(hit, delta_ref[x, y] * rate_ref[test], 0.0)
+            bet_ref[x, y] = bet_ref[x, y] - jnp.where(hit, delta_ref[x, y] * rate_ref[:, test : test + 1], 0.0)
 
     sweep(bet_ref, gamma_ref, bet_ref, one_ref, 2, wide_y - 2, lane, half)
     sweep(bet_ref, gamma_ref, one_ref, two_ref, 3, wide_y - 3, lane, half)
@@ -297,11 +338,11 @@
         head_ref[x, 3 : wide_y - 3] = two_ref[x, 3 : wide_y - 3] * inv_e_ref[x, 3 : wide_y - 3]
         return carry
 
-    lax.fori_loop(3, wide_x - 3, one_head, 0)
+    lax.fori_loop(3, wide_x - 3, one_head, 0, unroll=True)
     slot_of = lane - per_brick * (sub % tests)
     gathered = jnp.zeros((8, LANES), jnp.float32)
     for rank in range(per_brick):
-        packed = own_ref[rank]
+        packed = table_ref[listed_rows, rank]
         x, y, top = (packed >> 12) & 15, (packed >> 8) & 15, packed & 255
         hit = (z_of >= top) & (z_of < top + SCREEN)
         mean = jnp.sum(jnp.where(hit, head_ref[x, y], 0.0), axis=1, keepdims=True)
@@ -315,8 +356,9 @@
     per_brick,
     split,
     scale,
+    n_wells,
     resid_ref,
-    window_ref,
+    table_ref,
     gamma_ref,
     delta_ref,
     e_ref,
@@ -327,7 +369,6 @@
     outs, (weight_ref, bet_ref, one_ref, two_ref, adj_ref) = rest[:-5], rest[-5:]
     wide_x, wide_y = gamma_ref.shape[:2]
     size_x, size_y = wide_x - 2 * DEEP, wide_y - 2 * DEEP
-    n_wells = window_ref.shape[0] - 1
     sub, lane, half = tile_marks(tests)
     z_of = half * LANES + lane
     resid = resid_ref[:, 0, :]
@@ -344,27 +385,35 @@
         bet_ref[x] = jnp.zeros(bet_ref.shape[1:], jnp.float32)
         return carry
 
-    lax.fori_loop(0, wide_x, clear, 0)
+    lax.fori_loop(0, wide_x, clear, 0, unroll=True)
     slot_of = lane - per_brick * (sub % tests)
 
-    def one_well(place, carry):
-        packed = window_ref[place]
-        x, y, top = (packed >> 12) & 15, (packed >> 8) & 15, packed & 255
-        slot = (packed >> 16) & 0x1FFF
-        brick, rank = slot // per_brick, slot % per_brick
-        row = jnp.broadcast_to(weight_ref[pl.ds(brick, 1), :], (8, LANES))
-        value = jnp.sum(jnp.where(slot_of == rank, row, 0.0), axis=1, keepdims=True)
-        hit = (z_of >= top) & (z_of < top + SCREEN)
-        bet_ref[x, y] = bet_ref[x, y] + jnp.where(hit, value, 0.0)
-        return carry
-
-    lax.fori_loop(0, window_ref[n_wells], one_well, 0)
+    listed_rows = list_length(per_brick) // LANES
+    pick = per_brick * (sub % tests)
+
+    def some_wells(turn, carry):
+        todo = []
+        for step in range(WELLS_AT_ONCE):
+            place = turn * WELLS_AT_ONCE + step
+            packed = table_ref[place // LANES, place % LANES]
+            x, y, top = (packed >> 12) & 15, (packed >> 8) & 15, packed & 255
+            slot = (packed >> 16) & 0x1FFF
+            row = jnp.broadcast_to(weight_ref[pl.ds(slot // per_brick, 1), :], (8, LANES))
+            value = jnp.take_along_axis(row, pick + slot % per_brick, axis=1, mode="promise_in_bounds")
+            hit = (z_of >= top) & (z_of < top + SCREEN)
+            todo.append((x, y, jnp.where(hit, value, 0.0)))
+        for x, y, value in todo:
+            bet_ref[x, y] = bet_ref[x, y] + value
+        return carry
+
+    turns = (table_ref[listed_rows + 2, 0] + WELLS_AT_ONCE - 1) // WELLS_AT_ONCE
+    lax.fori_loop(0, turns, some_wells, 0)
 
     def scaled(x, carry):
         bet_ref[x, 1 : wide_y - 1] = bet_ref[x, 1 : wide_y - 1] * delta_ref[x, 1 : wide_y - 1]
         return carry
 
-    lax.fori_loop(1, wide_x - 1, scaled, 0)
+    lax.fori_loop(1, wide_x - 1, scaled, 0, unroll=True)
     sweep(bet_ref, gamma_ref, bet_ref, one_ref, 2, wide_y - 2, lane, half)
     sweep(bet_ref, gamma_ref, one_ref, two_ref, 3, wide_y - 3, lane, half)
 
@@ -372,7 +421,7 @@
         adj_ref[x, 3 : wide_y - 3] = two_ref[x, 3 : wide_y - 3] * inv_e_ref[x, 3 : wide_y - 3]
         return carry
 
-    lax.fori_loop(3, wide_x - 3, one_adjoint, 0)
+    lax.fori_loop(3, wide_x - 3, one_adjoint, 0, unroll=True)
     own_y = slice(DEEP, DEEP + size_y)
 
     def one_row(x, carry):
@@ -405,7 +454,7 @@
                 outs[0][x - DEEP, pl.ds(y, 1), LANES:] = high
         return carry
 
-    lax.fori_loop(DEEP, DEEP + size_x, one_row, 0)
+    lax.fori_loop(DEEP, DEEP + size_x, one_row, 0, unroll=True)
 
 
 def vmem():
@@ -439,35 +488,44 @@
     rows_x = (3 * DEEP - 2) * size_y + corner_rows(plan)
     wide_x, wide_y = size_x + 2 * DEEP, size_y + 2 * DEEP
 
+    inputs = (
+        log_conductivity,
+        storage,
+        recharge,
+        owner.reshape(1, n_wells),
+        screen_column.reshape(1, n_wells),
+        screen_top.reshape(1, n_wells),
+        observed,
+        pump_rate.reshape(1, tests),
+        pump_well.reshape(1, tests),
+    )
+    log_k, sto, rec, owner, column, top, observed, rate, wells_pumped, even_y, odd_y = pl.pallas_call(
+        load_and_pack,
+        out_shape=[jax.ShapeDtypeStruct(a.shape, a.dtype) for a in inputs] + [f32(rows_y, size_z)] * 2,
+        in_specs=[pl.BlockSpec(memory_space=pltpu.HBM)] * len(inputs),
+        out_specs=[vmem()] * (len(inputs) + 2),
+        scratch_shapes=[pltpu.SemaphoreType.DMA((len(inputs),))],
+        compiler_params=PARAMS,
+        name="load_and_pack",
+    )(*[pltpu.with_memory_space_constraint(a, pltpu.HBM) for a in inputs])
+    got_even_y, got_odd_y = swap_sides(even_y, odd_y, "by", groups)
+
     bx, by = lax.axis_index("bx"), lax.axis_index("by")
-    well_x = (owner // n_by - bx) * size_x + screen_column // size_y + DEEP
-    well_y = (owner % n_by - by) * size_y + screen_column % size_y + DEEP
+    well_x = (owner // n_by - bx) * size_x + column // size_y + DEEP
+    well_y = (owner % n_by - by) * size_y + column % size_y + DEEP
     out_x = jnp.maximum(jnp.maximum(DEEP - well_x, well_x - (DEEP + size_x - 1)), 0)
     out_y = jnp.maximum(jnp.maximum(DEEP - well_y, well_y - (DEEP + size_y - 1)), 0)
-    in_window = (out_x + out_y < DEEP).astype(jnp.int32)
-    owned = ((out_x == 0) & (out_y == 0)).astype(jnp.int32)
-    packed = (in_window << 30) + (owned << 29) + ((well_x & 15) << 12) + ((well_y & 15) << 8) + screen_top
-    pump_packed = packed[pump_well]
-
-    even_y, odd_y = pl.pallas_call(
-        pack_y,
-        out_shape=[f32(rows_y, size_z)] * 2,
-        in_specs=[vmem()] * 3,
+    in_window = (out_x + out_y < DEEP).astype(jnp.float32)
+    owned = ((out_x == 0) & (out_y == 0)).astype(jnp.float32)
+    xy = ((well_x & 15) << 4) + (well_y & 15)
+    table, obs = pl.pallas_call(
+        functools.partial(wells_kernel, tests, per_brick, bricks=bricks),
+        out_shape=[i32(8, LANES), f32(1, LANES)],
+        in_specs=[vmem()] * 7,
         out_specs=[vmem()] * 2,
         compiler_params=PARAMS,
-        name="pack_y",
-    )(log_conductivity, storage, recharge)
-    got_even_y, got_odd_y = swap_sides(even_y, odd_y, "by", groups)
-
-    window, own, obs = pl.pallas_call(
-        functools.partial(wells_kernel, tests, per_brick),
-        out_shape=[i32(n_wells + 1), i32(per_brick + 1), f32(1, LANES)],
-        in_specs=[smem()] * 3,
-        out_specs=[smem(), smem(), vmem()],
-        scratch_shapes=[pltpu.SMEM((bricks,), jnp.int32), pltpu.SMEM((per_brick + 1,), jnp.int32)],
-        compiler_params=PARAMS,
         name="wells",
-    )(owner, packed, observed)
+    )(owner, xy, top, in_window, owned, observed, wells_pumped)
 
     even_x, odd_x = pl.pallas_call(
         functools.partial(pack_x, plan),
@@ -476,7 +534,7 @@
         out_specs=[vmem()] * 2,
         compiler_params=PARAMS,
         name="pack_x",
-    )(log_conductivity, storage, recharge, got_even_y, got_odd_y)
+    )(log_k, sto, rec, got_even_y, got_odd_y)
     got_even_x, got_odd_x = swap_sides(even_x, odd_x, "bx", groups)
 
     tiles = (wide_x, wide_y, 8, LANES)
@@ -484,12 +542,12 @@
     gamma, delta, e, inv_e, head, row = pl.pallas_call(
         functools.partial(heads_kernel, plan, tests, per_brick),
         out_shape=[f32(*tiles)] * 5 + [f32(bricks, 1, LANES)],
-        in_specs=[vmem()] * 7 + [smem(), vmem(), smem(), smem()],
+        in_specs=[vmem()] * 7 + [smem(), vmem(), vmem()],
         out_specs=[vmem()] * 6,
         scratch_shapes=[pltpu.VMEM(wide, jnp.float32)] * 7 + [pltpu.VMEM(tiles, jnp.float32)] * 3,
         compiler_params=PARAMS,
         name="heads",
-    )(log_conductivity, storage, recharge, got_even_y, got_odd_y, got_even_x, got_odd_x, own, obs, pump_packed, pump_rate)
+    )(log_k, sto, rec, got_even_y, got_odd_y, got_even_x, got_odd_x, table, obs, rate)
 
     residuals = lax.all_to_all(row, ("bx", "by"), 0, 0)
 
@@ -497,14 +555,14 @@
     split = groups == 2
     out_shape = [f32(size_x, size_y, LANES)] * 2 if split else [f32(size_x, size_y, size_z)]
     partial = pl.pallas_call(
-        functools.partial(adjoint_kernel, tests, per_brick, split, -0.5 / all_tests),
+        functools.partial(adjoint_kernel, tests, per_brick, split, -0.5 / all_tests, n_wells),
         out_shape=out_shape,
         in_specs=[vmem(), smem()] + [vmem()] * 5,
         out_specs=[vmem()] * len(out_shape),
         scratch_shapes=[pltpu.VMEM((bricks, LANES), jnp.float32)] + [pltpu.VMEM(tiles, jnp.float32)] * 4,
         compiler_params=PARAMS,
         name="adjoint",
-    )(residuals, window, gamma, delta, e, inv_e, head)
+    )(residuals, table, gamma, delta, e, inv_e, head)
     if split:
         return partial[0] + lax.ppermute(partial[1], "test", [(0, 1), (1, 0)])
     return lax.psum_scatter(partial[0], "test", scatter_dimension=2, tiled=True)

time: 48.4 us -> 35.1 us (0.73)
  Pallas kernels: 19.4 us -> 6.81 us
  local copies, waits for them, and re-layouts: 5.21 us -> 0 us
  waiting for transfers between devices: 2.27 us -> 6.69 us
  blocking collectives: 15 us -> 15.5 us
    pallas_call x1, Pallas kernels: 9.11 us -> 2.98 us  [local(): pl.pallas_call(functools.partial(adjoint_kernel, tests, per_brick, split,...]
    unnamed x24 -> x0, local copies, waits for them, and re-layouts: 4.56 us -> none
    ppermute x2, waiting for transfers between devices: 1.07 us -> 5.49 us  [swap_sides(): lax.ppermute(send_even, ('test', axis), even)]
    pallas_call x2, Pallas kernels: 5.14 us -> 1.54 us  [the longest x1 1.05 us: local(): pl.pallas_call(load_and_pack, out_shape=[jax.ShapeDtypeStruct(a.shape, a....]
    pallas_call x1, Pallas kernels: 5.11 us -> 2.23 us  [local(): pl.pallas_call(functools.partial(heads_kernel, plan, tests, per_brick), o...]
    gather x1 -> x0, local copies, waits for them, and re-layouts: 0.64 us -> none  [local(): pump_packed = packed[pump_well]]
    all_to_all x1, blocking collectives: 15 us -> 15.5 us  [local(): residuals = lax.all_to_all(row, ('bx', 'by'), 0, 0)]
  transfers between devices with their start and end apart: 5 -> 5, of which waited for: 2 -> 3; matrix products, arithmetic and copies ran while one was open for 1% -> 0% of each run, Pallas kernels for 11% -> 1%
where the time goes in v2:
time: 35.1 us; the launch traced here: 34.9 us
  blocking collectives  15.5 us (44%)
  Pallas kernels  6.81 us (19%)
  waiting for transfers between devices  6.69 us (19%)
  starting transfers between devices  5.14 us (15%)
  other arithmetic  0.69 us (2%)
    all_to_all x1, blocking collectives, local(): residuals = lax.all_to_all(row, ('bx', 'by'), 0, 0)  15.5 us
    ppermute x2, waiting for transfers between devices, swap_sides(): lax.ppermute(send_even, ('test', axis), even)  5.49 us
    ppermute x2, starting transfers between devices, swap_sides(): lax.ppermute(send_even, ('test', axis), even)  5.07 us
    pallas_call x1, Pallas kernels, local(): pl.pallas_call(functools.partial(adjoint_kernel, tests, per_brick, split,...  2.98 us
    pallas_call x1, Pallas kernels, local(): pl.pallas_call(functools.partial(heads_kernel, plan, tests, per_brick), o...  2.23 us
    ppermute x1, waiting for transfers between devices, local(): return partial[0] + lax.ppermute(partial[1], 'test', [(0, 1), (1, 0)])  1.19 us
    pallas_call x1, Pallas kernels, local(): pl.pallas_call(load_and_pack, out_shape=[jax.ShapeDtypeStruct(a.shape, a....  1.05 us
  transfers between devices with their start and end apart: 5, of which 3 were waited for; matrix products, arithmetic and copies ran while one was open for 0% of the time, Pallas kernels for 1%

profile of v2, /device:TPU:0, one launch (start us, length us, event | category | flops | bytes accessed | tf_op | source)
XLA Modules:
  0.0 34.9 jit_solution(11431987893588209177)
XLA Ops:
  0.0 1.0 %load_and_pack.1 = (f32[8,8,256]{2,1,0:T(8,128)S(1)}, f32[8,8,256]{2,1,0:T(8,128)S(1)}, f32[8,8,256]{2,1,0:T(8,128)S(1)}, s32[1,512]{1,0:T(1,128)S(1)}, s32[1,51...) custom-call(f32[8,8,256]{2,1,0:T(8,128)} %refs_0_.1, ...), custom_call_target="tpu_custom_call" | custom-call | tf_op jit(solution)/shard_map/load_and_pack/pallas_call | solution.py:502
  1.1 3.1 %collective-permute-start = (f32[80,256]{1,0:T(8,128)S(1)}, f32[80,256]{1,0:T(8,128)S(1)}, u32[]{:S(2)}, u32[]{:S(2)}) collective-permute-start(f32[80,256]{1,0:T(8,128)S(1)} %get-tuple-element.31), channel_id=1, source_target_pairs={{0,1},{1,0},{2,3},{3,2},{16,17},{17,16},{18,19},{19,18},{4,5},{5,4... | collective-permute-start | bytes 245768 | tf_op jit(solution)/shard_map/ppermute | solution.py:53
  4.1 0.0 collective-permute-start.1
  4.2 2.4 %collective-permute-done.ey_ref = f32[80,256]{1,0:T(8,128)S(1)} collective-permute-done((f32[80,256]{1,0:T(8,128)S(1)}, f32[80,256]{1,0:T(8,128)S(1)}, u32[]{:S(2)}, u32[]{:S(2)}) %collective-permute-start) | collective-permute-done | bytes 81952 | tf_op jit(solution)/shard_map/ppermute | solution.py:53
  6.6 0.0 collective-permute-done.1.oy_ref
  6.6 0.1 pack_x.1
  6.7 2.0 %collective-permute-start.2 = (f32[104,256]{1,0:T(8,128)S(1)}, f32[104,256]{1,0:T(8,128)S(1)}, u32[]{:S(2)}, u32[]{:S(2)}) collective-permute-start(f32[104,256]{1,0:T(8,128)S(1)} %get-tuple-element.33), channel_id=1, source_target_pairs={{0,4},{4,0},{8,12},{12,8},{16,20},{20,16},{24,28},{28,24},{1,5},{5... | collective-permute-start | bytes 319496 | tf_op jit(solution)/shard_map/ppermute | solution.py:53
  8.6 0.0 collective-permute-start.3
  8.6 0.5 %wells.1 = (s32[8,128]{1,0:T(8,128)S(1)}, f32[1,128]{1,0:T(1,128)S(1)}) custom-call(s32[1,512]{1,0:T(1,128)S(1)} %get-tuple-element.35.owner_ref, s32[1,512]{1,0:T(1,128)S(1)} %and_add_fusion.xy_ref, s32[1,512]{1,0:T(1,128)S(1)} %get-tuple-element.37.top_ref, f32[1,512]{1,0:T(1,128)S(1)} %compare_convert_fusion.window_ref, ...), custom_call_target="tpu_custom_call" | custom-call | tf_op jit(solution)/shard_map/wells/pallas_call | solution.py:521
  9.1 3.1 %collective-permute-done.2.ex_ref = f32[104,256]{1,0:T(8,128)S(1)} collective-permute-done((f32[104,256]{1,0:T(8,128)S(1)}, f32[104,256]{1,0:T(8,128)S(1)}, u32[]{:S(2)}, u32[]{:S(2)}) %collective-permute-start.2) | collective-permute-done | bytes 106528 | tf_op jit(solution)/shard_map/ppermute | solution.py:53
  12.3 0.0 collective-permute-done.3.ox_ref
  12.3 2.2 %heads.1 = (f32[16,16,8,128]{3,2,1,0:T(8,128)S(1)}, f32[16,16,8,128]{3,2,1,0:T(8,128)S(1)}, f32[16,16,8,128]{3,2,1,0:T(8,128)S(1)}, f32[16,16,8,128]{3,2,1,0:T(8...) custom-call(f32[8,8,256]{2,1,0:T(8,128)S(1)} %get-tuple-element.28.log_ref, ...), custom_call_target="tpu_custom_call" | custom-call | tf_op jit(solution)/shard_map/heads/pallas_call | solution.py:542
  14.5 15.5 %all_to_all.5.resid_ref = f32[16,1,128]{2,1,0:T(1,128)S(1)} all-to-all(f32[16,1,128]{2,1,0:T(1,128)S(1)} %get-tuple-element.43), channel_id=1, replica_groups=mesh['test'=2,'bx'=4,'by'=4] {'bx','by'}, dimensions={0} | all-to-all | bytes 16384 | tf_op jit(solution)/shard_map/all_to_all | solution.py:552
  30.0 3.0 %adjoint.1 = (f32[8,8,128]{2,1,0:T(8,128)S(1)}, f32[8,8,128]{2,1,0:T(8,128)S(1)}) custom-call(f32[16,1,128]{2,1,0:T(1,128)S(1)} %all_to_all.5.resid_ref, s32[8,128]{1,0:T(8,128)S(1)} %get-tuple-element.40.table_ref, f32[16,16,8,128]{3,2,1,0:T(8,128)S(1)} %get-tuple-element.44.gamma_ref, f32[16,16,8,128]{3,2,1,0:T(8,128)S(1)} %get-tuple-element.45.delta_ref, ...), custom_call_target="tpu_custom_call" | custom-call | tf_op jit(solution)/shard_map/adjoint/pallas_call | solution.py:557
  33.0 0.1 collective-permute-start.4
  33.1 1.2 %collective-permute-done.4 = f32[8,8,128]{2,1,0:T(8,128)S(1)} collective-permute-done((f32[8,8,128]{2,1,0:T(8,128)S(1)}, f32[8,8,128]{2,1,0:T(8,128)S(1)}, u32[]{:S(2)}, u32[]{:S(2)}) %collective-permute-start.4) | collective-permute-done | bytes 32800 | tf_op jit(solution)/shard_map/ppermute | solution.py:567
  34.3 0.6 %add.47 = f32[8,8,128]{2,1,0:T(8,128)} add(f32[8,8,128]{2,1,0:T(8,128)S(1)} %get-tuple-element.49, f32[8,8,128]{2,1,0:T(8,128)S(1)} %collective-permute-done.4) | non-fusion elementwise | flops 8192 | bytes 98304 | tf_op jit(solution)/shard_map/add | solution.py:567
  (3 shorter events, 0.1 us)
Async XLA Ops:
  1.1 5.5 %collective-permute-start = (f32[80,256]{1,0:T(8,128)S(1)}, f32[80,256]{1,0:T(8,128)S(1)}, u32[]{:S(2)}, u32[]{:S(2)}) collective-permute-start(f32[80,256]{1,0:T(8,128)S(1)} %get-tuple-element.31), channel_id=1, source_target_pairs={{0,1},{1,0},{2,3},{3,2},{16,17},{17,16},{18,19},{19,18},{4,5},{5,4... | collective-permute-start | bytes 245768 | tf_op jit(solution)/shard_map/ppermute | solution.py:53
  4.1 2.4 %collective-permute-start.1 = (f32[80,256]{1,0:T(8,128)S(1)}, f32[80,256]{1,0:T(8,128)S(1)}, u32[]{:S(2)}, u32[]{:S(2)}) collective-permute-start(f32[80,256]{1,0:T(8,128)S(1)} %get-tuple-element.32), channel_id=1, source_target_pairs={{0,16},{1,2},{2,1},{3,19},{16,0},{17,18},{18,17},{19,3},{4,20},{5,... | collective-permute-start | bytes 245768 | tf_op jit(solution)/shard_map/ppermute | solution.py:53
  6.7 5.6 %collective-permute-start.2 = (f32[104,256]{1,0:T(8,128)S(1)}, f32[104,256]{1,0:T(8,128)S(1)}, u32[]{:S(2)}, u32[]{:S(2)}) collective-permute-start(f32[104,256]{1,0:T(8,128)S(1)} %get-tuple-element.33), channel_id=1, source_target_pairs={{0,4},{4,0},{8,12},{12,8},{16,20},{20,16},{24,28},{28,24},{1,5},{5... | collective-permute-start | bytes 319496 | tf_op jit(solution)/shard_map/ppermute | solution.py:53
  8.6 3.6 %collective-permute-start.3 = (f32[104,256]{1,0:T(8,128)S(1)}, f32[104,256]{1,0:T(8,128)S(1)}, u32[]{:S(2)}, u32[]{:S(2)}) collective-permute-start(f32[104,256]{1,0:T(8,128)S(1)} %get-tuple-element.34), channel_id=1, source_target_pairs={{0,16},{4,8},{8,4},{12,28},{16,0},{20,24},{24,20},{28,12},{1,17},{... | collective-permute-start | bytes 319496 | tf_op jit(solution)/shard_map/ppermute | solution.py:53
  33.0 1.3 %collective-permute-start.4 = (f32[8,8,128]{2,1,0:T(8,128)S(1)}, f32[8,8,128]{2,1,0:T(8,128)S(1)}, u32[]{:S(2)}, u32[]{:S(2)}) collective-permute-start(f32[8,8,128]{2,1,0:T(8,128)S(1)} %get-tuple-element.50), channel_id=1, source_target_pairs={{0,16},{16,0},{1,17},{17,1},{2,18},{18,2},{3,19},{19,3},{4,20},{20... | collective-permute-start | bytes 98312 | tf_op jit(solution)/shard_map/ppermute | solution.py:567

commit v3 on v0

v3 whole, which is shorter than its diff:
```python
import functools

import jax
import jax.numpy as jnp
from jax import lax
from jax.experimental import pallas as pl
from jax.experimental.pallas import tpu as pltpu
from jax.sharding import PartitionSpec as P

SCREEN = 8
LANES = 128
DEEP = 4
EPSILON = 1e-06
WELL_CHUNK = 512
WELLS_AT_ONCE = 16


def list_length(per_brick):
    return -(-6 * per_brick // LANES) * LANES


def slab_plan(half_x):
    plan = []
    for field, reach in ((0, DEEP), (1, DEEP - 1), (2, DEEP - 1)):
        for x in range(half_x + 2 * DEEP):
            rows = reach - max(DEEP - x, x - (DEEP + half_x - 1), 0)
            if rows > 0:
                plan.append((field, x, rows))
    return plan


def pair_of(test, tests):
    return test ^ 1 if (test ^ 1) < tests else test


def side_partners(count, tests):
    even, odd = [], []
    for test in range(tests):
        for place in range(count):
            me = test * count + place
            other = pair_of(test, tests) * count + place
            up = place ^ 1
            even.append((me, test * count + up if up < count else other))
            down = ((place + 1) ^ 1) - 1
            odd.append((me, test * count + down if 0 <= down < count else other))
    return even, odd


def circle(count, tests):
    pairs = []
    for test in range(tests):
        for place in range(count):
            to = place + 1 if test % 2 == 0 else place - 1
            me = test * count + place
            pairs.append((me, test * count + to if 0 <= to < count else pair_of(test, tests) * count + place))
    return pairs


def second_half():
    return lax.axis_index("test") % 2 == 1


def edge_kernel(log_ref, sto_ref, rec_ref, slab_ref, sems):
    size_x = log_ref.shape[0]
    copies, place = [], 0
    for field, (ref, reach) in enumerate(((log_ref, DEEP), (sto_ref, DEEP - 1), (rec_ref, DEEP - 1))):
        first = jnp.where(second_half(), 0, size_x - reach)
        copies.append(pltpu.make_async_copy(ref.at[pl.ds(first, reach)], slab_ref.at[pl.ds(place, reach)], sems.at[field]))
        place += reach
    for copy in copies:
        copy.start()
    for copy in copies:
        copy.wait()


def load_kernel(observed, rate, pumped, *refs):
    sources, loaded, facts_ref, (rate_ref, pumped_ref, sems) = refs[:6], refs[7:13], refs[13], refs[14:]
    tests = observed.shape[0]
    moves = [(observed, facts_ref.at[pl.ds(0, tests)]), (rate, rate_ref), (pumped, pumped_ref)] + list(zip(sources, loaded))
    copies = [pltpu.make_async_copy(a, b, sems.at[i]) for i, (a, b) in enumerate(moves)]
    for copy in copies:
        copy.start()
    for copy in copies:
        copy.wait()
    facts_ref[tests : tests + 1, 0:tests] = rate_ref[...]
    facts_ref[tests + 1 : tests + 2, 0:tests] = pumped_ref[...].astype(jnp.float32)


def wells_kernel(tests, per_brick, bricks, owner_ref, place_ref, top_ref, window_ref, owned_ref, facts_ref, other_ref, _, table_ref, obs_ref, clear_ref, clear_more_ref):
    n_wells = owner_ref.shape[1]
    chunk = WELL_CHUNK if n_wells % WELL_CHUNK == 0 else n_wells
    listed = list_length(per_brick)
    before = lax.broadcasted_iota(jnp.int32, (chunk, chunk), 0) < lax.broadcasted_iota(jnp.int32, (chunk, chunk), 1)
    before = jnp.where(before, 1.0, 0.0).astype(jnp.bfloat16)
    brick_at = lax.broadcasted_iota(jnp.int32, (bricks, chunk), 0)
    list_at = lax.broadcasted_iota(jnp.int32, (listed, chunk), 0).astype(jnp.float32)
    own_at = (lax.broadcasted_iota(jnp.int32, (LANES, chunk), 0) % per_brick).astype(jnp.float32)
    lane_at = lax.broadcasted_iota(jnp.int32, (1, chunk), 1).astype(jnp.float32)
    first_row = lax.broadcasted_iota(jnp.int32, (16, chunk), 0) == 0
    swapped = second_half()
    mine, theirs = facts_ref[...], other_ref[...]
    facts = (jnp.where(swapped, theirs, mine), jnp.where(swapped, mine, theirs))
    total = jnp.zeros((bricks + 16, 1), jnp.float32)
    result = jnp.zeros((32, listed + LANES + 16), jnp.float32)
    for start in range(0, n_wells, chunk):
        part = slice(start, start + chunk)
        owner = owner_ref[:, part]
        near, own = window_ref[:, part], owned_ref[:, part]
        ones = jnp.where(brick_at == owner, 1.0, 0.0)
        counted = jnp.concatenate([ones, jnp.where(first_row, near, 0.0)], axis=0)
        prefix = jnp.dot(counted.astype(jnp.bfloat16), before, preferred_element_type=jnp.float32) + total
        total = total + jnp.sum(counted, axis=1, keepdims=True)
        rank = jnp.sum(ones * prefix[:bricks], axis=0, keepdims=True)
        in_list = jnp.where((list_at == prefix[bricks : bricks + 1]) & (near > 0.5), 1.0, 0.0)
        in_own = jnp.where((own_at == rank) & (own > 0.5), 1.0, 0.0)
        pumps = []
        for test in range(2 * tests):
            pumped = facts[test // tests][tests + 1 : tests + 2, test % tests : test % tests + 1]
            pumps.append(jnp.where(lane_at + float(start) == pumped, 1.0, 0.0))
        pumps.append(jnp.zeros((16 - 2 * tests, chunk), jnp.float32))
        chosen = jnp.concatenate([in_list, in_own] + pumps, axis=0).astype(jnp.bfloat16)
        rows = [number.astype(jnp.float32) for number in (place_ref[:, part], top_ref[:, part], owner)] + [rank, near]
        for test in range(2 * tests):
            value = facts[test // tests][test % tests : test % tests + 1, part]
            for _ in range(3):
                piece = value.astype(jnp.bfloat16).astype(jnp.float32)
                rows.append(piece)
                value = value - piece
        rows.append(jnp.zeros((32 - len(rows), chunk), jnp.float32))
        carried = jnp.concatenate(rows, axis=0).astype(jnp.bfloat16)
        result = result + lax.dot_general(carried, chosen, (((1,), (1,)), ((), ())), preferred_element_type=jnp.float32)
    numbers = [result[row : row + 1].astype(jnp.int32) for row in range(5)]
    words = numbers[0] + (numbers[1] << 8) + (numbers[2] << 16) + (numbers[3] << 24) + (numbers[4] << 30)
    listed_rows = listed // LANES
    for row in range(listed_rows + 1):
        table_ref[row : row + 1, :] = words[:, row * LANES : (row + 1) * LANES]
    table_ref[listed_rows + 1 : listed_rows + 2, :16] = words[:, listed + LANES :]
    found = jnp.broadcast_to(total[bricks : bricks + 1], (1, LANES)).astype(jnp.int32)
    table_ref[listed_rows + 2 : listed_rows + 3, :] = found
    lane = lax.broadcasted_iota(jnp.int32, (1, LANES), 1)
    for part in range(2):
        values = jnp.zeros((1, LANES), jnp.float32)
        for test in range(tests):
            first = 5 + 3 * (part * tests + test)
            pieces = [result[row : row + 1, listed : listed + LANES] for row in range(first, first + 3)]
            values = jnp.where(lane // per_brick == test, pieces[0] + (pieces[1] + pieces[2]), values)
        obs_ref[part : part + 1, :] = values
        obs_ref[3 + part : 4 + part, 0:tests] = facts[part][tests : tests + 1, 0:tests]
    obs_ref[2:3, :] = result[4:5, listed : listed + LANES]
    clear_ref[...] = jnp.zeros(clear_ref.shape, jnp.float32)
    clear_more_ref[...] = jnp.zeros(clear_ref.shape, jnp.float32)


def at_window_rows(value):
    return pltpu.roll(jnp.concatenate([value, value], axis=0), DEEP, 0)


def window_kernel(log_ref, sto_ref, rec_ref, e_ref, sto_w, rec_w):
    base = jnp.where(second_half(), 0, DEEP)
    for x in range(log_ref.shape[0]):
        e_ref[base + x] = at_window_rows(jnp.exp(0.5 * log_ref[x]))
        sto_w[base + x] = at_window_rows(sto_ref[x])
        rec_w[base + x] = at_window_rows(rec_ref[x])


def pack_y(plan, slab_ref, e_in, sto_in, rec_in, e_ref, sto_w, rec_w, even_ref, odd_ref):
    size_y = slab_ref.shape[1]
    swapped = second_half()
    bx = lax.axis_index("bx")
    absent = jnp.where(swapped, bx == lax.axis_size("bx") - 1, bx == 0)
    y_even = lax.axis_index("by") % 2 == 0
    wides = (e_ref, sto_w, rec_w)
    half_x = e_ref.shape[0] - 2 * DEEP
    place = 0
    for field, reach in enumerate((DEEP, DEEP - 1, DEEP - 1)):
        base = jnp.where(swapped, DEEP + half_x, DEEP - reach)
        for i in range(reach):
            value = slab_ref[place + i]
            value = jnp.exp(0.5 * value) if field == 0 else value
            wides[field][base + i] = at_window_rows(jnp.where(absent, (1.0, 1.0, 0.0)[field], value))
        place += reach
    place = 0
    for field, x, count in plan:
        wide = wides[field]
        up = wide[x, DEEP + size_y - count : DEEP + size_y, :]
        down = wide[x, DEEP : DEEP + count, :]
        at = pl.ds(place, count)
        even_ref[at, :] = jnp.where(y_even, up, down)
        odd_ref[at, :] = jnp.where(y_even, down, up)
        place += count


def field_rows(e_ref, sto_w, rec_w, delta_ref, gamma_ref, beta_ref):
    wide_x, wide_y, size_z = e_ref.shape
    half_x, size_y = wide_x - 2 * DEEP, wide_y - 2 * DEEP
    bx, by, swapped = lax.axis_index("bx"), lax.axis_index("by"), second_half()
    row_at = lax.broadcasted_iota(jnp.int32, (wide_y, size_z), 0)
    z_at = lax.broadcasted_iota(jnp.int32, (wide_y, size_z), 1)
    inside_y = ((row_at >= DEEP) | (by > 0)) & ((row_at < DEEP + size_y) | (by < lax.axis_size("by") - 1))
    for x in range(1, wide_x - 1):
        e = e_ref[x]
        total = e_ref[x - 1] + e_ref[x + 1]
        total = total + pltpu.roll(e, 1, 0) + pltpu.roll(e, wide_y - 1, 0)
        total = total + jnp.where(z_at == 0, 1.0, pltpu.roll(e, 1, 1))
        total = total + jnp.where(z_at == size_z - 1, 1.0, pltpu.roll(e, size_z - 1, 1))
        inside = inside_y
        if x < DEEP:
            inside = inside & (swapped | (bx > 0))
        if x >= DEEP + half_x:
            inside = inside & (jnp.logical_not(swapped) | (bx < lax.axis_size("bx") - 1))
        delta = jnp.where(inside, e / (sto_w[x] + e * total), 0.0)
        delta_ref[x] = delta
        gamma_ref[x] = delta * e
        beta_ref[x] = delta * rec_w[x]


def spread(ref, x, low, high):
    tiles = []
    for y in range(low, high):
        halves = [ref[x, pl.ds(y, 1), part * LANES : (part + 1) * LANES] for part in range(2)]
        tiles.append(jnp.stack([jnp.broadcast_to(half, (8, LANES)) for half in halves]))
    return jnp.stack(tiles)


def lanes():
    return lax.broadcasted_iota(jnp.int32, (8, LANES), 1)


def z_down(values, edge):
    turned = pltpu.roll(values, 1, 3)
    first = lanes() == 0
    return jnp.stack([jnp.where(first, edge, turned[:, 0]), jnp.where(first, turned[:, 0], turned[:, 1])], axis=1)


def z_up(values, edge):
    turned = pltpu.roll(values, LANES - 1, 3)
    last = lanes() == LANES - 1
    return jnp.stack([jnp.where(last, turned[:, 1], turned[:, 0]), jnp.where(last, edge, turned[:, 1])], axis=1)


def columns(ref, wide_y, x, low, high):
    return ref[x * wide_y + low : x * wide_y + high]


def sweep(source_ref, gamma_ref, from_ref, x, low, high):
    wide_y = gamma_ref.shape[1]
    centre = columns(from_ref, wide_y, x, low, high)
    total = columns(from_ref, wide_y, x - 1, low, high) + columns(from_ref, wide_y, x + 1, low, high)
    total = total + columns(from_ref, wide_y, x, low - 1, high - 1) + columns(from_ref, wide_y, x, low + 1, high + 1)
    total = total + z_down(centre, 0.0) + z_up(centre, 0.0)
    return columns(source_ref, wide_y, x, low, high) + spread(gamma_ref, x, low, high) * total


def reached(wide_x, wide_y, reach):
    cells = []
    for x in range(DEEP - reach, wide_x - DEEP + reach):
        left = reach - max(DEEP - x, x - (wide_x - DEEP - 1), 0)
        cells.append((x, DEEP - left, wide_y - DEEP + left))
    return cells


def solve(bet_ref, gamma_ref, inv_ref, one_ref, two_ref):
    wide_x, wide_y, _ = gamma_ref.shape
    for x, low, high in reached(wide_x, wide_y, DEEP - 2):
        one_ref[x * wide_y + low : x * wide_y + high] = sweep(bet_ref, gamma_ref, bet_ref, x, low, high)
    for x, low, high in reached(wide_x, wide_y, DEEP - 3):
        scaled = sweep(bet_ref, gamma_ref, one_ref, x, low, high)
        two_ref[x * wide_y + low : x * wide_y + high] = scaled * spread(inv_ref, x, low, high)


def z_of_tile():
    return jnp.stack([lanes(), lanes() + LANES])


def unpack(packed):
    return packed & 255, (packed >> 8) & 255


def heads_kernel(plan, tests, per_brick, even_ref, odd_ref, e_in, sto_in, rec_in, table_in, obs_ref,
                 e_ref, delta_ref, gamma_ref, inv_ref, head_ref, row_ref, sto_w, rec_w, beta_ref, bet_ref, one_ref, table_ref, sem):
    wide_x, wide_y, _ = e_ref.shape
    table_copy = pltpu.make_async_copy(table_in, table_ref, sem)
    table_copy.start()
    by = lax.axis_index("by")
    y_even = by % 2 == 0
    no_low, no_high = by == 0, by == lax.axis_size("by") - 1
    place = 0
    for field, x, count in plan:
        wide = (e_ref, sto_w, rec_w)[field]
        fill = (1.0, 1.0, 0.0)[field]
        got_e, got_o = even_ref[pl.ds(place, count), :], odd_ref[pl.ds(place, count), :]
        low, high = jnp.where(y_even, got_o, got_e), jnp.where(y_even, got_e, got_o)
        wide[x, DEEP - count : DEEP, :] = jnp.where(no_low, fill, low)
        wide[x, wide_y - DEEP : wide_y - DEEP + count, :] = jnp.where(no_high, fill, high)
        place += count
    field_rows(e_ref, sto_w, rec_w, delta_ref, gamma_ref, beta_ref)
    for x in range(3, wide_x - 3):
        inv_ref[x] = 1.0 / e_ref[x]
    for x, low, high in reached(wide_x, wide_y, DEEP - 1):
        bet_ref[x * wide_y + low : x * wide_y + high] = spread(beta_ref, x, low, high)
    sub = lax.broadcasted_iota(jnp.int32, (8, LANES), 0)
    z_of = z_of_tile()
    listed_rows = list_length(per_brick) // LANES
    table_copy.wait()
    pumped = []
    for test in range(2 * tests):
        packed = table_ref[listed_rows + 1, test]
        place, top = unpack(packed)
        near = (packed >> 30) & 1 == 1
        rate = obs_ref[3 + test // tests : 4 + test // tests, test % tests : test % tests + 1]
        delta = delta_ref[place // wide_y, pl.ds(place % wide_y, 1), :]
        delta = jnp.stack([jnp.broadcast_to(delta[:, part * LANES : (part + 1) * LANES], (8, LANES)) for part in range(2)])
        hit = (z_of >= top) & (z_of < top + SCREEN) & (sub == test) & near
        pumped.append((place, jnp.where(hit, delta * rate, 0.0)))
    for place, taken in pumped:
        bet_ref[place] = bet_ref[place] - taken
    solve(bet_ref, gamma_ref, inv_ref, one_ref, head_ref)
    slot_of = lanes() - per_brick * (sub % tests)
    gathered = jnp.zeros((8, LANES), jnp.float32)
    for rank in range(per_brick):
        place, top = unpack(table_ref[listed_rows, rank])
        hit = (z_of >= top) & (z_of < top + SCREEN)
        values = jnp.where(hit, head_ref[place], 0.0)
        gathered = jnp.where(slot_of == rank, jnp.sum(values[0] + values[1], axis=1, keepdims=True), gathered)
    mine = obs_ref[2:3, :] > 0.5
    parts = []
    for part in range(2):
        total = jnp.sum(jnp.where(sub // tests == part, gathered, 0.0), axis=0, keepdims=True)
        parts.append(jnp.where(mine, total * (1.0 / SCREEN) - obs_ref[part : part + 1, :], 0.0))
    row_ref[...] = jnp.broadcast_to(jnp.concatenate(parts, axis=0)[None], row_ref.shape)


def adjoint_kernel(tests, per_brick, n_wells, joined, scale, resid_ref, table_in, clear_ref, clear_more_ref, e_ref, delta_ref, gamma_ref, inv_ref, head_ref,
                   bet_ref, more_ref, adj_ref, send_ref, weight_ref, one_ref, table_ref, sem):
    wide_x, wide_y, _ = e_ref.shape
    table_copy = pltpu.make_async_copy(table_in, table_ref, sem)
    table_copy.start()
    bricks = n_wells // per_brick
    sub = lax.broadcasted_iota(jnp.int32, (8, LANES), 0)
    z_of = z_of_tile()
    resid = resid_ref[:bricks] + resid_ref[bricks:] if joined else resid_ref[...]
    squares = jnp.sum(resid * resid, axis=0)
    lane = lax.broadcasted_iota(jnp.int32, (2, LANES), 1)
    misfit = jnp.zeros((2, LANES), jnp.float32)
    for test in range(tests):
        mine = lane // per_brick == test
        total = jnp.sum(jnp.where(mine, squares, 0.0), axis=1, keepdims=True)
        misfit = jnp.where(mine, total / n_wells + EPSILON, misfit)
    inverse = 1.0 / misfit
    for brick in range(bricks):
        row = resid[brick] * inverse
        weight_ref[brick] = jnp.where(sub < tests, row[0:1], row[1:2])
    listed_rows = list_length(per_brick) // LANES
    pick = per_brick * (sub % tests)

    def some_wells(turn, carry):
        todo = []
        for step in range(WELLS_AT_ONCE):
            packed = table_ref[turn // turns_a_row, (turn % turns_a_row) * WELLS_AT_ONCE + step]
            column, top = unpack(packed)
            brick, rank = (packed >> 16) & 255, (packed >> 24) & 31
            value = jnp.take_along_axis(weight_ref[brick], pick + rank, axis=1, mode="promise_in_bounds")
            todo.append((column, jnp.where((z_of >= top) & (z_of < top + SCREEN), value[None], 0.0)))
        for step, (column, value) in enumerate(todo):
            into_ref = (bet_ref, more_ref)[step % 2]
            into_ref[column] = into_ref[column] + value
        return carry

    turns_a_row = LANES // WELLS_AT_ONCE
    table_copy.wait()
    turns = (table_ref[listed_rows + 2, 0] + WELLS_AT_ONCE - 1) // WELLS_AT_ONCE
    lax.fori_loop(0, turns, some_wells, 0)
    for x, low, high in reached(wide_x, wide_y, DEEP - 1):
        row = pl.ds(x * wide_y + low, high - low)
        bet_ref[row] = (bet_ref[row] + more_ref[row]) * spread(delta_ref, x, low, high)
    solve(bet_ref, gamma_ref, inv_ref, one_ref, adj_ref)

    gradient_half(jnp.where(second_half(), 0, 1), scale, e_ref, head_ref, adj_ref, send_ref)


def keep_kernel(scale, e_ref, head_ref, adj_ref, keep_ref):
    gradient_half(jnp.where(second_half(), 1, 0), scale, e_ref, head_ref, adj_ref, keep_ref)


def gradient_half(part, scale, e_ref, head_ref, adj_ref, out_ref):
    wide_x, wide_y, _ = e_ref.shape
    low, high = DEEP, wide_y - DEEP
    is_first = part == 0
    at_first, at_last = lanes() == 0, lanes() == LANES - 1

    def spread_part(x, first, last):
        rows = [e_ref[x, pl.ds(y, 1), pl.ds(pl.multiple_of(part * LANES, LANES), LANES)] for y in range(first, last)]
        return jnp.stack([jnp.broadcast_to(row, (8, LANES)) for row in rows])

    def tiles(ref, x, first, last, which):
        return ref[x * wide_y + first : x * wide_y + last, which]

    def crossing(values, others, edge, turn, end):
        turned, other = pltpu.roll(values, turn, 2), pltpu.roll(others, turn, 2)
        return jnp.where(end, jnp.where(is_first == (turn != 1), other, edge), turned)

    before = None
    for x in range(DEEP - 1, wide_x - DEEP):
        e, head, adjoint = spread_part(x, low, high), tiles(head_ref, x, low, high, part), tiles(adj_ref, x, low, high, part)
        gap = (head - tiles(head_ref, x + 1, low, high, part)) * (adjoint - tiles(adj_ref, x + 1, low, high, part))
        after = e * spread_part(x + 1, low, high) * gap
        if x >= DEEP:
            total = before + after
            e_y = spread_part(x, low - 1, high + 1)
            head_y, adjoint_y = tiles(head_ref, x, low - 1, high + 1, part), tiles(adj_ref, x, low - 1, high + 1, part)
            sides = e_y[:-1] * e_y[1:] * (head_y[:-1] - head_y[1:]) * (adjoint_y[:-1] - adjoint_y[1:])
            total = total + sides[:-1] + sides[1:]
            halves = [ref[x, low:high, other * LANES : (other + 1) * LANES] for ref in (e_ref,) for other in range(2)]
            e_other = jnp.stack([jnp.broadcast_to(jnp.where(is_first, halves[1], halves[0])[y : y + 1], (8, LANES)) for y in range(high - low)])
            head_other, adjoint_other = tiles(head_ref, x, low, high, 1 - part), tiles(adj_ref, x, low, high, 1 - part)
            for turn, end in ((LANES - 1, at_last), (1, at_first)):
                e_near = crossing(e, e_other, 1.0, turn, end)
                head_near, adjoint_near = crossing(head, head_other, 0.0, turn, end), crossing(adjoint, adjoint_other, 0.0, turn, end)
                total = total + e * e_near * (head - head_near) * (adjoint - adjoint_near)
            total = jnp.sum(total, axis=1, keepdims=True) * scale
            for y in range(high - low):
                out_ref[x - DEEP, pl.ds(y, 1), :] = total[y]
        before = after


def vmem():
    return pl.BlockSpec(memory_space=pltpu.VMEM)


def smem():
    return pl.BlockSpec(memory_space=pltpu.SMEM)


def f32(*shape):
    return jax.ShapeDtypeStruct(shape, jnp.float32)


def i32(*shape):
    return jax.ShapeDtypeStruct(shape, jnp.int32)


PARAMS = pltpu.CompilerParams(vmem_limit_bytes=24 * 1024 * 1024)


def local(log_conductivity, storage, recharge, pump_rate, pump_well, observed, owner, screen_column, screen_top):
    size_x, size_y, size_z = log_conductivity.shape
    half_x = size_x // 2
    tests = pump_rate.shape[0]
    n_wells = owner.shape[0]
    groups, n_bx, n_by = lax.axis_size("test"), lax.axis_size("bx"), lax.axis_size("by")
    bricks = n_bx * n_by
    per_brick = n_wells // bricks
    plan = slab_plan(half_x)
    rows_x = 3 * DEEP - 2
    rows_y = sum(count for _, _, count in plan)
    wide_x, wide_y = half_x + 2 * DEEP, size_y + 2 * DEEP
    tiles = (wide_x * wide_y, 2, 8, LANES)
    table_scratch = [pltpu.SMEM((8, LANES), jnp.int32), pltpu.SemaphoreType.DMA]

    def in_hbm(*arrays):
        return [pltpu.with_memory_space_constraint(a, pltpu.HBM) for a in arrays]

    hbm = pl.BlockSpec(memory_space=pltpu.HBM)
    slab = pl.pallas_call(
        edge_kernel,
        out_shape=f32(rows_x, size_y, size_z),
        in_specs=[hbm] * 3,
        out_specs=vmem(),
        scratch_shapes=[pltpu.SemaphoreType.DMA((3,))],
        compiler_params=PARAMS,
        name="edge",
    )(*in_hbm(log_conductivity, storage, recharge))
    got_x = lax.ppermute(slab, ("test", "bx"), circle(n_bx, groups))

    inputs = (
        observed,
        pump_rate.reshape(1, tests),
        pump_well.reshape(1, tests),
        owner.reshape(1, n_wells),
        screen_column.reshape(1, n_wells),
        screen_top.reshape(1, n_wells),
        log_conductivity,
        storage,
        recharge,
    )
    owner, column, top, log_k, sto, rec, facts = pl.pallas_call(
        load_kernel,
        out_shape=[jax.ShapeDtypeStruct(a.shape, a.dtype) for a in inputs[3:]] + [f32(8, n_wells)],
        in_specs=[hbm] * len(inputs) + [vmem()],
        out_specs=[vmem()] * (len(inputs) - 2),
        scratch_shapes=[pltpu.VMEM((1, tests), jnp.float32), pltpu.VMEM((1, tests), jnp.int32), pltpu.SemaphoreType.DMA((len(inputs),))],
        compiler_params=PARAMS,
        name="load",
    )(*in_hbm(*inputs), slab)
    pairs = [(test, pair_of(test, groups)) for test in range(groups)]
    other_facts = lax.ppermute(facts, "test", pairs)

    bx, by, second = lax.axis_index("bx"), lax.axis_index("by"), lax.axis_index("test") % 2
    well_x = (owner // n_by - bx) * size_x + column // size_y + DEEP - second * half_x
    well_y = (owner % n_by - by) * size_y + column % size_y + DEEP
    out_x = jnp.maximum(jnp.maximum(DEEP - well_x, well_x - (DEEP + half_x - 1)), 0)
    out_y = jnp.maximum(jnp.maximum(DEEP - well_y, well_y - (DEEP + size_y - 1)), 0)
    in_window = (out_x + out_y < DEEP).astype(jnp.float32)
    owned = (out_x + out_y == 0).astype(jnp.float32)
    place = jnp.where(in_window > 0.5, well_x * wide_y + well_y, 0)
    window = f32(wide_x, wide_y, size_z)
    e, sto_w, rec_w = pl.pallas_call(
        window_kernel,
        out_shape=[window] * 3,
        in_specs=[vmem()] * 3,
        out_specs=[vmem()] * 3,
        compiler_params=PARAMS,
        name="window",
    )(log_k, sto, rec)
    e, sto_w, rec_w, even_y, odd_y = pl.pallas_call(
        functools.partial(pack_y, plan),
        out_shape=[window] * 3 + [f32(rows_y, size_z)] * 2,
        in_specs=[vmem()] * 4,
        out_specs=[vmem()] * 5,
        input_output_aliases={1: 0, 2: 1, 3: 2},
        compiler_params=PARAMS,
        name="pack_y",
    )(got_x, e, sto_w, rec_w)
    even, odd = side_partners(n_by, groups)
    got_even = lax.ppermute(even_y, ("test", "by"), even)
    got_odd = lax.ppermute(odd_y, ("test", "by"), odd)

    table, obs, clear, clear_more = pl.pallas_call(
        functools.partial(wells_kernel, tests, per_brick, bricks),
        out_shape=[i32(8, LANES), f32(8, LANES), f32(*tiles), f32(*tiles)],
        in_specs=[vmem()] * 8,
        out_specs=[vmem()] * 4,
        compiler_params=PARAMS,
        name="wells",
    )(owner, place, top, in_window, owned, facts, other_facts, even_y)

    joined = groups == 2
    copies = groups * bricks if joined else bricks
    e, delta, gamma, inverse, head, row, _, _ = pl.pallas_call(
        functools.partial(heads_kernel, plan, tests, per_brick),
        out_shape=[window] * 4 + [f32(*tiles), f32(copies, 2, LANES)] + [window] * 2,
        in_specs=[vmem()] * 7,
        out_specs=[vmem()] * 8,
        scratch_shapes=[pltpu.VMEM((wide_x, wide_y, size_z), jnp.float32)] + [pltpu.VMEM(tiles, jnp.float32)] * 2 + table_scratch,
        input_output_aliases={2: 0, 3: 6, 4: 7},
        compiler_params=PARAMS,
        name="heads",
    )(got_even, got_odd, e, sto_w, rec_w, table, obs)

    if joined:
        residuals = lax.all_to_all(row, ("test", "bx", "by"), 0, 0)
    else:
        residuals = lax.all_to_all(row + lax.ppermute(row, "test", pairs), ("bx", "by"), 0, 0)

    scale = -0.5 / (tests * groups)
    _, _, adjoint, send = pl.pallas_call(
        functools.partial(adjoint_kernel, tests, per_brick, n_wells, joined, scale),
        out_shape=[f32(*tiles)] * 3 + [f32(half_x, size_y, LANES)],
        in_specs=[vmem()] * 9,
        out_specs=[vmem()] * 4,
        scratch_shapes=[pltpu.VMEM((bricks, 8, LANES), jnp.float32), pltpu.VMEM(tiles, jnp.float32)] + table_scratch,
        input_output_aliases={2: 0, 3: 1},
        compiler_params=PARAMS,
        name="adjoint",
    )(residuals, table, clear, clear_more, e, delta, gamma, inverse, head)
    other = lax.ppermute(send, "test", pairs) if joined else send
    keep = pl.pallas_call(
        functools.partial(keep_kernel, scale),
        out_shape=f32(half_x, size_y, LANES),
        in_specs=[vmem()] * 3,
        out_specs=vmem(),
        compiler_params=PARAMS,
        name="keep",
    )(e, head, adjoint)
    if joined:
        return jnp.where(second == 0, jnp.concatenate([keep, other], axis=0), jnp.concatenate([other, keep], axis=0))
    low, high = jnp.where(second == 0, keep, send), jnp.where(second == 0, send, keep)
    half = jnp.concatenate([low, high], axis=2)
    none = jnp.zeros_like(half)
    whole = jnp.where(second == 0, jnp.concatenate([half, none], axis=0), jnp.concatenate([none, half], axis=0))
    return lax.psum_scatter(whole, "test", scatter_dimension=2, tiled=True)


def solution(mesh):
    placed = (
        P("bx", "by", None),
        P("bx", "by", None),
        P("bx", "by", None),
        P("test"),
        P("test"),
        P("test", None),
        P(),
        P(),
        P(),
    )
    return jax.shard_map(local, mesh=mesh, in_specs=placed, out_specs=P("bx", "by", "test"), check_vma=False)
```

time: 231 us -> 30.4 us (0.13)
  starting transfers between devices: 74 us -> 6.35 us
  other arithmetic: 36.6 us -> 0.68 us
  blocking collectives: 46.5 us -> 12.9 us
  local copies, waits for them, and re-layouts: 29.2 us -> 0 us
  waiting for transfers between devices: 29.8 us -> 2.99 us
  between operations: 13.9 us -> 0.13 us
  Pallas kernels: 0 us -> 7.19 us
    ppermute x24 -> x5, starting transfers between devices: 74 us -> 6.35 us  [the longest x1 3.14 us: local(): got_even = lax.ppermute(even_y, ('test', 'by'), even)]
    psum x1 -> x0, blocking collectives: 46.5 us -> none  [per_sweep_terms(): lax.psum(jnp.sum(residual * residual, axis=1), ('bx', 'by')) / well_count]
    scatter-add x2 -> x0, other arithmetic: 28.2 us -> none  [the longest x1 26.1 us: per_sweep_terms(): jnp.zeros((tests_here, cell_count), jnp.float32)]
    gather x3 -> x0, local copies, waits for them, and re-layouts: 16 us -> none  [the longest x1 14.1 us: per_sweep_terms(): heads_field.reshape(tests_here, cell_count)[:, screen_cells]]
    reduce_scatter x1 -> x0, waiting for transfers between devices: 13.7 us -> none  [local(): lax.psum_scatter(local_sum, 'test', scatter_dimension=2, tiled=True)]
    ppermute x24 -> x5, waiting for transfers between devices: 16.2 us -> 2.99 us  [the longest x1 1.59 us: local(): got_even = lax.ppermute(even_y, ('test', 'by'), even)]
    all_to_all x0 -> x1, blocking collectives: none -> 12.9 us  [local(): residuals = lax.all_to_all(row, ('test', 'bx', 'by'), 0, 0)]
    pallas_call x0 -> x8, Pallas kernels: none -> 7.19 us  [the longest x1 2.35 us: local(): pl.pallas_call(functools.partial(adjoint_kernel, tests, per_brick, n_well...]
  transfers between devices with their start and end apart: 25 -> 5, of which waited for: 13 -> 3; matrix products, arithmetic and copies ran while one was open for 4% -> 0% of each run, Pallas kernels for 0% -> 8%
where the time goes in v3:
time: 30.4 us; the launch traced here: 30.2 us
  blocking collectives  12.9 us (42%)
  Pallas kernels  7.19 us (24%)
  starting transfers between devices  6.35 us (21%)
  waiting for transfers between devices  2.99 us (10%)
  other arithmetic  0.68 us (2%)
    all_to_all x1, blocking collectives, local(): residuals = lax.all_to_all(row, ('test', 'bx', 'by'), 0, 0)  12.9 us
    ppermute x1, starting transfers between devices, local(): got_even = lax.ppermute(even_y, ('test', 'by'), even)  3.14 us
    ppermute x1, starting transfers between devices, local(): got_x = lax.ppermute(slab, ('test', 'bx'), circle(n_bx, groups))  3 us
    pallas_call x1, Pallas kernels, local(): pl.pallas_call(functools.partial(adjoint_kernel, tests, per_brick, n_well...  2.35 us
    pallas_call x1, Pallas kernels, local(): pl.pallas_call(functools.partial(heads_kernel, plan, tests, per_brick), o...  1.7 us
    ppermute x1, waiting for transfers between devices, local(): got_even = lax.ppermute(even_y, ('test', 'by'), even)  1.59 us
    pallas_call x1, Pallas kernels, local(): pl.pallas_call(load_kernel, out_shape=[jax.ShapeDtypeStruct(a.shape, a.dt...  1.08 us
    pallas_call x1, Pallas kernels, local(): pl.pallas_call(edge_kernel, out_shape=f32(rows_x, size_y, size_z), in_spe...  0.8 us
  transfers between devices with their start and end apart: 5, of which 3 were waited for; matrix products, arithmetic and copies ran while one was open for 0% of the time, Pallas kernels for 8%

profile of v3, /device:TPU:0, one launch (start us, length us, event | category | flops | bytes accessed | tf_op | source)
XLA Modules:
  0.0 30.2 jit_solution(5320243834184110566)
XLA Ops:
  0.0 0.8 %edge.1.refs_6_ = f32[10,8,256]{2,1,0:T(8,128)S(1)} custom-call(f32[8,8,256]{2,1,0:T(8,128)} %refs_3_.1, f32[8,8,256]{2,1,0:T(8,128)} %refs_4_.1, f32[8,8,256]{2,1,0:T(8,128)} %refs_5_.1), custom_call_target="tpu_custom_call" | custom-call | tf_op jit(solution)/shard_map/edge/pallas_call | solution.py:464
  0.8 3.0 %collective-permute-start = (f32[10,8,256]{2,1,0:T(8,128)S(1)}, f32[10,8,256]{2,1,0:T(8,128)S(1)}, u32[]{:S(2)}, u32[]{:S(2)}) collective-permute-start(f32[10,8,256]{2,1,0:T(8,128)S(1)} %edge.1.refs_6_), channel_id=1, source_target_pairs={{0,4},{4,8},{8,12},{12,28},{16,0},{20,16},{24,20},{28,24},{1,5},{5... | collective-permute-start | bytes 245768 | tf_op jit(solution)/shard_map/ppermute | solution.py:473
  3.8 1.1 %load.1 = (s32[1,512]{1,0:T(1,128)S(1)}, s32[1,512]{1,0:T(1,128)S(1)}, s32[1,512]{1,0:T(1,128)S(1)}, f32[8,8,256]{2,1,0:T(8,128)S(1)}, f32[8,8,256]{2,1,0:T(8,12...) custom-call(f32[4,512]{1,0:T(4,128)} %observed.1, f32[1,4]{1,0:T(1,128)} %bitcast.8, s32[1,4]{1,0:T(1,128)} %bitcast.9, ...), custom_call_target="tpu_custom_call" | custom-call | tf_op jit(solution)/shard_map/load/pallas_call | solution.py:486
  4.9 0.1 collective-permute-start.3
  5.0 0.1 compare_convert_fusion
  5.1 0.8 %collective-permute-done.slab_ref = f32[10,8,256]{2,1,0:T(8,128)S(1)} collective-permute-done((f32[10,8,256]{2,1,0:T(8,128)S(1)}, f32[10,8,256]{2,1,0:T(8,128)S(1)}, u32[]{:S(2)}, u32[]{:S(2)}) %collective-permute-start) | collective-permute-done | bytes 81952 | tf_op jit(solution)/shard_map/ppermute | solution.py:473
  5.9 0.1 pack_y.1
  5.9 0.1 collective-permute-start.2
  6.0 3.1 %collective-permute-start.1 = (f32[64,256]{1,0:T(8,128)S(1)}, f32[64,256]{1,0:T(8,128)S(1)}, u32[]{:S(2)}, u32[]{:S(2)}) collective-permute-start(f32[64,256]{1,0:T(8,128)S(1)} %get-tuple-element.38._), channel_id=1, source_target_pairs={{0,1},{1,0},{2,3},{3,2},{16,17},{17,16},{18,19},{19,18},{4,5},{5,4... | collective-permute-start | bytes 196616 | tf_op jit(solution)/shard_map/ppermute | solution.py:525
  9.2 0.0 collective-permute-done.3.other_ref
  9.2 0.6 %wells.1 = (s32[8,128]{1,0:T(8,128)S(1)}, f32[8,128]{1,0:T(8,128)S(1)}, f32[192,2,8,128]{3,2,1,0:T(8,128)S(1)}, f32[192,2,8,128]{3,2,1,0:T(8,128)S(1)}) custom-call(s32[1,512]{1,0:T(1,128)S(1)} %get-tuple-element.43.owner_ref, s32[1,512]{1,0:T(1,128)S(1)} %compare_select_fusion.place_ref, s32[1,512]{1,0:T(1,128)S(1)} %get-tuple-element.45.top_ref, ...), custom_call_target="tpu_custom_call" | custom-call | tf_op jit(solution)/shard_map/wells/pallas_call | solution.py:528
  9.8 0.0 collective-permute-done.2.odd_ref
  9.8 1.6 %collective-permute-done.1.even_ref = f32[64,256]{1,0:T(8,128)S(1)} collective-permute-done((f32[64,256]{1,0:T(8,128)S(1)}, f32[64,256]{1,0:T(8,128)S(1)}, u32[]{:S(2)}, u32[]{:S(2)}) %collective-permute-start.1) | collective-permute-done | bytes 65568 | tf_op jit(solution)/shard_map/ppermute | solution.py:525
  11.4 1.7 %heads.1 = (f32[12,16,256]{2,1,0:T(8,128)S(1)}, f32[12,16,256]{2,1,0:T(8,128)S(1)}, f32[12,16,256]{2,1,0:T(8,128)S(1)}, f32[12,16,256]{2,1,0:T(8,128)S(1)}, f32[...) custom-call(f32[64,256]{1,0:T(8,128)S(1)} %collective-permute-done.1, ...), custom_call_target="tpu_custom_call", output_to_operand_aliasing={{0}: (2, {}), {6}: (3, {}), {7}: (4, {})} | custom-call | tf_op jit(solution)/shard_map/heads/pallas_call | solution.py:539
  13.1 12.9 %all_to_all.5.resid_ref = f32[32,2,128]{2,1,0:T(2,128)S(1)} all-to-all(f32[32,2,128]{2,1,0:T(2,128)S(1)} %get-tuple-element.51), channel_id=1, replica_groups=mesh['test'=2,'bx'=4,'by'=4] {'test','bx','by'}, dimensions={0} | all-to-all | bytes 65536 | tf_op jit(solution)/shard_map/all_to_all | solution.py:551
  26.0 2.3 %adjoint.1 = (f32[192,2,8,128]{3,2,1,0:T(8,128)S(1)}, f32[192,2,8,128]{3,2,1,0:T(8,128)S(1)}, f32[192,2,8,128]{3,2,1,0:T(8,128)S(1)}, f32[4,8,128]{2,1,0:T(8,128)S(1)}) custom-call(f32[32,2,128]{2,1,0:T(2,128)S(1)} %all_to_all.5.resid_ref, s32[8,128]{1,0:T(8,128)S(1)} %get-tuple-element.47.table_in, ...), custom_call_target="tpu_custom_call", output_to_operand_aliasing={{0}: (2, {}), {1}: (3, {})} | custom-call | tf_op jit(solution)/shard_map/adjoint/pallas_call | solution.py:556
  28.3 0.1 collective-permute-start.4
  28.4 0.5 %keep.1 = f32[4,8,128]{2,1,0:T(8,128)S(1)} custom-call(f32[12,16,256]{2,1,0:T(8,128)S(1)} %get-tuple-element.49.e_ref, f32[192,2,8,128]{3,2,1,0:T(8,128)S(1)} %get-tuple-element.50.head_ref, f32[192,2,8,128]{3,2,1,0:T(8,128)S(1)} %get-tuple-element.57.adj_ref), custom_call_target="tpu_custom_call" | custom-call | tf_op jit(solution)/shard_map/keep/pallas_call | solution.py:567
  29.0 0.6 %collective-permute-done.4 = f32[4,8,128]{2,1,0:T(8,128)S(1)} collective-permute-done((f32[4,8,128]{2,1,0:T(8,128)S(1)}, f32[4,8,128]{2,1,0:T(8,128)S(1)}, u32[]{:S(2)}, u32[]{:S(2)}) %collective-permute-start.4) | collective-permute-done | bytes 16416 | tf_op jit(solution)/shard_map/ppermute | solution.py:566
  29.6 0.6 %maximum_select_fusion = f32[8,8,128]{2,1,0:T(8,128)} fusion(f32[4,8,128]{2,1,0:T(8,128)S(1)} %collective-permute-done.4, f32[4,8,128]{2,1,0:T(8,128)S(1)} %keep.1, pred[]{:T(512)S(6)} %eq.11), kind=kLoop, calls=%fused_computation | loop fusion | flops 24576 | bytes 65537 | tf_op jit(solution)/shard_map/jit(_where)/select_n | solution.py:576
  (3 shorter events, 0.1 us)
Async XLA Ops:
  0.8 5.1 %collective-permute-start = (f32[10,8,256]{2,1,0:T(8,128)S(1)}, f32[10,8,256]{2,1,0:T(8,128)S(1)}, u32[]{:S(2)}, u32[]{:S(2)}) collective-permute-start(f32[10,8,256]{2,1,0:T(8,128)S(1)} %edge.1.refs_6_), channel_id=1, source_target_pairs={{0,4},{4,8},{8,12},{12,28},{16,0},{20,16},{24,20},{28,24},{1,5},{5... | collective-permute-start | bytes 245768 | tf_op jit(solution)/shard_map/ppermute | solution.py:473
  4.9 4.3 %collective-permute-start.3 = (f32[8,512]{1,0:T(8,128)S(1)}, f32[8,512]{1,0:T(8,128)S(1)}, u32[]{:S(2)}, u32[]{:S(2)}) collective-permute-start(f32[8,512]{1,0:T(8,128)S(1)} %get-tuple-element.46.facts_ref), channel_id=1, source_target_pairs={{0,16},{16,0},{1,17},{17,1},{2,18},{18,2},{3,19},{19,3},{4,20},{20... | collective-permute-start | bytes 49160 | tf_op jit(solution)/shard_map/ppermute | solution.py:496
  5.9 3.9 %collective-permute-start.2 = (f32[64,256]{1,0:T(8,128)S(1)}, f32[64,256]{1,0:T(8,128)S(1)}, u32[]{:S(2)}, u32[]{:S(2)}) collective-permute-start(f32[64,256]{1,0:T(8,128)S(1)} %get-tuple-element.39), channel_id=1, source_target_pairs={{0,16},{1,2},{2,1},{3,19},{16,0},{17,18},{18,17},{19,3},{4,20},{5,... | collective-permute-start | bytes 196616 | tf_op jit(solution)/shard_map/ppermute | solution.py:526
  6.0 5.4 %collective-permute-start.1 = (f32[64,256]{1,0:T(8,128)S(1)}, f32[64,256]{1,0:T(8,128)S(1)}, u32[]{:S(2)}, u32[]{:S(2)}) collective-permute-start(f32[64,256]{1,0:T(8,128)S(1)} %get-tuple-element.38._), channel_id=1, source_target_pairs={{0,1},{1,0},{2,3},{3,2},{16,17},{17,16},{18,19},{19,18},{4,5},{5,4... | collective-permute-start | bytes 196616 | tf_op jit(solution)/shard_map/ppermute | solution.py:525
  28.3 1.2 %collective-permute-start.4 = (f32[4,8,128]{2,1,0:T(8,128)S(1)}, f32[4,8,128]{2,1,0:T(8,128)S(1)}, u32[]{:S(2)}, u32[]{:S(2)}) collective-permute-start(f32[4,8,128]{2,1,0:T(8,128)S(1)} %get-tuple-element.58), channel_id=1, source_target_pairs={{0,16},{16,0},{1,17},{17,1},{2,18},{18,2},{3,19},{19,3},{4,20},{20... | collective-permute-start | bytes 49160 | tf_op jit(solution)/shard_map/ppermute | solution.py:566

commit v4 on v3

--- a/solution.py
+++ b/solution.py
@@ -13,6 +13,7 @@
 EPSILON = 1e-06
 WELL_CHUNK = 512
 WELLS_AT_ONCE = 16
+COLUMNS_AT_ONCE = 1
 
 
 def list_length(per_brick):
@@ -101,7 +102,8 @@
     mine, theirs = facts_ref[...], other_ref[...]
     facts = (jnp.where(swapped, theirs, mine), jnp.where(swapped, mine, theirs))
     total = jnp.zeros((bricks + 16, 1), jnp.float32)
-    result = jnp.zeros((32, listed + LANES + 16), jnp.float32)
+    found = jnp.zeros((listed + LANES + 16, 32), jnp.float32)
+    result = jnp.zeros((32, LANES), jnp.float32)
     for start in range(0, n_wells, chunk):
         part = slice(start, start + chunk)
         owner = owner_ref[:, part]
@@ -128,25 +130,25 @@
                 value = value - piece
         rows.append(jnp.zeros((32 - len(rows), chunk), jnp.float32))
         carried = jnp.concatenate(rows, axis=0).astype(jnp.bfloat16)
-        result = result + lax.dot_general(carried, chosen, (((1,), (1,)), ((), ())), preferred_element_type=jnp.float32)
-    numbers = [result[row : row + 1].astype(jnp.int32) for row in range(5)]
-    words = numbers[0] + (numbers[1] << 8) + (numbers[2] << 16) + (numbers[3] << 24) + (numbers[4] << 30)
-    listed_rows = listed // LANES
-    for row in range(listed_rows + 1):
-        table_ref[row : row + 1, :] = words[:, row * LANES : (row + 1) * LANES]
-    table_ref[listed_rows + 1 : listed_rows + 2, :16] = words[:, listed + LANES :]
-    found = jnp.broadcast_to(total[bricks : bricks + 1], (1, LANES)).astype(jnp.int32)
-    table_ref[listed_rows + 2 : listed_rows + 3, :] = found
+        over_wells = (((1,), (1,)), ((), ()))
+        found = found + lax.dot_general(chosen, carried, over_wells, preferred_element_type=jnp.float32)
+        result = result + lax.dot_general(carried, chosen[listed : listed + LANES], over_wells, preferred_element_type=jnp.float32)
+    column = lax.broadcasted_iota(jnp.int32, found.shape, 1)
+    low = jnp.where(column == 0, 1.0, jnp.where(column == 1, 256.0, 0.0))
+    high = jnp.where(column == 2, 1.0, jnp.where(column == 3, 256.0, jnp.where(column == 4, 16384.0, 0.0)))
+    low, high = (jnp.sum(found * weights, axis=1, keepdims=True).astype(jnp.int32) for weights in (low, high))
+    table_ref[0 : listed + LANES + 16, :] = low + (high << 16)
+    table_ref[listed + LANES + 16 :, :] = jnp.broadcast_to(total[bricks : bricks + 1], (8, 1)).astype(jnp.int32)
     lane = lax.broadcasted_iota(jnp.int32, (1, LANES), 1)
     for part in range(2):
         values = jnp.zeros((1, LANES), jnp.float32)
         for test in range(tests):
             first = 5 + 3 * (part * tests + test)
-            pieces = [result[row : row + 1, listed : listed + LANES] for row in range(first, first + 3)]
+            pieces = [result[row : row + 1] for row in range(first, first + 3)]
             values = jnp.where(lane // per_brick == test, pieces[0] + (pieces[1] + pieces[2]), values)
         obs_ref[part : part + 1, :] = values
         obs_ref[3 + part : 4 + part, 0:tests] = facts[part][tests : tests + 1, 0:tests]
-    obs_ref[2:3, :] = result[4:5, listed : listed + LANES]
+    obs_ref[2:3, :] = result[4:5]
     clear_ref[...] = jnp.zeros(clear_ref.shape, jnp.float32)
     clear_more_ref[...] = jnp.zeros(clear_ref.shape, jnp.float32)
 
@@ -259,11 +261,17 @@
     return cells
 
 
+def grouped(cells):
+    for x, first, end in cells:
+        for low in range(first, end, COLUMNS_AT_ONCE):
+            yield x, low, min(low + COLUMNS_AT_ONCE, end)
+
+
 def solve(bet_ref, gamma_ref, inv_ref, one_ref, two_ref):
     wide_x, wide_y, _ = gamma_ref.shape
-    for x, low, high in reached(wide_x, wide_y, DEEP - 2):
+    for x, low, high in grouped(reached(wide_x, wide_y, DEEP - 2)):
         one_ref[x * wide_y + low : x * wide_y + high] = sweep(bet_ref, gamma_ref, bet_ref, x, low, high)
-    for x, low, high in reached(wide_x, wide_y, DEEP - 3):
+    for x, low, high in grouped(reached(wide_x, wide_y, DEEP - 3)):
         scaled = sweep(bet_ref, gamma_ref, one_ref, x, low, high)
         two_ref[x * wide_y + low : x * wide_y + high] = scaled * spread(inv_ref, x, low, high)
 
@@ -276,11 +284,9 @@
     return packed & 255, (packed >> 8) & 255
 
 
-def heads_kernel(plan, tests, per_brick, even_ref, odd_ref, e_in, sto_in, rec_in, table_in, obs_ref,
-                 e_ref, delta_ref, gamma_ref, inv_ref, head_ref, row_ref, sto_w, rec_w, beta_ref, bet_ref, one_ref, table_ref, sem):
+def heads_kernel(plan, tests, per_brick, even_ref, odd_ref, e_in, sto_in, rec_in, table_ref, obs_ref,
+                 e_ref, delta_ref, gamma_ref, inv_ref, head_ref, row_ref, sto_w, rec_w, beta_ref, bet_ref, one_ref):
     wide_x, wide_y, _ = e_ref.shape
-    table_copy = pltpu.make_async_copy(table_in, table_ref, sem)
-    table_copy.start()
     by = lax.axis_index("by")
     y_even = by % 2 == 0
     no_low, no_high = by == 0, by == lax.axis_size("by") - 1
@@ -300,11 +306,10 @@
         bet_ref[x * wide_y + low : x * wide_y + high] = spread(beta_ref, x, low, high)
     sub = lax.broadcasted_iota(jnp.int32, (8, LANES), 0)
     z_of = z_of_tile()
-    listed_rows = list_length(per_brick) // LANES
-    table_copy.wait()
+    listed = list_length(per_brick)
     pumped = []
     for test in range(2 * tests):
-        packed = table_ref[listed_rows + 1, test]
+        packed = table_ref[listed + LANES + test, 0]
         place, top = unpack(packed)
         near = (packed >> 30) & 1 == 1
         rate = obs_ref[3 + test // tests : 4 + test // tests, test % tests : test % tests + 1]
@@ -318,7 +323,7 @@
     slot_of = lanes() - per_brick * (sub % tests)
     gathered = jnp.zeros((8, LANES), jnp.float32)
     for rank in range(per_brick):
-        place, top = unpack(table_ref[listed_rows, rank])
+        place, top = unpack(table_ref[listed + rank, 0])
         hit = (z_of >= top) & (z_of < top + SCREEN)
         values = jnp.where(hit, head_ref[place], 0.0)
         gathered = jnp.where(slot_of == rank, jnp.sum(values[0] + values[1], axis=1, keepdims=True), gathered)
@@ -330,33 +335,22 @@
     row_ref[...] = jnp.broadcast_to(jnp.concatenate(parts, axis=0)[None], row_ref.shape)
 
 
-def adjoint_kernel(tests, per_brick, n_wells, joined, scale, resid_ref, table_in, clear_ref, clear_more_ref, e_ref, delta_ref, gamma_ref, inv_ref, head_ref,
-                   bet_ref, more_ref, adj_ref, send_ref, weight_ref, one_ref, table_ref, sem):
+def adjoint_kernel(tests, per_brick, n_wells, joined, scale, resid_ref, table_ref, clear_ref, clear_more_ref, e_ref, delta_ref, gamma_ref, inv_ref, head_ref,
+                   bet_ref, more_ref, adj_ref, send_ref, norm_ref, weight_ref, one_ref):
     wide_x, wide_y, _ = e_ref.shape
-    table_copy = pltpu.make_async_copy(table_in, table_ref, sem)
-    table_copy.start()
     bricks = n_wells // per_brick
     sub = lax.broadcasted_iota(jnp.int32, (8, LANES), 0)
     z_of = z_of_tile()
     resid = resid_ref[:bricks] + resid_ref[bricks:] if joined else resid_ref[...]
-    squares = jnp.sum(resid * resid, axis=0)
-    lane = lax.broadcasted_iota(jnp.int32, (2, LANES), 1)
-    misfit = jnp.zeros((2, LANES), jnp.float32)
-    for test in range(tests):
-        mine = lane // per_brick == test
-        total = jnp.sum(jnp.where(mine, squares, 0.0), axis=1, keepdims=True)
-        misfit = jnp.where(mine, total / n_wells + EPSILON, misfit)
-    inverse = 1.0 / misfit
     for brick in range(bricks):
-        row = resid[brick] * inverse
-        weight_ref[brick] = jnp.where(sub < tests, row[0:1], row[1:2])
-    listed_rows = list_length(per_brick) // LANES
+        weight_ref[brick] = jnp.where(sub < tests, resid[brick, 0:1], resid[brick, 1:2])
+    listed = list_length(per_brick)
     pick = per_brick * (sub % tests)
 
     def some_wells(turn, carry):
         todo = []
         for step in range(WELLS_AT_ONCE):
-            packed = table_ref[turn // turns_a_row, (turn % turns_a_row) * WELLS_AT_ONCE + step]
+            packed = table_ref[turn * WELLS_AT_ONCE + step, 0]
             column, top = unpack(packed)
             brick, rank = (packed >> 16) & 255, (packed >> 24) & 31
             value = jnp.take_along_axis(weight_ref[brick], pick + rank, axis=1, mode="promise_in_bounds")
@@ -366,23 +360,24 @@
             into_ref[column] = into_ref[column] + value
         return carry
 
-    turns_a_row = LANES // WELLS_AT_ONCE
-    table_copy.wait()
-    turns = (table_ref[listed_rows + 2, 0] + WELLS_AT_ONCE - 1) // WELLS_AT_ONCE
+    turns = (table_ref[listed + LANES + 16, 0] + WELLS_AT_ONCE - 1) // WELLS_AT_ONCE
     lax.fori_loop(0, turns, some_wells, 0)
     for x, low, high in reached(wide_x, wide_y, DEEP - 1):
         row = pl.ds(x * wide_y + low, high - low)
         bet_ref[row] = (bet_ref[row] + more_ref[row]) * spread(delta_ref, x, low, high)
     solve(bet_ref, gamma_ref, inv_ref, one_ref, adj_ref)
-
-    gradient_half(jnp.where(second_half(), 0, 1), scale, e_ref, head_ref, adj_ref, send_ref)
-
-
-def keep_kernel(scale, e_ref, head_ref, adj_ref, keep_ref):
-    gradient_half(jnp.where(second_half(), 1, 0), scale, e_ref, head_ref, adj_ref, keep_ref)
-
-
-def gradient_half(part, scale, e_ref, head_ref, adj_ref, out_ref):
+    squares = jnp.sum(resid * resid, axis=0)
+    squares = jnp.where(sub < tests, squares[0:1], squares[1:2])
+    misfit = jnp.sum(jnp.where(lanes() // per_brick == sub % tests, squares, 0.0), axis=1, keepdims=True) / n_wells + EPSILON
+    norm_ref[...] = jnp.broadcast_to(scale / misfit, (8, LANES))
+    gradient_half(jnp.where(second_half(), 0, 1), norm_ref, e_ref, head_ref, adj_ref, send_ref)
+
+
+def keep_kernel(norm_ref, e_ref, head_ref, adj_ref, keep_ref):
+    gradient_half(jnp.where(second_half(), 1, 0), norm_ref, e_ref, head_ref, adj_ref, keep_ref)
+
+
+def gradient_half(part, norm_ref, e_ref, head_ref, adj_ref, out_ref):
     wide_x, wide_y, _ = e_ref.shape
     low, high = DEEP, wide_y - DEEP
     is_first = part == 0
@@ -417,7 +412,7 @@
                 e_near = crossing(e, e_other, 1.0, turn, end)
                 head_near, adjoint_near = crossing(head, head_other, 0.0, turn, end), crossing(adjoint, adjoint_other, 0.0, turn, end)
                 total = total + e * e_near * (head - head_near) * (adjoint - adjoint_near)
-            total = jnp.sum(total, axis=1, keepdims=True) * scale
+            total = jnp.sum(total * norm_ref[...], axis=1, keepdims=True)
             for y in range(high - low):
                 out_ref[x - DEEP, pl.ds(y, 1), :] = total[y]
         before = after
@@ -455,7 +450,6 @@
     rows_y = sum(count for _, _, count in plan)
     wide_x, wide_y = half_x + 2 * DEEP, size_y + 2 * DEEP
     tiles = (wide_x * wide_y, 2, 8, LANES)
-    table_scratch = [pltpu.SMEM((8, LANES), jnp.int32), pltpu.SemaphoreType.DMA]
 
     def in_hbm(*arrays):
         return [pltpu.with_memory_space_constraint(a, pltpu.HBM) for a in arrays]
@@ -527,7 +521,7 @@
 
     table, obs, clear, clear_more = pl.pallas_call(
         functools.partial(wells_kernel, tests, per_brick, bricks),
-        out_shape=[i32(8, LANES), f32(8, LANES), f32(*tiles), f32(*tiles)],
+        out_shape=[i32(list_length(per_brick) + LANES + 24, 1), f32(8, LANES), f32(*tiles), f32(*tiles)],
         in_specs=[vmem()] * 8,
         out_specs=[vmem()] * 4,
         compiler_params=PARAMS,
@@ -541,7 +535,7 @@
         out_shape=[window] * 4 + [f32(*tiles), f32(copies, 2, LANES)] + [window] * 2,
         in_specs=[vmem()] * 7,
         out_specs=[vmem()] * 8,
-        scratch_shapes=[pltpu.VMEM((wide_x, wide_y, size_z), jnp.float32)] + [pltpu.VMEM(tiles, jnp.float32)] * 2 + table_scratch,
+        scratch_shapes=[pltpu.VMEM((wide_x, wide_y, size_z), jnp.float32)] + [pltpu.VMEM(tiles, jnp.float32)] * 2,
         input_output_aliases={2: 0, 3: 6, 4: 7},
         compiler_params=PARAMS,
         name="heads",
@@ -553,25 +547,25 @@
         residuals = lax.all_to_all(row + lax.ppermute(row, "test", pairs), ("bx", "by"), 0, 0)
 
     scale = -0.5 / (tests * groups)
-    _, _, adjoint, send = pl.pallas_call(
+    _, _, adjoint, send, norm = pl.pallas_call(
         functools.partial(adjoint_kernel, tests, per_brick, n_wells, joined, scale),
-        out_shape=[f32(*tiles)] * 3 + [f32(half_x, size_y, LANES)],
+        out_shape=[f32(*tiles)] * 3 + [f32(half_x, size_y, LANES), f32(8, LANES)],
         in_specs=[vmem()] * 9,
-        out_specs=[vmem()] * 4,
-        scratch_shapes=[pltpu.VMEM((bricks, 8, LANES), jnp.float32), pltpu.VMEM(tiles, jnp.float32)] + table_scratch,
+        out_specs=[vmem()] * 5,
+        scratch_shapes=[pltpu.VMEM((bricks, 8, LANES), jnp.float32), pltpu.VMEM(tiles, jnp.float32)],
         input_output_aliases={2: 0, 3: 1},
         compiler_params=PARAMS,
         name="adjoint",
     )(residuals, table, clear, clear_more, e, delta, gamma, inverse, head)
     other = lax.ppermute(send, "test", pairs) if joined else send
     keep = pl.pallas_call(
-        functools.partial(keep_kernel, scale),
+        keep_kernel,
         out_shape=f32(half_x, size_y, LANES),
-        in_specs=[vmem()] * 3,
+        in_specs=[vmem()] * 4,
         out_specs=vmem(),
         compiler_params=PARAMS,
         name="keep",
-    )(e, head, adjoint)
+    )(norm, e, head, adjoint)
     if joined:
         return jnp.where(second == 0, jnp.concatenate([keep, other], axis=0), jnp.concatenate([other, keep], axis=0))
     low, high = jnp.where(second == 0, keep, send), jnp.where(second == 0, send, keep)

time: 30.4 us -> 29.4 us (0.967)
  Pallas kernels: 7.19 us -> 6.22 us
    pallas_call x1, Pallas kernels: 2.35 us -> 1.8 us  [local(): pl.pallas_call(functools.partial(adjoint_kernel, tests, per_brick, n_well...]
    pallas_call x1, Pallas kernels: 1.7 us -> 1.18 us  [local(): pl.pallas_call(functools.partial(heads_kernel, plan, tests, per_brick), o...]
where the time goes in v4:
time: 29.4 us; the launch traced here: 29.2 us
  blocking collectives  12.9 us (44%)
  starting transfers between devices  6.35 us (22%)
  Pallas kernels  6.22 us (21%)
  waiting for transfers between devices  2.89 us (10%)
  other arithmetic  0.68 us (2%)
    all_to_all x1, blocking collectives, local(): residuals = lax.all_to_all(row, ('test', 'bx', 'by'), 0, 0)  12.9 us
    ppermute x1, starting transfers between devices, local(): got_even = lax.ppermute(even_y, ('test', 'by'), even)  3.14 us
    ppermute x1, starting transfers between devices, local(): got_x = lax.ppermute(slab, ('test', 'bx'), circle(n_bx, groups))  3 us
    pallas_call x1, Pallas kernels, local(): pl.pallas_call(functools.partial(adjoint_kernel, tests, per_brick, n_well...  1.8 us
    ppermute x1, waiting for transfers between devices, local(): got_even = lax.ppermute(even_y, ('test', 'by'), even)  1.49 us
    pallas_call x1, Pallas kernels, local(): pl.pallas_call(functools.partial(heads_kernel, plan, tests, per_brick), o...  1.18 us
    pallas_call x1, Pallas kernels, local(): pl.pallas_call(load_kernel, out_shape=[jax.ShapeDtypeStruct(a.shape, a.dt...  1.08 us
    pallas_call x1, Pallas kernels, local(): pl.pallas_call(edge_kernel, out_shape=f32(rows_x, size_y, size_z), in_spe...  0.8 us
  transfers between devices with their start and end apart: 5, of which 3 were waited for; matrix products, arithmetic and copies ran while one was open for 0% of the time, Pallas kernels for 8%

profile of v4, /device:TPU:0, one launch (start us, length us, event | category | flops | bytes accessed | tf_op | source)
XLA Modules:
  0.0 29.2 jit_solution(4066160556835465531)
XLA Ops:
  0.0 0.8 %edge.1.refs_6_ = f32[10,8,256]{2,1,0:T(8,128)S(1)} custom-call(f32[8,8,256]{2,1,0:T(8,128)} %refs_3_.1, f32[8,8,256]{2,1,0:T(8,128)} %refs_4_.1, f32[8,8,256]{2,1,0:T(8,128)} %refs_5_.1), custom_call_target="tpu_custom_call" | custom-call | tf_op jit(solution)/shard_map/edge/pallas_call | solution.py:458
  0.8 3.0 %collective-permute-start = (f32[10,8,256]{2,1,0:T(8,128)S(1)}, f32[10,8,256]{2,1,0:T(8,128)S(1)}, u32[]{:S(2)}, u32[]{:S(2)}) collective-permute-start(f32[10,8,256]{2,1,0:T(8,128)S(1)} %edge.1.refs_6_), channel_id=1, source_target_pairs={{0,4},{4,8},{8,12},{12,28},{16,0},{20,16},{24,20},{28,24},{1,5},{5... | collective-permute-start | bytes 245768 | tf_op jit(solution)/shard_map/ppermute | solution.py:467
  3.8 1.1 %load.1 = (s32[1,512]{1,0:T(1,128)S(1)}, s32[1,512]{1,0:T(1,128)S(1)}, s32[1,512]{1,0:T(1,128)S(1)}, f32[8,8,256]{2,1,0:T(8,128)S(1)}, f32[8,8,256]{2,1,0:T(8,12...) custom-call(f32[4,512]{1,0:T(4,128)} %observed.1, f32[1,4]{1,0:T(1,128)} %bitcast.8, s32[1,4]{1,0:T(1,128)} %bitcast.9, ...), custom_call_target="tpu_custom_call" | custom-call | tf_op jit(solution)/shard_map/load/pallas_call | solution.py:480
  4.9 0.1 collective-permute-start.3
  5.0 0.1 compare_convert_fusion
  5.1 0.8 %collective-permute-done.slab_ref = f32[10,8,256]{2,1,0:T(8,128)S(1)} collective-permute-done((f32[10,8,256]{2,1,0:T(8,128)S(1)}, f32[10,8,256]{2,1,0:T(8,128)S(1)}, u32[]{:S(2)}, u32[]{:S(2)}) %collective-permute-start) | collective-permute-done | bytes 81952 | tf_op jit(solution)/shard_map/ppermute | solution.py:467
  5.9 0.1 pack_y.1
  5.9 0.1 collective-permute-start.2
  6.0 3.1 %collective-permute-start.1 = (f32[64,256]{1,0:T(8,128)S(1)}, f32[64,256]{1,0:T(8,128)S(1)}, u32[]{:S(2)}, u32[]{:S(2)}) collective-permute-start(f32[64,256]{1,0:T(8,128)S(1)} %get-tuple-element.39._), channel_id=1, source_target_pairs={{0,1},{1,0},{2,3},{3,2},{16,17},{17,16},{18,19},{19,18},{4,5},{5,4... | collective-permute-start | bytes 196616 | tf_op jit(solution)/shard_map/ppermute | solution.py:519
  9.2 0.0 collective-permute-done.3.other_ref
  9.2 0.7 %wells.1 = (s32[408,1]{1,0:T(8,128)S(1)}, f32[8,128]{1,0:T(8,128)S(1)}, f32[192,2,8,128]{3,2,1,0:T(8,128)S(1)}, f32[192,2,8,128]{3,2,1,0:T(8,128)S(1)}) custom-call(s32[1,512]{1,0:T(1,128)S(1)} %get-tuple-element.44.owner_ref, s32[1,512]{1,0:T(1,128)S(1)} %compare_select_fusion.place_ref, s32[1,512]{1,0:T(1,128)S(1)} %get-tuple-element.46.top_ref, ...), custom_call_target="tpu_custom_call" | custom-call | tf_op jit(solution)/shard_map/wells/pallas_call | solution.py:522
  9.9 0.0 collective-permute-done.2.odd_ref
  9.9 1.5 %collective-permute-done.1.even_ref = f32[64,256]{1,0:T(8,128)S(1)} collective-permute-done((f32[64,256]{1,0:T(8,128)S(1)}, f32[64,256]{1,0:T(8,128)S(1)}, u32[]{:S(2)}, u32[]{:S(2)}) %collective-permute-start.1) | collective-permute-done | bytes 65568 | tf_op jit(solution)/shard_map/ppermute | solution.py:519
  11.4 1.2 %heads.1 = (f32[12,16,256]{2,1,0:T(8,128)S(1)}, f32[12,16,256]{2,1,0:T(8,128)S(1)}, f32[12,16,256]{2,1,0:T(8,128)S(1)}, f32[12,16,256]{2,1,0:T(8,128)S(1)}, f32[...) custom-call(f32[64,256]{1,0:T(8,128)S(1)} %collective-permute-done.1, ...), custom_call_target="tpu_custom_call", output_to_operand_aliasing={{0}: (2, {}), {6}: (3, {}), {7}: (4, {})} | custom-call | tf_op jit(solution)/shard_map/heads/pallas_call | solution.py:533
  12.6 12.9 %all_to_all.5.resid_ref = f32[32,2,128]{2,1,0:T(2,128)S(1)} all-to-all(f32[32,2,128]{2,1,0:T(2,128)S(1)} %get-tuple-element.50), channel_id=1, replica_groups=mesh['test'=2,'bx'=4,'by'=4] {'test','bx','by'}, dimensions={0} | all-to-all | bytes 65536 | tf_op jit(solution)/shard_map/all_to_all | solution.py:545
  25.5 1.8 %adjoint.1 = (f32[192,2,8,128]{3,2,1,0:T(8,128)S(1)}, f32[192,2,8,128]{3,2,1,0:T(8,128)S(1)}, f32[192,2,8,128]{3,2,1,0:T(8,128)S(1)}, f32[4,8,128]{2,1,0:T(8,128)S(1)}, f32[8,128]{1,0:T(8,128)S(1)}) custom-call(f32[32,2,128]{2,1,0:T(2,128)S(1)} %all_to_all.5.resid_ref, ...), custom_call_target="tpu_custom_call", output_to_operand_aliasing={{0}: (2, {}), {1}: (3, {})} | custom-call | tf_op jit(solution)/shard_map/adjoint/pallas_call | solution.py:550
  27.3 0.1 collective-permute-start.4
  27.4 0.5 %keep.1 = f32[4,8,128]{2,1,0:T(8,128)S(1)} custom-call(f32[8,128]{1,0:T(8,128)S(1)} %get-tuple-element.58.norm_ref, f32[12,16,256]{2,1,0:T(8,128)S(1)} %get-tuple-element.53.e_ref, f32[192,2,8,128]{3,2,1,0:T(8,128)S(1)} %get-tuple-element.57.head_ref, f32[192,2,8,128]{3,2,1,0:T(8,128)S(1)} %get-tuple-element.59.adj_ref), custom_call_target="tpu_custom_call" | custom-call | tf_op jit(solution)/shard_map/keep/pallas_call | solution.py:561
  27.9 0.6 %collective-permute-done.4 = f32[4,8,128]{2,1,0:T(8,128)S(1)} collective-permute-done((f32[4,8,128]{2,1,0:T(8,128)S(1)}, f32[4,8,128]{2,1,0:T(8,128)S(1)}, u32[]{:S(2)}, u32[]{:S(2)}) %collective-permute-start.4) | collective-permute-done | bytes 16416 | tf_op jit(solution)/shard_map/ppermute | solution.py:560
  28.5 0.6 %maximum_select_fusion = f32[8,8,128]{2,1,0:T(8,128)} fusion(f32[4,8,128]{2,1,0:T(8,128)S(1)} %collective-permute-done.4, f32[4,8,128]{2,1,0:T(8,128)S(1)} %keep.1, pred[]{:T(512)S(6)} %eq.11), kind=kLoop, calls=%fused_computation | loop fusion | flops 24576 | bytes 65537 | tf_op jit(solution)/shard_map/jit(_where)/select_n | solution.py:570
  (3 shorter events, 0.1 us)
Async XLA Ops:
  0.8 5.1 %collective-permute-start = (f32[10,8,256]{2,1,0:T(8,128)S(1)}, f32[10,8,256]{2,1,0:T(8,128)S(1)}, u32[]{:S(2)}, u32[]{:S(2)}) collective-permute-start(f32[10,8,256]{2,1,0:T(8,128)S(1)} %edge.1.refs_6_), channel_id=1, source_target_pairs={{0,4},{4,8},{8,12},{12,28},{16,0},{20,16},{24,20},{28,24},{1,5},{5... | collective-permute-start | bytes 245768 | tf_op jit(solution)/shard_map/ppermute | solution.py:467
  4.9 4.3 %collective-permute-start.3 = (f32[8,512]{1,0:T(8,128)S(1)}, f32[8,512]{1,0:T(8,128)S(1)}, u32[]{:S(2)}, u32[]{:S(2)}) collective-permute-start(f32[8,512]{1,0:T(8,128)S(1)} %get-tuple-element.47.facts_ref), channel_id=1, source_target_pairs={{0,16},{16,0},{1,17},{17,1},{2,18},{18,2},{3,19},{19,3},{4,20},{20... | collective-permute-start | bytes 49160 | tf_op jit(solution)/shard_map/ppermute | solution.py:490
  5.9 4.0 %collective-permute-start.2 = (f32[64,256]{1,0:T(8,128)S(1)}, f32[64,256]{1,0:T(8,128)S(1)}, u32[]{:S(2)}, u32[]{:S(2)}) collective-permute-start(f32[64,256]{1,0:T(8,128)S(1)} %get-tuple-element.40), channel_id=1, source_target_pairs={{0,16},{1,2},{2,1},{3,19},{16,0},{17,18},{18,17},{19,3},{4,20},{5,... | collective-permute-start | bytes 196616 | tf_op jit(solution)/shard_map/ppermute | solution.py:520
  6.0 5.4 %collective-permute-start.1 = (f32[64,256]{1,0:T(8,128)S(1)}, f32[64,256]{1,0:T(8,128)S(1)}, u32[]{:S(2)}, u32[]{:S(2)}) collective-permute-start(f32[64,256]{1,0:T(8,128)S(1)} %get-tuple-element.39._), channel_id=1, source_target_pairs={{0,1},{1,0},{2,3},{3,2},{16,17},{17,16},{18,19},{19,18},{4,5},{5,4... | collective-permute-start | bytes 196616 | tf_op jit(solution)/shard_map/ppermute | solution.py:519
  27.3 1.2 %collective-permute-start.4 = (f32[4,8,128]{2,1,0:T(8,128)S(1)}, f32[4,8,128]{2,1,0:T(8,128)S(1)}, u32[]{:S(2)}, u32[]{:S(2)}) collective-permute-start(f32[4,8,128]{2,1,0:T(8,128)S(1)} %get-tuple-element.60), channel_id=1, source_target_pairs={{0,16},{16,0},{1,17},{17,1},{2,18},{18,2},{3,19},{19,3},{4,20},{20... | collective-permute-start | bytes 49160 | tf_op jit(solution)/shard_map/ppermute | solution.py:560

commit v5 on v4

--- a/solution.py
+++ b/solution.py
@@ -157,10 +157,13 @@
     return pltpu.roll(jnp.concatenate([value, value], axis=0), DEEP, 0)
 
 
-def window_kernel(log_ref, sto_ref, rec_ref, e_ref, sto_w, rec_w):
+def window_kernel(log_ref, sto_ref, rec_ref, e_ref, sto_w, rec_w, up_ref):
     base = jnp.where(second_half(), 0, DEEP)
     for x in range(log_ref.shape[0]):
-        e_ref[base + x] = at_window_rows(jnp.exp(0.5 * log_ref[x]))
+        e = jnp.exp(0.5 * log_ref[x])
+        e_ref[base + x] = at_window_rows(e)
+        last = lax.broadcasted_iota(jnp.int32, e.shape, 1) == e.shape[1] - 1
+        up_ref[base + x] = at_window_rows(e * jnp.where(last, 1.0, pltpu.roll(e, e.shape[1] - 1, 1)))
         sto_w[base + x] = at_window_rows(sto_ref[x])
         rec_w[base + x] = at_window_rows(rec_ref[x])
 
@@ -335,8 +338,8 @@
     row_ref[...] = jnp.broadcast_to(jnp.concatenate(parts, axis=0)[None], row_ref.shape)
 
 
-def adjoint_kernel(tests, per_brick, n_wells, joined, scale, resid_ref, table_ref, clear_ref, clear_more_ref, e_ref, delta_ref, gamma_ref, inv_ref, head_ref,
-                   bet_ref, more_ref, adj_ref, send_ref, norm_ref, weight_ref, one_ref):
+def adjoint_kernel(tests, per_brick, n_wells, joined, scale, resid_ref, table_ref, clear_ref, clear_more_ref, e_ref, delta_ref, gamma_ref, inv_ref,
+                   bet_ref, more_ref, adj_ref, norm_ref, weight_ref, one_ref):
     wide_x, wide_y, _ = e_ref.shape
     bricks = n_wells // per_brick
     sub = lax.broadcasted_iota(jnp.int32, (8, LANES), 0)
@@ -370,52 +373,55 @@
     squares = jnp.where(sub < tests, squares[0:1], squares[1:2])
     misfit = jnp.sum(jnp.where(lanes() // per_brick == sub % tests, squares, 0.0), axis=1, keepdims=True) / n_wells + EPSILON
     norm_ref[...] = jnp.broadcast_to(scale / misfit, (8, LANES))
-    gradient_half(jnp.where(second_half(), 0, 1), norm_ref, e_ref, head_ref, adj_ref, send_ref)
-
-
-def keep_kernel(norm_ref, e_ref, head_ref, adj_ref, keep_ref):
-    gradient_half(jnp.where(second_half(), 1, 0), norm_ref, e_ref, head_ref, adj_ref, keep_ref)
-
-
-def gradient_half(part, norm_ref, e_ref, head_ref, adj_ref, out_ref):
+
+
+def gradient_kernel(kept, norm_ref, e_ref, up_ref, head_ref, adj_ref, out_ref):
     wide_x, wide_y, _ = e_ref.shape
     low, high = DEEP, wide_y - DEEP
+    part = jnp.where(second_half(), 1, 0) if kept else jnp.where(second_half(), 0, 1)
     is_first = part == 0
     at_first, at_last = lanes() == 0, lanes() == LANES - 1
 
-    def spread_part(x, first, last):
-        rows = [e_ref[x, pl.ds(y, 1), pl.ds(pl.multiple_of(part * LANES, LANES), LANES)] for y in range(first, last)]
+    def spread_part(ref, x, first, last, which):
+        rows = [ref[x, pl.ds(y, 1), pl.ds(pl.multiple_of(which * LANES, LANES), LANES)] for y in range(first, last)]
         return jnp.stack([jnp.broadcast_to(row, (8, LANES)) for row in rows])
 
     def tiles(ref, x, first, last, which):
         return ref[x * wide_y + first : x * wide_y + last, which]
 
-    def crossing(values, others, edge, turn, end):
-        turned, other = pltpu.roll(values, turn, 2), pltpu.roll(others, turn, 2)
-        return jnp.where(end, jnp.where(is_first == (turn != 1), other, edge), turned)
+    def next_cell(values, others):
+        return pltpu.roll(jnp.where(at_first & is_first, others, values), LANES - 1, 2)
 
     before = None
     for x in range(DEEP - 1, wide_x - DEEP):
-        e, head, adjoint = spread_part(x, low, high), tiles(head_ref, x, low, high, part), tiles(adj_ref, x, low, high, part)
+        e, head, adjoint = spread_part(e_ref, x, low, high, part), tiles(head_ref, x, low, high, part), tiles(adj_ref, x, low, high, part)
         gap = (head - tiles(head_ref, x + 1, low, high, part)) * (adjoint - tiles(adj_ref, x + 1, low, high, part))
-        after = e * spread_part(x + 1, low, high) * gap
+        after = e * spread_part(e_ref, x + 1, low, high, part) * gap
         if x >= DEEP:
             total = before + after
-            e_y = spread_part(x, low - 1, high + 1)
+            e_y = spread_part(e_ref, x, low - 1, high + 1, part)
             head_y, adjoint_y = tiles(head_ref, x, low - 1, high + 1, part), tiles(adj_ref, x, low - 1, high + 1, part)
             sides = e_y[:-1] * e_y[1:] * (head_y[:-1] - head_y[1:]) * (adjoint_y[:-1] - adjoint_y[1:])
             total = total + sides[:-1] + sides[1:]
-            halves = [ref[x, low:high, other * LANES : (other + 1) * LANES] for ref in (e_ref,) for other in range(2)]
-            e_other = jnp.stack([jnp.broadcast_to(jnp.where(is_first, halves[1], halves[0])[y : y + 1], (8, LANES)) for y in range(high - low)])
             head_other, adjoint_other = tiles(head_ref, x, low, high, 1 - part), tiles(adj_ref, x, low, high, 1 - part)
-            for turn, end in ((LANES - 1, at_last), (1, at_first)):
-                e_near = crossing(e, e_other, 1.0, turn, end)
-                head_near, adjoint_near = crossing(head, head_other, 0.0, turn, end), crossing(adjoint, adjoint_other, 0.0, turn, end)
-                total = total + e * e_near * (head - head_near) * (adjoint - adjoint_near)
+            head_next, adjoint_next = next_cell(head, head_other), next_cell(adjoint, adjoint_other)
+            at_top = at_last & jnp.logical_not(is_first)
+            gap = (head - jnp.where(at_top, 0.0, head_next)) * (adjoint - jnp.where(at_top, 0.0, adjoint_next))
+            upper = spread_part(up_ref, x, low, high, part) * gap
+            middle = spread_part(up_ref, x, low, high, 1 - part) * (head_other - head_next) * (adjoint_other - adjoint_next)
+            lower = pltpu.roll(jnp.where(at_top, middle, upper), 1, 2)
+            total = total + upper + jnp.where(at_first & is_first, e * head * adjoint, lower)
             total = jnp.sum(total * norm_ref[...], axis=1, keepdims=True)
             for y in range(high - low):
                 out_ref[x - DEEP, pl.ds(y, 1), :] = total[y]
         before = after
+
+
+def join_kernel(keep_ref, other_ref, out_ref):
+    half_x = keep_ref.shape[0]
+    mine = jnp.where(second_half(), half_x, 0)
+    out_ref[pl.ds(mine, half_x)] = keep_ref[...]
+    out_ref[pl.ds(half_x - mine, half_x)] = other_ref[...]
 
 
 def vmem():
@@ -498,11 +504,11 @@
     owned = (out_x + out_y == 0).astype(jnp.float32)
     place = jnp.where(in_window > 0.5, well_x * wide_y + well_y, 0)
     window = f32(wide_x, wide_y, size_z)
-    e, sto_w, rec_w = pl.pallas_call(
+    e, sto_w, rec_w, up = pl.pallas_call(
         window_kernel,
-        out_shape=[window] * 3,
+        out_shape=[window] * 4,
         in_specs=[vmem()] * 3,
-        out_specs=[vmem()] * 3,
+        out_specs=[vmem()] * 4,
         compiler_params=PARAMS,
         name="window",
     )(log_k, sto, rec)
@@ -547,27 +553,39 @@
         residuals = lax.all_to_all(row + lax.ppermute(row, "test", pairs), ("bx", "by"), 0, 0)
 
     scale = -0.5 / (tests * groups)
-    _, _, adjoint, send, norm = pl.pallas_call(
+    _, _, adjoint, norm = pl.pallas_call(
         functools.partial(adjoint_kernel, tests, per_brick, n_wells, joined, scale),
-        out_shape=[f32(*tiles)] * 3 + [f32(half_x, size_y, LANES), f32(8, LANES)],
-        in_specs=[vmem()] * 9,
-        out_specs=[vmem()] * 5,
+        out_shape=[f32(*tiles)] * 3 + [f32(8, LANES)],
+        in_specs=[vmem()] * 8,
+        out_specs=[vmem()] * 4,
         scratch_shapes=[pltpu.VMEM((bricks, 8, LANES), jnp.float32), pltpu.VMEM(tiles, jnp.float32)],
         input_output_aliases={2: 0, 3: 1},
         compiler_params=PARAMS,
         name="adjoint",
-    )(residuals, table, clear, clear_more, e, delta, gamma, inverse, head)
+    )(residuals, table, clear, clear_more, e, delta, gamma, inverse)
+
+    def gradient_of(kept):
+        return pl.pallas_call(
+            functools.partial(gradient_kernel, kept),
+            out_shape=f32(half_x, size_y, LANES),
+            in_specs=[vmem()] * 5,
+            out_specs=vmem(),
+            compiler_params=PARAMS,
+            name="keep" if kept else "send",
+        )(norm, e, up, head, adjoint)
+
+    send = gradient_of(False)
     other = lax.ppermute(send, "test", pairs) if joined else send
-    keep = pl.pallas_call(
-        keep_kernel,
-        out_shape=f32(half_x, size_y, LANES),
-        in_specs=[vmem()] * 4,
-        out_specs=vmem(),
-        compiler_params=PARAMS,
-        name="keep",
-    )(norm, e, head, adjoint)
+    keep = gradient_of(True)
     if joined:
-        return jnp.where(second == 0, jnp.concatenate([keep, other], axis=0), jnp.concatenate([other, keep], axis=0))
+        return pl.pallas_call(
+            join_kernel,
+            out_shape=f32(size_x, size_y, LANES),
+            in_specs=[vmem()] * 2,
+            out_specs=vmem(),
+            compiler_params=PARAMS,
+            name="join",
+        )(pltpu.with_memory_space_constraint(keep, pltpu.VMEM), pltpu.with_memory_space_constraint(other, pltpu.VMEM))
     low, high = jnp.where(second == 0, keep, send), jnp.where(second == 0, send, keep)
     half = jnp.concatenate([low, high], axis=2)
     none = jnp.zeros_like(half)

time: 29.4 us -> 29.1 us (0.990)
  other arithmetic: 0.68 us -> 0.06 us
    pallas_call x2 -> x4, Pallas kernels: 0.56 us -> 1.24 us  [the longest x1 0.62 us: local(): pl.pallas_call(join_kernel, out_shape=f32(size_x, size_y, LANES), in_spec...]
    select_n x1 -> x0, other arithmetic: 0.62 us -> none  [local(): jnp.where(second == 0, jnp.concatenate([keep, other], axis=0), jnp.concat...]
    pallas_call x1, Pallas kernels: 1.8 us -> 1.22 us  [local(): pl.pallas_call(functools.partial(adjoint_kernel, tests, per_brick, n_well...]
where the time goes in v5:
time: 29.1 us; the launch traced here: 28.8 us
  blocking collectives  12.9 us (44%)
  starting transfers between devices  6.35 us (22%)
  Pallas kernels  6.33 us (22%)
  waiting for transfers between devices  3.1 us (11%)
    all_to_all x1, blocking collectives, local(): residuals = lax.all_to_all(row, ('test', 'bx', 'by'), 0, 0)  12.9 us
    ppermute x1, starting transfers between devices, local(): got_even = lax.ppermute(even_y, ('test', 'by'), even)  3.14 us
    ppermute x1, starting transfers between devices, local(): got_x = lax.ppermute(slab, ('test', 'bx'), circle(n_bx, groups))  3 us
    ppermute x1, waiting for transfers between devices, local(): got_even = lax.ppermute(even_y, ('test', 'by'), even)  1.49 us
    pallas_call x1, Pallas kernels, local(): pl.pallas_call(functools.partial(adjoint_kernel, tests, per_brick, n_well...  1.22 us
    pallas_call x1, Pallas kernels, local(): pl.pallas_call(functools.partial(heads_kernel, plan, tests, per_brick), o...  1.18 us
    pallas_call x1, Pallas kernels, local(): pl.pallas_call(load_kernel, out_shape=[jax.ShapeDtypeStruct(a.shape, a.dt...  1.08 us
    ppermute x1, waiting for transfers between devices, local(): other = lax.ppermute(send, 'test', pairs) if joined else send  0.9 us
  transfers between devices with their start and end apart: 5, of which 3 were waited for; matrix products, arithmetic and copies ran while one was open for 0% of the time, Pallas kernels for 8%

profile of v5, /device:TPU:0, one launch (start us, length us, event | category | flops | bytes accessed | tf_op | source)
XLA Modules:
  0.0 28.8 jit_solution(4786122459861713504)
XLA Ops:
  0.0 0.8 %edge.1.refs_6_ = f32[10,8,256]{2,1,0:T(8,128)S(1)} custom-call(f32[8,8,256]{2,1,0:T(8,128)} %refs_3_.1, f32[8,8,256]{2,1,0:T(8,128)} %refs_4_.1, f32[8,8,256]{2,1,0:T(8,128)} %refs_5_.1), custom_call_target="tpu_custom_call" | custom-call | tf_op jit(solution)/shard_map/edge/pallas_call | solution.py:464
  0.8 3.0 %collective-permute-start = (f32[10,8,256]{2,1,0:T(8,128)S(1)}, f32[10,8,256]{2,1,0:T(8,128)S(1)}, u32[]{:S(2)}, u32[]{:S(2)}) collective-permute-start(f32[10,8,256]{2,1,0:T(8,128)S(1)} %edge.1.refs_6_), channel_id=1, source_target_pairs={{0,4},{4,8},{8,12},{12,28},{16,0},{20,16},{24,20},{28,24},{1,5},{5... | collective-permute-start | bytes 245768 | tf_op jit(solution)/shard_map/ppermute | solution.py:473
  3.8 1.1 %load.1 = (s32[1,512]{1,0:T(1,128)S(1)}, s32[1,512]{1,0:T(1,128)S(1)}, s32[1,512]{1,0:T(1,128)S(1)}, f32[8,8,256]{2,1,0:T(8,128)S(1)}, f32[8,8,256]{2,1,0:T(8,12...) custom-call(f32[4,512]{1,0:T(4,128)} %observed.1, f32[1,4]{1,0:T(1,128)} %bitcast.8, s32[1,4]{1,0:T(1,128)} %bitcast.9, ...), custom_call_target="tpu_custom_call" | custom-call | tf_op jit(solution)/shard_map/load/pallas_call | solution.py:486
  4.9 0.1 collective-permute-start.3
  5.0 0.1 compare_convert_fusion
  5.1 0.1 window.1
  5.2 0.7 %collective-permute-done.slab_ref = f32[10,8,256]{2,1,0:T(8,128)S(1)} collective-permute-done((f32[10,8,256]{2,1,0:T(8,128)S(1)}, f32[10,8,256]{2,1,0:T(8,128)S(1)}, u32[]{:S(2)}, u32[]{:S(2)}) %collective-permute-start) | collective-permute-done | bytes 81952 | tf_op jit(solution)/shard_map/ppermute | solution.py:473
  5.9 0.1 pack_y.1
  5.9 0.1 collective-permute-start.2
  6.0 3.1 %collective-permute-start.1 = (f32[64,256]{1,0:T(8,128)S(1)}, f32[64,256]{1,0:T(8,128)S(1)}, u32[]{:S(2)}, u32[]{:S(2)}) collective-permute-start(f32[64,256]{1,0:T(8,128)S(1)} %get-tuple-element.39._), channel_id=1, source_target_pairs={{0,1},{1,0},{2,3},{3,2},{16,17},{17,16},{18,19},{19,18},{4,5},{5,4... | collective-permute-start | bytes 196616 | tf_op jit(solution)/shard_map/ppermute | solution.py:525
  9.2 0.0 collective-permute-done.3.other_ref
  9.2 0.7 %wells.1 = (s32[408,1]{1,0:T(8,128)S(1)}, f32[8,128]{1,0:T(8,128)S(1)}, f32[192,2,8,128]{3,2,1,0:T(8,128)S(1)}, f32[192,2,8,128]{3,2,1,0:T(8,128)S(1)}) custom-call(s32[1,512]{1,0:T(1,128)S(1)} %get-tuple-element.44.owner_ref, s32[1,512]{1,0:T(1,128)S(1)} %compare_select_fusion.place_ref, s32[1,512]{1,0:T(1,128)S(1)} %get-tuple-element.46.top_ref, ...), custom_call_target="tpu_custom_call" | custom-call | tf_op jit(solution)/shard_map/wells/pallas_call | solution.py:528
  9.9 0.0 collective-permute-done.2.odd_ref
  9.9 1.5 %collective-permute-done.1.even_ref = f32[64,256]{1,0:T(8,128)S(1)} collective-permute-done((f32[64,256]{1,0:T(8,128)S(1)}, f32[64,256]{1,0:T(8,128)S(1)}, u32[]{:S(2)}, u32[]{:S(2)}) %collective-permute-start.1) | collective-permute-done | bytes 65568 | tf_op jit(solution)/shard_map/ppermute | solution.py:525
  11.4 1.2 %heads.1 = (f32[12,16,256]{2,1,0:T(8,128)S(1)}, f32[12,16,256]{2,1,0:T(8,128)S(1)}, f32[12,16,256]{2,1,0:T(8,128)S(1)}, f32[12,16,256]{2,1,0:T(8,128)S(1)}, f32[...) custom-call(f32[64,256]{1,0:T(8,128)S(1)} %collective-permute-done.1, ...), custom_call_target="tpu_custom_call", output_to_operand_aliasing={{0}: (2, {}), {6}: (3, {}), {7}: (4, {})} | custom-call | tf_op jit(solution)/shard_map/heads/pallas_call | solution.py:539
  12.6 12.9 %all_to_all.5.resid_ref = f32[32,2,128]{2,1,0:T(2,128)S(1)} all-to-all(f32[32,2,128]{2,1,0:T(2,128)S(1)} %get-tuple-element.50), channel_id=1, replica_groups=mesh['test'=2,'bx'=4,'by'=4] {'test','bx','by'}, dimensions={0} | all-to-all | bytes 65536 | tf_op jit(solution)/shard_map/all_to_all | solution.py:551
  25.5 1.2 %adjoint.1 = (f32[192,2,8,128]{3,2,1,0:T(8,128)S(1)}, f32[192,2,8,128]{3,2,1,0:T(8,128)S(1)}, f32[192,2,8,128]{3,2,1,0:T(8,128)S(1)}, f32[8,128]{1,0:T(8,128)S(1)}) custom-call(f32[32,2,128]{2,1,0:T(2,128)S(1)} %all_to_all.5.resid_ref, s32[408,1]{1,0:T(8,128)S(1)} %get-tuple-element.48.table_ref, ...), custom_call_target="tpu_custom_call", output_to_operand_aliasing={{0}: (2, {}), {1}: (3, {})} | custom-call | tf_op jit(solution)/shard_map/adjoint/pallas_call | solution.py:556
  26.7 0.3 send.1
  27.0 0.1 collective-permute-start.4
  27.0 0.3 keep.1.keep_ref
  27.3 0.9 %collective-permute-done.4.other_ref = f32[4,8,128]{2,1,0:T(8,128)S(1)} collective-permute-done((f32[4,8,128]{2,1,0:T(8,128)S(1)}, f32[4,8,128]{2,1,0:T(8,128)S(1)}, u32[]{:S(2)}, u32[]{:S(2)}) %collective-permute-start.4) | collective-permute-done | bytes 16416 | tf_op jit(solution)/shard_map/ppermute | solution.py:578
  28.2 0.6 %join.1 = f32[8,8,128]{2,1,0:T(8,128)} custom-call(f32[4,8,128]{2,1,0:T(8,128)S(1)} %keep.1.keep_ref, f32[4,8,128]{2,1,0:T(8,128)S(1)} %collective-permute-done.4.other_ref), custom_call_target="tpu_custom_call" | custom-call | tf_op jit(solution)/shard_map/join/pallas_call | solution.py:581
  (2 shorter events, 0.0 us)
Async XLA Ops:
  0.8 5.1 %collective-permute-start = (f32[10,8,256]{2,1,0:T(8,128)S(1)}, f32[10,8,256]{2,1,0:T(8,128)S(1)}, u32[]{:S(2)}, u32[]{:S(2)}) collective-permute-start(f32[10,8,256]{2,1,0:T(8,128)S(1)} %edge.1.refs_6_), channel_id=1, source_target_pairs={{0,4},{4,8},{8,12},{12,28},{16,0},{20,16},{24,20},{28,24},{1,5},{5... | collective-permute-start | bytes 245768 | tf_op jit(solution)/shard_map/ppermute | solution.py:473
  4.9 4.3 %collective-permute-start.3 = (f32[8,512]{1,0:T(8,128)S(1)}, f32[8,512]{1,0:T(8,128)S(1)}, u32[]{:S(2)}, u32[]{:S(2)}) collective-permute-start(f32[8,512]{1,0:T(8,128)S(1)} %get-tuple-element.47.facts_ref), channel_id=1, source_target_pairs={{0,16},{16,0},{1,17},{17,1},{2,18},{18,2},{3,19},{19,3},{4,20},{20... | collective-permute-start | bytes 49160 | tf_op jit(solution)/shard_map/ppermute | solution.py:496
  5.9 4.0 %collective-permute-start.2 = (f32[64,256]{1,0:T(8,128)S(1)}, f32[64,256]{1,0:T(8,128)S(1)}, u32[]{:S(2)}, u32[]{:S(2)}) collective-permute-start(f32[64,256]{1,0:T(8,128)S(1)} %get-tuple-element.40), channel_id=1, source_target_pairs={{0,16},{1,2},{2,1},{3,19},{16,0},{17,18},{18,17},{19,3},{4,20},{5,... | collective-permute-start | bytes 196616 | tf_op jit(solution)/shard_map/ppermute | solution.py:526
  6.0 5.4 %collective-permute-start.1 = (f32[64,256]{1,0:T(8,128)S(1)}, f32[64,256]{1,0:T(8,128)S(1)}, u32[]{:S(2)}, u32[]{:S(2)}) collective-permute-start(f32[64,256]{1,0:T(8,128)S(1)} %get-tuple-element.39._), channel_id=1, source_target_pairs={{0,1},{1,0},{2,3},{3,2},{16,17},{17,16},{18,19},{19,18},{4,5},{5,4... | collective-permute-start | bytes 196616 | tf_op jit(solution)/shard_map/ppermute | solution.py:525
  27.0 1.2 %collective-permute-start.4 = (f32[4,8,128]{2,1,0:T(8,128)S(1)}, f32[4,8,128]{2,1,0:T(8,128)S(1)}, u32[]{:S(2)}, u32[]{:S(2)}) collective-permute-start(f32[4,8,128]{2,1,0:T(8,128)S(1)} %send.1), channel_id=1, source_target_pairs={{0,16},{16,0},{1,17},{17,1},{2,18},{18,2},{3,19},{19,3},{4,20},{20... | collective-permute-start | bytes 49160 | tf_op jit(solution)/shard_map/ppermute | solution.py:578

commit v6 on v5

--- a/solution.py
+++ b/solution.py
@@ -12,7 +12,7 @@
 DEEP = 4
 EPSILON = 1e-06
 WELL_CHUNK = 512
-WELLS_AT_ONCE = 16
+WELLS_AT_ONCE = 32
 COLUMNS_AT_ONCE = 1
 
 

time: 29.1 us -> 29.1 us (level)
  no operation moved by 1% of the time
where the time goes in v6:
time: 29.1 us; the launch traced here: 28.8 us
  blocking collectives  12.9 us (44%)
  starting transfers between devices  6.35 us (22%)
  Pallas kernels  6.3 us (22%)
  waiting for transfers between devices  3.1 us (11%)
    all_to_all x1, blocking collectives, local(): residuals = lax.all_to_all(row, ('test', 'bx', 'by'), 0, 0)  12.9 us
    ppermute x1, starting transfers between devices, local(): got_even = lax.ppermute(even_y, ('test', 'by'), even)  3.14 us
    ppermute x1, starting transfers between devices, local(): got_x = lax.ppermute(slab, ('test', 'bx'), circle(n_bx, groups))  3 us
    ppermute x1, waiting for transfers between devices, local(): got_even = lax.ppermute(even_y, ('test', 'by'), even)  1.49 us
    pallas_call x1, Pallas kernels, local(): pl.pallas_call(functools.partial(adjoint_kernel, tests, per_brick, n_well...  1.2 us
    pallas_call x1, Pallas kernels, local(): pl.pallas_call(functools.partial(heads_kernel, plan, tests, per_brick), o...  1.18 us
    pallas_call x1, Pallas kernels, local(): pl.pallas_call(load_kernel, out_shape=[jax.ShapeDtypeStruct(a.shape, a.dt...  1.08 us
    ppermute x1, waiting for transfers between devices, local(): other = lax.ppermute(send, 'test', pairs) if joined else send  0.9 us
  transfers between devices with their start and end apart: 5, of which 3 were waited for; matrix products, arithmetic and copies ran while one was open for 0% of the time, Pallas kernels for 8%

profile of v6, /device:TPU:0, one launch (start us, length us, event | category | flops | bytes accessed | tf_op | source)
XLA Modules:
  0.0 28.8 jit_solution(12710890162717243432)
XLA Ops:
  0.0 0.8 %edge.1.refs_6_ = f32[10,8,256]{2,1,0:T(8,128)S(1)} custom-call(f32[8,8,256]{2,1,0:T(8,128)} %refs_3_.1, f32[8,8,256]{2,1,0:T(8,128)} %refs_4_.1, f32[8,8,256]{2,1,0:T(8,128)} %refs_5_.1), custom_call_target="tpu_custom_call" | custom-call | tf_op jit(solution)/shard_map/edge/pallas_call | solution.py:464
  0.8 3.0 %collective-permute-start = (f32[10,8,256]{2,1,0:T(8,128)S(1)}, f32[10,8,256]{2,1,0:T(8,128)S(1)}, u32[]{:S(2)}, u32[]{:S(2)}) collective-permute-start(f32[10,8,256]{2,1,0:T(8,128)S(1)} %edge.1.refs_6_), channel_id=1, source_target_pairs={{0,4},{4,8},{8,12},{12,28},{16,0},{20,16},{24,20},{28,24},{1,5},{5... | collective-permute-start | bytes 245768 | tf_op jit(solution)/shard_map/ppermute | solution.py:473
  3.8 1.1 %load.1 = (s32[1,512]{1,0:T(1,128)S(1)}, s32[1,512]{1,0:T(1,128)S(1)}, s32[1,512]{1,0:T(1,128)S(1)}, f32[8,8,256]{2,1,0:T(8,128)S(1)}, f32[8,8,256]{2,1,0:T(8,12...) custom-call(f32[4,512]{1,0:T(4,128)} %observed.1, f32[1,4]{1,0:T(1,128)} %bitcast.8, s32[1,4]{1,0:T(1,128)} %bitcast.9, ...), custom_call_target="tpu_custom_call" | custom-call | tf_op jit(solution)/shard_map/load/pallas_call | solution.py:486
  4.9 0.1 collective-permute-start.3
  5.0 0.1 compare_convert_fusion
  5.1 0.1 window.1
  5.2 0.7 %collective-permute-done.slab_ref = f32[10,8,256]{2,1,0:T(8,128)S(1)} collective-permute-done((f32[10,8,256]{2,1,0:T(8,128)S(1)}, f32[10,8,256]{2,1,0:T(8,128)S(1)}, u32[]{:S(2)}, u32[]{:S(2)}) %collective-permute-start) | collective-permute-done | bytes 81952 | tf_op jit(solution)/shard_map/ppermute | solution.py:473
  5.9 0.1 pack_y.1
  5.9 0.1 collective-permute-start.2
  6.0 3.1 %collective-permute-start.1 = (f32[64,256]{1,0:T(8,128)S(1)}, f32[64,256]{1,0:T(8,128)S(1)}, u32[]{:S(2)}, u32[]{:S(2)}) collective-permute-start(f32[64,256]{1,0:T(8,128)S(1)} %get-tuple-element.39._), channel_id=1, source_target_pairs={{0,1},{1,0},{2,3},{3,2},{16,17},{17,16},{18,19},{19,18},{4,5},{5,4... | collective-permute-start | bytes 196616 | tf_op jit(solution)/shard_map/ppermute | solution.py:525
  9.2 0.0 collective-permute-done.3.other_ref
  9.2 0.7 %wells.1 = (s32[408,1]{1,0:T(8,128)S(1)}, f32[8,128]{1,0:T(8,128)S(1)}, f32[192,2,8,128]{3,2,1,0:T(8,128)S(1)}, f32[192,2,8,128]{3,2,1,0:T(8,128)S(1)}) custom-call(s32[1,512]{1,0:T(1,128)S(1)} %get-tuple-element.44.owner_ref, s32[1,512]{1,0:T(1,128)S(1)} %compare_select_fusion.place_ref, s32[1,512]{1,0:T(1,128)S(1)} %get-tuple-element.46.top_ref, ...), custom_call_target="tpu_custom_call" | custom-call | tf_op jit(solution)/shard_map/wells/pallas_call | solution.py:528
  9.9 0.0 collective-permute-done.2.odd_ref
  9.9 1.5 %collective-permute-done.1.even_ref = f32[64,256]{1,0:T(8,128)S(1)} collective-permute-done((f32[64,256]{1,0:T(8,128)S(1)}, f32[64,256]{1,0:T(8,128)S(1)}, u32[]{:S(2)}, u32[]{:S(2)}) %collective-permute-start.1) | collective-permute-done | bytes 65568 | tf_op jit(solution)/shard_map/ppermute | solution.py:525
  11.4 1.2 %heads.1 = (f32[12,16,256]{2,1,0:T(8,128)S(1)}, f32[12,16,256]{2,1,0:T(8,128)S(1)}, f32[12,16,256]{2,1,0:T(8,128)S(1)}, f32[12,16,256]{2,1,0:T(8,128)S(1)}, f32[...) custom-call(f32[64,256]{1,0:T(8,128)S(1)} %collective-permute-done.1, ...), custom_call_target="tpu_custom_call", output_to_operand_aliasing={{0}: (2, {}), {6}: (3, {}), {7}: (4, {})} | custom-call | tf_op jit(solution)/shard_map/heads/pallas_call | solution.py:539
  12.6 12.9 %all_to_all.5.resid_ref = f32[32,2,128]{2,1,0:T(2,128)S(1)} all-to-all(f32[32,2,128]{2,1,0:T(2,128)S(1)} %get-tuple-element.50), channel_id=1, replica_groups=mesh['test'=2,'bx'=4,'by'=4] {'test','bx','by'}, dimensions={0} | all-to-all | bytes 65536 | tf_op jit(solution)/shard_map/all_to_all | solution.py:551
  25.5 1.2 %adjoint.1 = (f32[192,2,8,128]{3,2,1,0:T(8,128)S(1)}, f32[192,2,8,128]{3,2,1,0:T(8,128)S(1)}, f32[192,2,8,128]{3,2,1,0:T(8,128)S(1)}, f32[8,128]{1,0:T(8,128)S(1)}) custom-call(f32[32,2,128]{2,1,0:T(2,128)S(1)} %all_to_all.5.resid_ref, s32[408,1]{1,0:T(8,128)S(1)} %get-tuple-element.48.table_ref, ...), custom_call_target="tpu_custom_call", output_to_operand_aliasing={{0}: (2, {}), {1}: (3, {})} | custom-call | tf_op jit(solution)/shard_map/adjoint/pallas_call | solution.py:556
  26.7 0.3 send.1
  26.9 0.1 collective-permute-start.4
  27.0 0.3 keep.1.keep_ref
  27.3 0.9 %collective-permute-done.4.other_ref = f32[4,8,128]{2,1,0:T(8,128)S(1)} collective-permute-done((f32[4,8,128]{2,1,0:T(8,128)S(1)}, f32[4,8,128]{2,1,0:T(8,128)S(1)}, u32[]{:S(2)}, u32[]{:S(2)}) %collective-permute-start.4) | collective-permute-done | bytes 16416 | tf_op jit(solution)/shard_map/ppermute | solution.py:578
  28.2 0.6 %join.1 = f32[8,8,128]{2,1,0:T(8,128)} custom-call(f32[4,8,128]{2,1,0:T(8,128)S(1)} %keep.1.keep_ref, f32[4,8,128]{2,1,0:T(8,128)S(1)} %collective-permute-done.4.other_ref), custom_call_target="tpu_custom_call" | custom-call | tf_op jit(solution)/shard_map/join/pallas_call | solution.py:581
  (2 shorter events, 0.0 us)
Async XLA Ops:
  0.8 5.1 %collective-permute-start = (f32[10,8,256]{2,1,0:T(8,128)S(1)}, f32[10,8,256]{2,1,0:T(8,128)S(1)}, u32[]{:S(2)}, u32[]{:S(2)}) collective-permute-start(f32[10,8,256]{2,1,0:T(8,128)S(1)} %edge.1.refs_6_), channel_id=1, source_target_pairs={{0,4},{4,8},{8,12},{12,28},{16,0},{20,16},{24,20},{28,24},{1,5},{5... | collective-permute-start | bytes 245768 | tf_op jit(solution)/shard_map/ppermute | solution.py:473
  4.9 4.3 %collective-permute-start.3 = (f32[8,512]{1,0:T(8,128)S(1)}, f32[8,512]{1,0:T(8,128)S(1)}, u32[]{:S(2)}, u32[]{:S(2)}) collective-permute-start(f32[8,512]{1,0:T(8,128)S(1)} %get-tuple-element.47.facts_ref), channel_id=1, source_target_pairs={{0,16},{16,0},{1,17},{17,1},{2,18},{18,2},{3,19},{19,3},{4,20},{20... | collective-permute-start | bytes 49160 | tf_op jit(solution)/shard_map/ppermute | solution.py:496
  5.9 4.0 %collective-permute-start.2 = (f32[64,256]{1,0:T(8,128)S(1)}, f32[64,256]{1,0:T(8,128)S(1)}, u32[]{:S(2)}, u32[]{:S(2)}) collective-permute-start(f32[64,256]{1,0:T(8,128)S(1)} %get-tuple-element.40), channel_id=1, source_target_pairs={{0,16},{1,2},{2,1},{3,19},{16,0},{17,18},{18,17},{19,3},{4,20},{5,... | collective-permute-start | bytes 196616 | tf_op jit(solution)/shard_map/ppermute | solution.py:526
  6.0 5.4 %collective-permute-start.1 = (f32[64,256]{1,0:T(8,128)S(1)}, f32[64,256]{1,0:T(8,128)S(1)}, u32[]{:S(2)}, u32[]{:S(2)}) collective-permute-start(f32[64,256]{1,0:T(8,128)S(1)} %get-tuple-element.39._), channel_id=1, source_target_pairs={{0,1},{1,0},{2,3},{3,2},{16,17},{17,16},{18,19},{19,18},{4,5},{5,4... | collective-permute-start | bytes 196616 | tf_op jit(solution)/shard_map/ppermute | solution.py:525
  26.9 1.2 %collective-permute-start.4 = (f32[4,8,128]{2,1,0:T(8,128)S(1)}, f32[4,8,128]{2,1,0:T(8,128)S(1)}, u32[]{:S(2)}, u32[]{:S(2)}) collective-permute-start(f32[4,8,128]{2,1,0:T(8,128)S(1)} %send.1), channel_id=1, source_target_pairs={{0,16},{16,0},{1,17},{17,1},{2,18},{18,2},{3,19},{19,3},{4,20},{20... | collective-permute-start | bytes 49160 | tf_op jit(solution)/shard_map/ppermute | solution.py:578

commit v7 on v6

--- a/solution.py
+++ b/solution.py
@@ -264,6 +264,12 @@
     return cells
 
 
+def without(cells, wide_y, margin):
+    for x, low, high in cells:
+        yield x, low, margin
+        yield x, wide_y - margin, high
+
+
 def grouped(cells):
     for x, first, end in cells:
         for low in range(first, end, COLUMNS_AT_ONCE):
@@ -287,8 +293,46 @@
     return packed & 255, (packed >> 8) & 255
 
 
-def heads_kernel(plan, tests, per_brick, even_ref, odd_ref, e_in, sto_in, rec_in, table_ref, obs_ref,
-                 e_ref, delta_ref, gamma_ref, inv_ref, head_ref, row_ref, sto_w, rec_w, beta_ref, bet_ref, one_ref):
+def pump(tests, per_brick, inner, wide_y, table_ref, obs_ref, delta_ref, bet_ref):
+    sub = lax.broadcasted_iota(jnp.int32, (8, LANES), 0)
+    z_of = z_of_tile()
+    listed = list_length(per_brick)
+    pumped = []
+    for test in range(2 * tests):
+        packed = table_ref[listed + LANES + test, 0]
+        place, top = unpack(packed)
+        y = place % wide_y
+        is_inner = (y >= DEEP + 1) & (y < wide_y - DEEP - 1)
+        near = ((packed >> 30) & 1 == 1) & (is_inner if inner else jnp.logical_not(is_inner))
+        rate = obs_ref[3 + test // tests : 4 + test // tests, test % tests : test % tests + 1]
+        delta = delta_ref[place // wide_y, pl.ds(y, 1), :]
+        delta = jnp.stack([jnp.broadcast_to(delta[:, part * LANES : (part + 1) * LANES], (8, LANES)) for part in range(2)])
+        hit = (z_of >= top) & (z_of < top + SCREEN) & (sub == test) & near
+        pumped.append((place, jnp.where(hit, delta * rate, 0.0)))
+    for place, taken in pumped:
+        bet_ref[place] = bet_ref[place] - taken
+
+
+def inner_kernel(tests, per_brick, e_ref, sto_w, rec_w, table_ref, obs_ref,
+                 bet_ref, one_ref, head_ref, delta_ref, gamma_ref, beta_ref, inv_ref):
+    wide_x, wide_y, _ = e_ref.shape
+    field_rows(e_ref, sto_w, rec_w, delta_ref, gamma_ref, beta_ref)
+    for x in range(3, wide_x - 3):
+        inv_ref[x] = 1.0 / e_ref[x]
+    for x in range(1, wide_x - 1):
+        bet_ref[x * wide_y + DEEP + 1 : (x + 1) * wide_y - DEEP - 1] = spread(beta_ref, x, DEEP + 1, wide_y - DEEP - 1)
+    pump(tests, per_brick, True, wide_y, table_ref, obs_ref, delta_ref, bet_ref)
+    for x in range(2, wide_x - 2):
+        low, high = DEEP + 2, wide_y - DEEP - 2
+        one_ref[x * wide_y + low : x * wide_y + high] = sweep(bet_ref, gamma_ref, bet_ref, x, low, high)
+    for x in range(3, wide_x - 3):
+        low, high = DEEP + 3, wide_y - DEEP - 3
+        scaled = sweep(bet_ref, gamma_ref, one_ref, x, low, high)
+        head_ref[x * wide_y + low : x * wide_y + high] = scaled * spread(inv_ref, x, low, high)
+
+
+def heads_kernel(plan, tests, per_brick, even_ref, odd_ref, e_in, sto_in, rec_in, table_ref, obs_ref, bet_in, one_in, head_in,
+                 e_ref, delta_ref, gamma_ref, inv_ref, head_ref, row_ref, sto_w, rec_w, bet_ref, one_ref, beta_ref):
     wide_x, wide_y, _ = e_ref.shape
     by = lax.axis_index("by")
     y_even = by % 2 == 0
@@ -305,24 +349,17 @@
     field_rows(e_ref, sto_w, rec_w, delta_ref, gamma_ref, beta_ref)
     for x in range(3, wide_x - 3):
         inv_ref[x] = 1.0 / e_ref[x]
-    for x, low, high in reached(wide_x, wide_y, DEEP - 1):
+    for x, low, high in without(reached(wide_x, wide_y, DEEP - 1), wide_y, DEEP + 1):
         bet_ref[x * wide_y + low : x * wide_y + high] = spread(beta_ref, x, low, high)
     sub = lax.broadcasted_iota(jnp.int32, (8, LANES), 0)
     z_of = z_of_tile()
     listed = list_length(per_brick)
-    pumped = []
-    for test in range(2 * tests):
-        packed = table_ref[listed + LANES + test, 0]
-        place, top = unpack(packed)
-        near = (packed >> 30) & 1 == 1
-        rate = obs_ref[3 + test // tests : 4 + test // tests, test % tests : test % tests + 1]
-        delta = delta_ref[place // wide_y, pl.ds(place % wide_y, 1), :]
-        delta = jnp.stack([jnp.broadcast_to(delta[:, part * LANES : (part + 1) * LANES], (8, LANES)) for part in range(2)])
-        hit = (z_of >= top) & (z_of < top + SCREEN) & (sub == test) & near
-        pumped.append((place, jnp.where(hit, delta * rate, 0.0)))
-    for place, taken in pumped:
-        bet_ref[place] = bet_ref[place] - taken
-    solve(bet_ref, gamma_ref, inv_ref, one_ref, head_ref)
+    pump(tests, per_brick, False, wide_y, table_ref, obs_ref, delta_ref, bet_ref)
+    for x, low, high in without(reached(wide_x, wide_y, DEEP - 2), wide_y, DEEP + 2):
+        one_ref[x * wide_y + low : x * wide_y + high] = sweep(bet_ref, gamma_ref, bet_ref, x, low, high)
+    for x, low, high in without(reached(wide_x, wide_y, DEEP - 3), wide_y, DEEP + 3):
+        scaled = sweep(bet_ref, gamma_ref, one_ref, x, low, high)
+        head_ref[x * wide_y + low : x * wide_y + high] = scaled * spread(inv_ref, x, low, high)
     slot_of = lanes() - per_brick * (sub % tests)
     gathered = jnp.zeros((8, LANES), jnp.float32)
     for rank in range(per_brick):
@@ -536,16 +573,25 @@
 
     joined = groups == 2
     copies = groups * bricks if joined else bricks
-    e, delta, gamma, inverse, head, row, _, _ = pl.pallas_call(
+    inner = pl.pallas_call(
+        functools.partial(inner_kernel, tests, per_brick),
+        out_shape=[f32(*tiles)] * 3,
+        in_specs=[vmem()] * 5,
+        out_specs=[vmem()] * 3,
+        scratch_shapes=[pltpu.VMEM((wide_x, wide_y, size_z), jnp.float32)] * 4,
+        compiler_params=PARAMS,
+        name="inner",
+    )(e, sto_w, rec_w, table, obs)
+    e, delta, gamma, inverse, head, row = pl.pallas_call(
         functools.partial(heads_kernel, plan, tests, per_brick),
-        out_shape=[window] * 4 + [f32(*tiles), f32(copies, 2, LANES)] + [window] * 2,
-        in_specs=[vmem()] * 7,
-        out_specs=[vmem()] * 8,
-        scratch_shapes=[pltpu.VMEM((wide_x, wide_y, size_z), jnp.float32)] + [pltpu.VMEM(tiles, jnp.float32)] * 2,
-        input_output_aliases={2: 0, 3: 6, 4: 7},
+        out_shape=[window] * 4 + [f32(*tiles), f32(copies, 2, LANES)] + [window] * 2 + [f32(*tiles)] * 2,
+        in_specs=[vmem()] * 10,
+        out_specs=[vmem()] * 10,
+        scratch_shapes=[pltpu.VMEM((wide_x, wide_y, size_z), jnp.float32)],
+        input_output_aliases={2: 0, 3: 6, 4: 7, 7: 8, 8: 9, 9: 4},
         compiler_params=PARAMS,
         name="heads",
-    )(got_even, got_odd, e, sto_w, rec_w, table, obs)
+    )(got_even, got_odd, e, sto_w, rec_w, table, obs, *inner)[:6]
 
     if joined:
         residuals = lax.all_to_all(row, ("test", "bx", "by"), 0, 0)

time: 29.1 us -> 28.9 us (level)
  waiting for transfers between devices: 3.1 us -> 2.52 us
  Pallas kernels: 6.3 us -> 6.76 us
    ppermute x1, waiting for transfers between devices: 1.49 us -> 0.91 us  [local(): got_even = lax.ppermute(even_y, ('test', 'by'), even)]
    pallas_call x0 -> x1, Pallas kernels: none -> 0.57 us  [local(): pl.pallas_call(functools.partial(inner_kernel, tests, per_brick), out_sha...]
  transfers between devices with their start and end apart: 5 -> 5, of which waited for: 3 -> 3; matrix products, arithmetic and copies ran while one was open for 0% -> 0% of each run, Pallas kernels for 8% -> 10%
where the time goes in v7:
time: 28.9 us; the launch traced here: 28.7 us
  blocking collectives  12.9 us (45%)
  Pallas kernels  6.76 us (23%)
  starting transfers between devices  6.35 us (22%)
  waiting for transfers between devices  2.52 us (9%)
    all_to_all x1, blocking collectives, local(): residuals = lax.all_to_all(row, ('test', 'bx', 'by'), 0, 0)  12.9 us
    ppermute x1, starting transfers between devices, local(): got_even = lax.ppermute(even_y, ('test', 'by'), even)  3.14 us
    ppermute x1, starting transfers between devices, local(): got_x = lax.ppermute(slab, ('test', 'bx'), circle(n_bx, groups))  3 us
    pallas_call x1, Pallas kernels, local(): pl.pallas_call(functools.partial(adjoint_kernel, tests, per_brick, n_well...  1.33 us
    pallas_call x1, Pallas kernels, local(): pl.pallas_call(load_kernel, out_shape=[jax.ShapeDtypeStruct(a.shape, a.dt...  1.08 us
    pallas_call x1, Pallas kernels, local(): pl.pallas_call(functools.partial(heads_kernel, plan, tests, per_brick), o...  0.94 us
    ppermute x1, waiting for transfers between devices, local(): got_even = lax.ppermute(even_y, ('test', 'by'), even)  0.91 us
    ppermute x1, waiting for transfers between devices, local(): other = lax.ppermute(send, 'test', pairs) if joined else send  0.9 us
  transfers between devices with their start and end apart: 5, of which 3 were waited for; matrix products, arithmetic and copies ran while one was open for 0% of the time, Pallas kernels for 10%

profile of v7, /device:TPU:0, one launch (start us, length us, event | category | flops | bytes accessed | tf_op | source)
XLA Modules:
  0.0 28.7 jit_solution(1343106544664644632)
XLA Ops:
  0.0 0.8 %edge.1.refs_6_ = f32[10,8,256]{2,1,0:T(8,128)S(1)} custom-call(f32[8,8,256]{2,1,0:T(8,128)} %refs_3_.1, f32[8,8,256]{2,1,0:T(8,128)} %refs_4_.1, f32[8,8,256]{2,1,0:T(8,128)} %refs_5_.1), custom_call_target="tpu_custom_call" | custom-call | tf_op jit(solution)/shard_map/edge/pallas_call | solution.py:501
  0.8 3.0 %collective-permute-start = (f32[10,8,256]{2,1,0:T(8,128)S(1)}, f32[10,8,256]{2,1,0:T(8,128)S(1)}, u32[]{:S(2)}, u32[]{:S(2)}) collective-permute-start(f32[10,8,256]{2,1,0:T(8,128)S(1)} %edge.1.refs_6_), channel_id=1, source_target_pairs={{0,4},{4,8},{8,12},{12,28},{16,0},{20,16},{24,20},{28,24},{1,5},{5... | collective-permute-start | bytes 245768 | tf_op jit(solution)/shard_map/ppermute | solution.py:510
  3.8 1.1 %load.1 = (s32[1,512]{1,0:T(1,128)S(1)}, s32[1,512]{1,0:T(1,128)S(1)}, s32[1,512]{1,0:T(1,128)S(1)}, f32[8,8,256]{2,1,0:T(8,128)S(1)}, f32[8,8,256]{2,1,0:T(8,12...) custom-call(f32[4,512]{1,0:T(4,128)} %observed.1, f32[1,4]{1,0:T(1,128)} %bitcast.8, s32[1,4]{1,0:T(1,128)} %bitcast.9, ...), custom_call_target="tpu_custom_call" | custom-call | tf_op jit(solution)/shard_map/load/pallas_call | solution.py:523
  4.9 0.1 collective-permute-start.3
  5.0 0.1 compare_convert_fusion
  5.1 0.1 window.1
  5.2 0.7 %collective-permute-done.slab_ref = f32[10,8,256]{2,1,0:T(8,128)S(1)} collective-permute-done((f32[10,8,256]{2,1,0:T(8,128)S(1)}, f32[10,8,256]{2,1,0:T(8,128)S(1)}, u32[]{:S(2)}, u32[]{:S(2)}) %collective-permute-start) | collective-permute-done | bytes 81952 | tf_op jit(solution)/shard_map/ppermute | solution.py:510
  5.9 0.1 pack_y.1
  5.9 0.1 collective-permute-start.2
  6.0 3.1 %collective-permute-start.1 = (f32[64,256]{1,0:T(8,128)S(1)}, f32[64,256]{1,0:T(8,128)S(1)}, u32[]{:S(2)}, u32[]{:S(2)}) collective-permute-start(f32[64,256]{1,0:T(8,128)S(1)} %get-tuple-element.42._), channel_id=1, source_target_pairs={{0,1},{1,0},{2,3},{3,2},{16,17},{17,16},{18,19},{19,18},{4,5},{5,4... | collective-permute-start | bytes 196616 | tf_op jit(solution)/shard_map/ppermute | solution.py:562
  9.2 0.0 collective-permute-done.3.other_ref
  9.2 0.7 %wells.1 = (s32[408,1]{1,0:T(8,128)S(1)}, f32[8,128]{1,0:T(8,128)S(1)}, f32[192,2,8,128]{3,2,1,0:T(8,128)S(1)}, f32[192,2,8,128]{3,2,1,0:T(8,128)S(1)}) custom-call(s32[1,512]{1,0:T(1,128)S(1)} %get-tuple-element.47.owner_ref, s32[1,512]{1,0:T(1,128)S(1)} %compare_select_fusion.place_ref, s32[1,512]{1,0:T(1,128)S(1)} %get-tuple-element.49.top_ref, ...), custom_call_target="tpu_custom_call" | custom-call | tf_op jit(solution)/shard_map/wells/pallas_call | solution.py:565
  9.9 0.6 %inner.1 = (f32[192,2,8,128]{3,2,1,0:T(8,128)S(1)}, f32[192,2,8,128]{3,2,1,0:T(8,128)S(1)}, f32[192,2,8,128]{3,2,1,0:T(8,128)S(1)}) custom-call(f32[12,16,256]{2,1,0:T(8,128)S(1)} %get-tuple-element.44.e_ref.e_in, f32[12,16,256]{2,1,0:T(8,128)S(1)} %get-tuple-element.45.sto_w.sto_in, f32[12,16,256]{2,1,0:T(8,128)S(1)} %get-tuple-element.46.rec_w.rec_in, ...), custom_call_target="tpu_custom_call" | custom-call | tf_op jit(solution)/shard_map/inner/pallas_call | solution.py:576
  10.5 0.0 collective-permute-done.2.odd_ref
  10.5 0.9 %collective-permute-done.1.even_ref = f32[64,256]{1,0:T(8,128)S(1)} collective-permute-done((f32[64,256]{1,0:T(8,128)S(1)}, f32[64,256]{1,0:T(8,128)S(1)}, u32[]{:S(2)}, u32[]{:S(2)}) %collective-permute-start.1) | collective-permute-done | bytes 65568 | tf_op jit(solution)/shard_map/ppermute | solution.py:562
  11.4 0.9 %heads.1 = (f32[12,16,256]{2,1,0:T(8,128)S(1)}, f32[12,16,256]{2,1,0:T(8,128)S(1)}, f32[12,16,256]{2,1,0:T(8,128)S(1)}, f32[12,16,256]{2,1,0:T(8,128)S(1)}, f32[...) custom-call(f32[64,256]{1,0:T(8,128)S(1)} %collective-permute-done.1, ...), custom_call_target="tpu_custom_call", output_to_operand_aliasing={{0}: (2, {}), {6}: (3, {}), {7}: (4, {}), {8}: (7, {}), {9}... | custom-call | tf_op jit(solution)/shard_map/heads/pallas_call | solution.py:585
  12.4 12.9 %all_to_all.5.resid_ref = f32[32,2,128]{2,1,0:T(2,128)S(1)} all-to-all(f32[32,2,128]{2,1,0:T(2,128)S(1)} %get-tuple-element.56), channel_id=1, replica_groups=mesh['test'=2,'bx'=4,'by'=4] {'test','bx','by'}, dimensions={0} | all-to-all | bytes 65536 | tf_op jit(solution)/shard_map/all_to_all | solution.py:597
  25.2 1.3 %adjoint.1 = (f32[192,2,8,128]{3,2,1,0:T(8,128)S(1)}, f32[192,2,8,128]{3,2,1,0:T(8,128)S(1)}, f32[192,2,8,128]{3,2,1,0:T(8,128)S(1)}, f32[8,128]{1,0:T(8,128)S(1)}) custom-call(f32[32,2,128]{2,1,0:T(2,128)S(1)} %all_to_all.5.resid_ref, s32[408,1]{1,0:T(8,128)S(1)} %get-tuple-element.51.table_ref, ...), custom_call_target="tpu_custom_call", output_to_operand_aliasing={{0}: (2, {}), {1}: (3, {})} | custom-call | tf_op jit(solution)/shard_map/adjoint/pallas_call | solution.py:602
  26.6 0.3 send.1
  26.8 0.1 collective-permute-start.4
  26.9 0.3 keep.1.keep_ref
  27.2 0.9 %collective-permute-done.4.other_ref = f32[4,8,128]{2,1,0:T(8,128)S(1)} collective-permute-done((f32[4,8,128]{2,1,0:T(8,128)S(1)}, f32[4,8,128]{2,1,0:T(8,128)S(1)}, u32[]{:S(2)}, u32[]{:S(2)}) %collective-permute-start.4) | collective-permute-done | bytes 16416 | tf_op jit(solution)/shard_map/ppermute | solution.py:624
  28.1 0.6 %join.1 = f32[8,8,128]{2,1,0:T(8,128)} custom-call(f32[4,8,128]{2,1,0:T(8,128)S(1)} %keep.1.keep_ref, f32[4,8,128]{2,1,0:T(8,128)S(1)} %collective-permute-done.4.other_ref), custom_call_target="tpu_custom_call" | custom-call | tf_op jit(solution)/shard_map/join/pallas_call | solution.py:627
  (2 shorter events, 0.0 us)
Async XLA Ops:
  0.8 5.1 %collective-permute-start = (f32[10,8,256]{2,1,0:T(8,128)S(1)}, f32[10,8,256]{2,1,0:T(8,128)S(1)}, u32[]{:S(2)}, u32[]{:S(2)}) collective-permute-start(f32[10,8,256]{2,1,0:T(8,128)S(1)} %edge.1.refs_6_), channel_id=1, source_target_pairs={{0,4},{4,8},{8,12},{12,28},{16,0},{20,16},{24,20},{28,24},{1,5},{5... | collective-permute-start | bytes 245768 | tf_op jit(solution)/shard_map/ppermute | solution.py:510
  4.9 4.3 %collective-permute-start.3 = (f32[8,512]{1,0:T(8,128)S(1)}, f32[8,512]{1,0:T(8,128)S(1)}, u32[]{:S(2)}, u32[]{:S(2)}) collective-permute-start(f32[8,512]{1,0:T(8,128)S(1)} %get-tuple-element.50.facts_ref), channel_id=1, source_target_pairs={{0,16},{16,0},{1,17},{17,1},{2,18},{18,2},{3,19},{19,3},{4,20},{20... | collective-permute-start | bytes 49160 | tf_op jit(solution)/shard_map/ppermute | solution.py:533
  5.9 4.5 %collective-permute-start.2 = (f32[64,256]{1,0:T(8,128)S(1)}, f32[64,256]{1,0:T(8,128)S(1)}, u32[]{:S(2)}, u32[]{:S(2)}) collective-permute-start(f32[64,256]{1,0:T(8,128)S(1)} %get-tuple-element.43), channel_id=1, source_target_pairs={{0,16},{1,2},{2,1},{3,19},{16,0},{17,18},{18,17},{19,3},{4,20},{5,... | collective-permute-start | bytes 196616 | tf_op jit(solution)/shard_map/ppermute | solution.py:563
  6.0 5.4 %collective-permute-start.1 = (f32[64,256]{1,0:T(8,128)S(1)}, f32[64,256]{1,0:T(8,128)S(1)}, u32[]{:S(2)}, u32[]{:S(2)}) collective-permute-start(f32[64,256]{1,0:T(8,128)S(1)} %get-tuple-element.42._), channel_id=1, source_target_pairs={{0,1},{1,0},{2,3},{3,2},{16,17},{17,16},{18,19},{19,18},{4,5},{5,4... | collective-permute-start | bytes 196616 | tf_op jit(solution)/shard_map/ppermute | solution.py:562
  26.8 1.2 %collective-permute-start.4 = (f32[4,8,128]{2,1,0:T(8,128)S(1)}, f32[4,8,128]{2,1,0:T(8,128)S(1)}, u32[]{:S(2)}, u32[]{:S(2)}) collective-permute-start(f32[4,8,128]{2,1,0:T(8,128)S(1)} %send.1), channel_id=1, source_target_pairs={{0,16},{16,0},{1,17},{17,1},{2,18},{18,2},{3,19},{19,3},{4,20},{20... | collective-permute-start | bytes 49160 | tf_op jit(solution)/shard_map/ppermute | solution.py:624

commit v8 on v7

--- a/solution.py
+++ b/solution.py
@@ -372,7 +372,7 @@
     for part in range(2):
         total = jnp.sum(jnp.where(sub // tests == part, gathered, 0.0), axis=0, keepdims=True)
         parts.append(jnp.where(mine, total * (1.0 / SCREEN) - obs_ref[part : part + 1, :], 0.0))
-    row_ref[...] = jnp.broadcast_to(jnp.concatenate(parts, axis=0)[None], row_ref.shape)
+    row_ref[...] = jnp.broadcast_to(jnp.concatenate(parts, axis=1)[None], row_ref.shape)
 
 
 def adjoint_kernel(tests, per_brick, n_wells, joined, scale, resid_ref, table_ref, clear_ref, clear_more_ref, e_ref, delta_ref, gamma_ref, inv_ref,
@@ -383,7 +383,7 @@
     z_of = z_of_tile()
     resid = resid_ref[:bricks] + resid_ref[bricks:] if joined else resid_ref[...]
     for brick in range(bricks):
-        weight_ref[brick] = jnp.where(sub < tests, resid[brick, 0:1], resid[brick, 1:2])
+        weight_ref[brick] = jnp.where(sub < tests, resid[brick, :, :LANES], resid[brick, :, LANES:])
     listed = list_length(per_brick)
     pick = per_brick * (sub % tests)
 
@@ -407,7 +407,7 @@
         bet_ref[row] = (bet_ref[row] + more_ref[row]) * spread(delta_ref, x, low, high)
     solve(bet_ref, gamma_ref, inv_ref, one_ref, adj_ref)
     squares = jnp.sum(resid * resid, axis=0)
-    squares = jnp.where(sub < tests, squares[0:1], squares[1:2])
+    squares = jnp.where(sub < tests, squares[:, :LANES], squares[:, LANES:])
     misfit = jnp.sum(jnp.where(lanes() // per_brick == sub % tests, squares, 0.0), axis=1, keepdims=True) / n_wells + EPSILON
     norm_ref[...] = jnp.broadcast_to(scale / misfit, (8, LANES))
 
@@ -584,7 +584,7 @@
     )(e, sto_w, rec_w, table, obs)
     e, delta, gamma, inverse, head, row = pl.pallas_call(
         functools.partial(heads_kernel, plan, tests, per_brick),
-        out_shape=[window] * 4 + [f32(*tiles), f32(copies, 2, LANES)] + [window] * 2 + [f32(*tiles)] * 2,
+        out_shape=[window] * 4 + [f32(*tiles), f32(copies, 1, 2 * LANES)] + [window] * 2 + [f32(*tiles)] * 2,
         in_specs=[vmem()] * 10,
         out_specs=[vmem()] * 10,
         scratch_shapes=[pltpu.VMEM((wide_x, wide_y, size_z), jnp.float32)],

time: 28.9 us -> 28.9 us (level)
  no operation moved by 1% of the time
where the time goes in v8:
time: 28.9 us; the launch traced here: 28.7 us
  blocking collectives  12.9 us (45%)
  Pallas kernels  6.75 us (23%)
  starting transfers between devices  6.35 us (22%)
  waiting for transfers between devices  2.52 us (9%)
    all_to_all x1, blocking collectives, local(): residuals = lax.all_to_all(row, ('test', 'bx', 'by'), 0, 0)  12.9 us
    ppermute x1, starting transfers between devices, local(): got_even = lax.ppermute(even_y, ('test', 'by'), even)  3.14 us
    ppermute x1, starting transfers between devices, local(): got_x = lax.ppermute(slab, ('test', 'bx'), circle(n_bx, groups))  3 us
    pallas_call x1, Pallas kernels, local(): pl.pallas_call(functools.partial(adjoint_kernel, tests, per_brick, n_well...  1.32 us
    pallas_call x1, Pallas kernels, local(): pl.pallas_call(load_kernel, out_shape=[jax.ShapeDtypeStruct(a.shape, a.dt...  1.08 us
    pallas_call x1, Pallas kernels, local(): pl.pallas_call(functools.partial(heads_kernel, plan, tests, per_brick), o...  0.94 us
    ppermute x1, waiting for transfers between devices, local(): got_even = lax.ppermute(even_y, ('test', 'by'), even)  0.91 us
    ppermute x1, waiting for transfers between devices, local(): other = lax.ppermute(send, 'test', pairs) if joined else send  0.9 us
  transfers between devices with their start and end apart: 5, of which 3 were waited for; matrix products, arithmetic and copies ran while one was open for 0% of the time, Pallas kernels for 10%

profile of v8, /device:TPU:0, one launch (start us, length us, event | category | flops | bytes accessed | tf_op | source)
XLA Modules:
  0.0 28.7 jit_solution(2200076711251062268)
XLA Ops:
  0.0 0.8 %edge.1.refs_6_ = f32[10,8,256]{2,1,0:T(8,128)S(1)} custom-call(f32[8,8,256]{2,1,0:T(8,128)} %refs_3_.1, f32[8,8,256]{2,1,0:T(8,128)} %refs_4_.1, f32[8,8,256]{2,1,0:T(8,128)} %refs_5_.1), custom_call_target="tpu_custom_call" | custom-call | tf_op jit(solution)/shard_map/edge/pallas_call | solution.py:501
  0.8 3.0 %collective-permute-start = (f32[10,8,256]{2,1,0:T(8,128)S(1)}, f32[10,8,256]{2,1,0:T(8,128)S(1)}, u32[]{:S(2)}, u32[]{:S(2)}) collective-permute-start(f32[10,8,256]{2,1,0:T(8,128)S(1)} %edge.1.refs_6_), channel_id=1, source_target_pairs={{0,4},{4,8},{8,12},{12,28},{16,0},{20,16},{24,20},{28,24},{1,5},{5... | collective-permute-start | bytes 245768 | tf_op jit(solution)/shard_map/ppermute | solution.py:510
  3.8 1.1 %load.1 = (s32[1,512]{1,0:T(1,128)S(1)}, s32[1,512]{1,0:T(1,128)S(1)}, s32[1,512]{1,0:T(1,128)S(1)}, f32[8,8,256]{2,1,0:T(8,128)S(1)}, f32[8,8,256]{2,1,0:T(8,12...) custom-call(f32[4,512]{1,0:T(4,128)} %observed.1, f32[1,4]{1,0:T(1,128)} %bitcast.8, s32[1,4]{1,0:T(1,128)} %bitcast.9, ...), custom_call_target="tpu_custom_call" | custom-call | tf_op jit(solution)/shard_map/load/pallas_call | solution.py:523
  4.9 0.1 collective-permute-start.3
  5.0 0.1 compare_convert_fusion
  5.1 0.1 window.1
  5.2 0.7 %collective-permute-done.slab_ref = f32[10,8,256]{2,1,0:T(8,128)S(1)} collective-permute-done((f32[10,8,256]{2,1,0:T(8,128)S(1)}, f32[10,8,256]{2,1,0:T(8,128)S(1)}, u32[]{:S(2)}, u32[]{:S(2)}) %collective-permute-start) | collective-permute-done | bytes 81952 | tf_op jit(solution)/shard_map/ppermute | solution.py:510
  5.9 0.1 pack_y.1
  5.9 0.1 collective-permute-start.2
  6.0 3.1 %collective-permute-start.1 = (f32[64,256]{1,0:T(8,128)S(1)}, f32[64,256]{1,0:T(8,128)S(1)}, u32[]{:S(2)}, u32[]{:S(2)}) collective-permute-start(f32[64,256]{1,0:T(8,128)S(1)} %get-tuple-element.42._), channel_id=1, source_target_pairs={{0,1},{1,0},{2,3},{3,2},{16,17},{17,16},{18,19},{19,18},{4,5},{5,4... | collective-permute-start | bytes 196616 | tf_op jit(solution)/shard_map/ppermute | solution.py:562
  9.2 0.0 collective-permute-done.3.other_ref
  9.2 0.7 %wells.1 = (s32[408,1]{1,0:T(8,128)S(1)}, f32[8,128]{1,0:T(8,128)S(1)}, f32[192,2,8,128]{3,2,1,0:T(8,128)S(1)}, f32[192,2,8,128]{3,2,1,0:T(8,128)S(1)}) custom-call(s32[1,512]{1,0:T(1,128)S(1)} %get-tuple-element.47.owner_ref, s32[1,512]{1,0:T(1,128)S(1)} %compare_select_fusion.place_ref, s32[1,512]{1,0:T(1,128)S(1)} %get-tuple-element.49.top_ref, ...), custom_call_target="tpu_custom_call" | custom-call | tf_op jit(solution)/shard_map/wells/pallas_call | solution.py:565
  9.9 0.6 %inner.1 = (f32[192,2,8,128]{3,2,1,0:T(8,128)S(1)}, f32[192,2,8,128]{3,2,1,0:T(8,128)S(1)}, f32[192,2,8,128]{3,2,1,0:T(8,128)S(1)}) custom-call(f32[12,16,256]{2,1,0:T(8,128)S(1)} %get-tuple-element.44.e_ref.e_in, f32[12,16,256]{2,1,0:T(8,128)S(1)} %get-tuple-element.45.sto_w.sto_in, f32[12,16,256]{2,1,0:T(8,128)S(1)} %get-tuple-element.46.rec_w.rec_in, ...), custom_call_target="tpu_custom_call" | custom-call | tf_op jit(solution)/shard_map/inner/pallas_call | solution.py:576
  10.5 0.0 collective-permute-done.2.odd_ref
  10.5 0.9 %collective-permute-done.1.even_ref = f32[64,256]{1,0:T(8,128)S(1)} collective-permute-done((f32[64,256]{1,0:T(8,128)S(1)}, f32[64,256]{1,0:T(8,128)S(1)}, u32[]{:S(2)}, u32[]{:S(2)}) %collective-permute-start.1) | collective-permute-done | bytes 65568 | tf_op jit(solution)/shard_map/ppermute | solution.py:562
  11.4 0.9 %heads.1 = (f32[12,16,256]{2,1,0:T(8,128)S(1)}, f32[12,16,256]{2,1,0:T(8,128)S(1)}, f32[12,16,256]{2,1,0:T(8,128)S(1)}, f32[12,16,256]{2,1,0:T(8,128)S(1)}, f32[...) custom-call(f32[64,256]{1,0:T(8,128)S(1)} %collective-permute-done.1, ...), custom_call_target="tpu_custom_call", output_to_operand_aliasing={{0}: (2, {}), {6}: (3, {}), {7}: (4, {}), {8}: (7, {}), {9}... | custom-call | tf_op jit(solution)/shard_map/heads/pallas_call | solution.py:585
  12.4 12.9 %all_to_all.5.resid_ref = f32[32,1,256]{2,1,0:T(1,128)S(1)} all-to-all(f32[32,1,256]{2,1,0:T(1,128)S(1)} %get-tuple-element.56), channel_id=1, replica_groups=mesh['test'=2,'bx'=4,'by'=4] {'test','bx','by'}, dimensions={0} | all-to-all | bytes 65536 | tf_op jit(solution)/shard_map/all_to_all | solution.py:597
  25.2 1.3 %adjoint.1 = (f32[192,2,8,128]{3,2,1,0:T(8,128)S(1)}, f32[192,2,8,128]{3,2,1,0:T(8,128)S(1)}, f32[192,2,8,128]{3,2,1,0:T(8,128)S(1)}, f32[8,128]{1,0:T(8,128)S(1)}) custom-call(f32[32,1,256]{2,1,0:T(1,128)S(1)} %all_to_all.5.resid_ref, s32[408,1]{1,0:T(8,128)S(1)} %get-tuple-element.51.table_ref, ...), custom_call_target="tpu_custom_call", output_to_operand_aliasing={{0}: (2, {}), {1}: (3, {})} | custom-call | tf_op jit(solution)/shard_map/adjoint/pallas_call | solution.py:602
  26.6 0.3 send.1
  26.8 0.1 collective-permute-start.4
  26.9 0.3 keep.1.keep_ref
  27.2 0.9 %collective-permute-done.4.other_ref = f32[4,8,128]{2,1,0:T(8,128)S(1)} collective-permute-done((f32[4,8,128]{2,1,0:T(8,128)S(1)}, f32[4,8,128]{2,1,0:T(8,128)S(1)}, u32[]{:S(2)}, u32[]{:S(2)}) %collective-permute-start.4) | collective-permute-done | bytes 16416 | tf_op jit(solution)/shard_map/ppermute | solution.py:624
  28.1 0.6 %join.1 = f32[8,8,128]{2,1,0:T(8,128)} custom-call(f32[4,8,128]{2,1,0:T(8,128)S(1)} %keep.1.keep_ref, f32[4,8,128]{2,1,0:T(8,128)S(1)} %collective-permute-done.4.other_ref), custom_call_target="tpu_custom_call" | custom-call | tf_op jit(solution)/shard_map/join/pallas_call | solution.py:627
  (2 shorter events, 0.0 us)
Async XLA Ops:
  0.8 5.1 %collective-permute-start = (f32[10,8,256]{2,1,0:T(8,128)S(1)}, f32[10,8,256]{2,1,0:T(8,128)S(1)}, u32[]{:S(2)}, u32[]{:S(2)}) collective-permute-start(f32[10,8,256]{2,1,0:T(8,128)S(1)} %edge.1.refs_6_), channel_id=1, source_target_pairs={{0,4},{4,8},{8,12},{12,28},{16,0},{20,16},{24,20},{28,24},{1,5},{5... | collective-permute-start | bytes 245768 | tf_op jit(solution)/shard_map/ppermute | solution.py:510
  4.9 4.3 %collective-permute-start.3 = (f32[8,512]{1,0:T(8,128)S(1)}, f32[8,512]{1,0:T(8,128)S(1)}, u32[]{:S(2)}, u32[]{:S(2)}) collective-permute-start(f32[8,512]{1,0:T(8,128)S(1)} %get-tuple-element.50.facts_ref), channel_id=1, source_target_pairs={{0,16},{16,0},{1,17},{17,1},{2,18},{18,2},{3,19},{19,3},{4,20},{20... | collective-permute-start | bytes 49160 | tf_op jit(solution)/shard_map/ppermute | solution.py:533
  5.9 4.5 %collective-permute-start.2 = (f32[64,256]{1,0:T(8,128)S(1)}, f32[64,256]{1,0:T(8,128)S(1)}, u32[]{:S(2)}, u32[]{:S(2)}) collective-permute-start(f32[64,256]{1,0:T(8,128)S(1)} %get-tuple-element.43), channel_id=1, source_target_pairs={{0,16},{1,2},{2,1},{3,19},{16,0},{17,18},{18,17},{19,3},{4,20},{5,... | collective-permute-start | bytes 196616 | tf_op jit(solution)/shard_map/ppermute | solution.py:563
  6.0 5.4 %collective-permute-start.1 = (f32[64,256]{1,0:T(8,128)S(1)}, f32[64,256]{1,0:T(8,128)S(1)}, u32[]{:S(2)}, u32[]{:S(2)}) collective-permute-start(f32[64,256]{1,0:T(8,128)S(1)} %get-tuple-element.42._), channel_id=1, source_target_pairs={{0,1},{1,0},{2,3},{3,2},{16,17},{17,16},{18,19},{19,18},{4,5},{5,4... | collective-permute-start | bytes 196616 | tf_op jit(solution)/shard_map/ppermute | solution.py:562
  26.8 1.2 %collective-permute-start.4 = (f32[4,8,128]{2,1,0:T(8,128)S(1)}, f32[4,8,128]{2,1,0:T(8,128)S(1)}, u32[]{:S(2)}, u32[]{:S(2)}) collective-permute-start(f32[4,8,128]{2,1,0:T(8,128)S(1)} %send.1), channel_id=1, source_target_pairs={{0,16},{16,0},{1,17},{17,1},{2,18},{18,2},{3,19},{19,3},{4,20},{20... | collective-permute-start | bytes 49160 | tf_op jit(solution)/shard_map/ppermute | solution.py:624
